TPU v7x, 32 devices: a whole 2x2x4 slice. The times are simulated.
32 devices in a mesh: row: 8 (over y, x, core), col: 4 (over z).
Axes of the slice: x: 2, y: 2, z: 4, core: 2. Of those that a mesh axis runs over, the one named last changes fastest.
Arguments:
- node_features: bfloat16 [32768, 256], P(('row', 'col')), may hold values from -6 to 6
- tile_cols: int32 [512, 8], P(('row', 'col')), may hold values from 0 to 511, as said below
- tile_weights: int32 [512, 64, 512], P(('row', 'col')), may hold values from 0 to 7
- w_self: bfloat16 [256, 1024], replicated, may hold values from -0.375 to 0.375
- w_neigh: bfloat16 [256, 1024], replicated, may hold values from -0.375 to 0.375
- bias_hidden: float32 [1024], replicated, may hold values from -3 to 3
- w_out: bfloat16 [1024, 256], replicated, may hold values from -0.1875 to 0.1875
- bias_out: float32 [256], replicated, may hold values from -3 to 3
- cotangent: bfloat16 [32768, 256], P(('row', 'col')), may hold values from -6 to 6
Outputs:
- embed: bfloat16 [32768, 256], P(('row', 'col'))
- grad_features: bfloat16 [32768, 256], P(('row', 'col'))
- grad_w_self: float32 [256, 1024], replicated
- grad_w_neigh: float32 [256, 1024], replicated
- grad_bias_hidden: float32 [1024], replicated
- grad_w_out: float32 [1024, 256], replicated
- grad_bias_out: float32 [256], replicated
Inputs may be any that keep to these rules, and one draw needn't show every extreme that they name: `tile_cols`: the first tile of block row b is its diagonal block b. The second lies exactly 16 block rows before or after b (the side drawn for each row), clipped to the graph. Every tile's block column differs from its block row by at most 16.
All inputs are finite; a program needn't handle non-finite values.
Results may differ from a plain program's by a relative error of at most 0.0071.
Values may be sent and summed in bfloat16 or wider, within the bound.
No kernel may reach another device: no remote copies, remote signals or barrier semaphores. Data moves between devices by JAX's collectives and lax.ppermute only.
A program may use at most 128 MiB of HBM per device.

v0:
```python
import math

import jax
import jax.numpy as jnp
from jax import lax
from jax.sharding import PartitionSpec as P


def extended(block, sides, width):
    for axis, dim in sides:
        count = lax.axis_size(axis)
        forward = [(i, i + 1) for i in range(count - 1)]
        backward = [(target, source) for source, target in forward]
        low = lax.ppermute(
            lax.slice_in_dim(block, block.shape[dim] - width, None, axis=dim), axis, forward
        )
        high = lax.ppermute(lax.slice_in_dim(block, 0, width, axis=dim), axis, backward)
        block = jnp.concatenate([low, block, high], axis=dim)
    return block


def gelu_tanh(values):
    return jax.nn.gelu(values, approximate=True)


def reduce_grads(partials):
    return lax.psum(
        (partials[0], partials[1], partials[2], partials[3], partials[4]), ("row", "col")
    )


def adjoint_part(adjacency, d_aggregate, local_idx, block_rows, tile_size, per_row, width):
    rows_here = block_rows * tile_size
    spread = jnp.einsum(
        "bij,bif->bjf",
        adjacency,
        d_aggregate.reshape(block_rows, tile_size, width),
        preferred_element_type=jnp.float32,
    )
    spread = spread.reshape(block_rows * per_row, tile_size, width)
    spread_sum = jnp.zeros((3 * block_rows, tile_size, width), jnp.float32)
    spread_sum = spread_sum.at[local_idx.reshape(-1)].add(spread)
    spread_sum = spread_sum.reshape(3 * rows_here, width)
    outer_parts = jnp.concatenate([spread_sum[:rows_here], spread_sum[2 * rows_here :]], axis=0)
    padded = extended(outer_parts, ((("row", "col"), 0),), rows_here)
    return spread_sum[rows_here : 2 * rows_here] + padded[:rows_here] + padded[3 * rows_here :]


def local(
    node_features, tile_cols, tile_weights, w_self, w_neigh, bias_hidden, w_out, bias_out, cotangent
):
    rows_here = node_features.shape[0]
    width = node_features.shape[1]
    tile_size = tile_weights.shape[1]
    per_row = tile_cols.shape[1]
    block_rows = rows_here // tile_size
    devices_all = lax.axis_size(("row", "col"))
    tile_scale = 0.25 / math.sqrt(per_row * tile_size)
    grad_scale = 1.0 / math.sqrt(rows_here * devices_all)
    window = extended(node_features, ((("row", "col"), 0),), rows_here)
    first_block = lax.axis_index(("row", "col")) * block_rows - block_rows
    local_idx = tile_cols - first_block
    all_blocks = window.reshape(3 * block_rows, tile_size, width)
    gathered = all_blocks[local_idx].reshape(block_rows, per_row * tile_size, width)
    adjacency = (tile_weights.astype(jnp.float32) * tile_scale).astype(jnp.bfloat16)
    aggregate = jnp.einsum("bij,bjf->bif", adjacency, gathered, preferred_element_type=jnp.float32)
    aggregate = aggregate.reshape(rows_here, width).astype(jnp.bfloat16)
    preact = (
        jnp.dot(node_features, w_self, preferred_element_type=jnp.float32)
        + jnp.dot(aggregate, w_neigh, preferred_element_type=jnp.float32)
        + bias_hidden
    )
    activated, pullback = jax.vjp(gelu_tanh, preact)
    hidden = activated.astype(jnp.bfloat16)
    embed = (jnp.dot(hidden, w_out, preferred_element_type=jnp.float32) + bias_out).astype(
        jnp.bfloat16
    )
    d_act = jnp.dot(cotangent, w_out.T, preferred_element_type=jnp.float32)
    d_hidden = pullback(d_act)[0].astype(jnp.bfloat16)
    partials = (
        jnp.dot(node_features.T, d_hidden, preferred_element_type=jnp.float32),
        jnp.dot(aggregate.T, d_hidden, preferred_element_type=jnp.float32),
        jnp.sum(d_hidden.astype(jnp.float32), axis=0),
        jnp.dot(hidden.T, cotangent, preferred_element_type=jnp.float32),
        jnp.sum(cotangent.astype(jnp.float32), axis=0),
    )
    d_aggregate = jnp.dot(d_hidden, w_neigh.T, preferred_element_type=jnp.float32).astype(
        jnp.bfloat16
    )
    d_self = jnp.dot(d_hidden, w_self.T, preferred_element_type=jnp.float32)
    rim_total = adjoint_part(
        adjacency, d_aggregate, local_idx, block_rows, tile_size, per_row, width
    )
    reduced = reduce_grads(partials)
    grad_features = (d_self + rim_total).astype(jnp.bfloat16)
    return (
        embed,
        grad_features,
        reduced[0] * grad_scale,
        reduced[1] * grad_scale,
        reduced[2] * grad_scale,
        reduced[3] * grad_scale,
        reduced[4] * grad_scale,
    )


def solution(mesh):
    in_specs = (
        P(("row", "col"), None),
        P(("row", "col"), None),
        P(("row", "col"), None, None),
        P(),
        P(),
        P(),
        P(),
        P(),
        P(("row", "col"), None),
    )
    out_specs = (P(("row", "col"), None), P(("row", "col"), None), P(), P(), P(), P(), P())
    return jax.shard_map(local, mesh=mesh, in_specs=in_specs, out_specs=out_specs, check_vma=False)
```

profile of v0, /device:TPU:0, one launch (start us, length us, event | category | flops | bytes accessed | tf_op | source)
XLA Modules:
  0.0 271.6 jit_solution(532061286075266170)
XLA Ops:
  7.2 1.4 collective-permute-start.1
  8.7 6.4 %collective-permute-start = (bf16[1024,256]{1,0:T(8,128)(2,1)}, bf16[1024,256]{1,0:T(8,128)(2,1)}, u32[]{:S(2)}, u32[]{:S(2)}) collective-permute-start(bf16[1024,256]{1,0:T(8,128)(2,1)} %param.9), channel_id=1, source_target_pairs={{0,1},{1,2},{2,3},{3,4},{4,5},{5,6},{6,7},{7,8},{8,9},{9,10},{10,1... | collective-permute-start | bytes 1572872 | tf_op jit(solution)/shard_map/ppermute | solution.py:14
  16.1 3.9 %fusion.16 = f32[1024,1024]{1,0:T(8,128)} fusion(bf16[1024,256]{1,0:T(8,128)(2,1)} %param.9, bf16[256,1024]{1,0:T(8,128)(2,1)} %param.12), kind=kOutput, calls=%fused_computation.40 | convolution fusion | flops 536870912 | bytes 5242880 | tf_op jit(solution)/shard_map/dot_general | solution.py:69
  20.0 4.4 %collective-permute-done.1 = bf16[1024,256]{1,0:T(8,128)(2,1)S(1)} collective-permute-done((bf16[1024,256]{1,0:T(8,128)(2,1)}, bf16[1024,256]{1,0:T(8,128)(2,1)S(1)}, u32[]{:S(2)}, u32[]{:S(2)}) %collective-permute-start.1) | collective-permute-done | bytes 524320 | tf_op jit(solution)/shard_map/ppermute | solution.py:17
  24.4 2.3 collective-permute-done
  27.9 2.8 %gather_fusion = bf16[128,64,256]{2,1,0:T(8,128)(2,1)} fusion(bf16[48,64,256]{2,1,0:T(8,128)(2,1)S(1)} %bitcast.40, s32[1024]{0:T(1024)S(1)} %pad_clamp_fusion), kind=kCustom, calls=%fused_computation | custom fusion | bytes 8389120 | tf_op jit(solution)/shard_map/gather | solution.py:64
  30.7 3.7 %convolution_convert_fusion = bf16[16,64,256]{2,1,0:T(8,128)(2,1)S(1)} fusion(bf16[16,512,256]{2,1,0:T(8,128)(2,1)} %bitcast.41, s32[16,64,512]{2,1,0:T(8,128)} %param.11), kind=kOutput, calls=%fused_computation.18 | convolution fusion | flops 270270464 | bytes 6815744 | tf_op jit(solution)/shard_map/bij,bjf->bif/dot_general | solution.py:66
  34.7 2.0 multiply_convert_fusion
  36.7 3.4 %convert_reduce_fusion = (f32[1024]{0:T(1024)S(1)}, bf16[1024,1024]{1,0:T(8,128)(2,1)S(1)}) fusion(f32[1024,1024]{1,0:T(8,128)S(1)} %get-tuple-element.32, bf16[1024,256]{1,0:T(8,128)(2,1)S(1)} %copy-done.6, bf16[1024,256]{1,0:T(8,128)(2,1)S(1)} %copy-done.8), kind=kOutput, calls=%fused_computation.11 | convolution fusion | flops 559938560 | bytes 7344128 | tf_op jit(solution)/shard_map/dot_general | solution.py:78
  40.9 1.7 convolution_bitcast_fusion
  42.6 1.9 fusion.17
  44.5 4.5 %fusion.11 = f32[16,512,256]{2,1,0:T(8,128)} fusion(bf16[16,64,256]{2,1,0:T(8,128)(2,1)S(1)} %bitcast.44, s32[16,64,512]{2,1,0:T(8,128)S(1)} %copy-done.2), kind=kOutput, calls=%fused_computation.29 | convolution fusion | flops 270008320 | bytes 11010048 | tf_op jit(solution)/shard_map/bij,bif->bjf/dot_general | solution.py:34
  49.0 1.7 fusion.18
  50.7 2.1 broadcast_in_dim.10
  52.8 26.3 %scatter_fusion = f32[48,64,256]{2,1,0:T(8,128)} fusion(f32[48,64,256]{2,1,0:T(8,128)} %broadcast_in_dim.10, s32[128]{0:T(128)S(1)} %fusion.12, f32[128,64,256]{2,1,0:T(8,128)} %bitcast.39), kind=kCustom, calls=%fused_computation.1 | custom fusion | flops 2097152 | bytes 25166336 | tf_op jit(solution)/shard_map/scatter-add | solution.py:42
  79.2 3.7 %fusion.15 = (f32[16,64,256]{2,1,0:T(8,128)}, f32[16,64,256]{2,1,0:T(8,128)}, f32[16,64,256]{2,1,0:T(8,128)}) fusion(f32[48,64,256]{2,1,0:T(8,128)} %scatter_fusion), kind=kLoop, calls=%fused_computation.39 | loop fusion | bytes 6291456 | tf_op jit(solution)/shard_map/slice | solution.py:46
  82.9 1.4 collective-permute-start.3
  84.3 9.8 %collective-permute-start.2 = (f32[1024,256]{1,0:T(8,128)}, f32[1024,256]{1,0:T(8,128)}, u32[]{:S(2)}, u32[]{:S(2)}) collective-permute-start(f32[1024,256]{1,0:T(8,128)} %bitcast.7), channel_id=1, source_target_pairs={{0,1},{1,2},{2,3},{3,4},{4,5},{5,6},{6,7},{7,8},{8,9},{9,10},{10,1... | collective-permute-start | bytes 3145736 | tf_op jit(solution)/shard_map/ppermute | solution.py:14
  94.3 88.0 %all-reduce = (f32[1024]{0:T(1024)S(1)}, f32[256]{0:T(256)S(1)}) all-reduce(f32[1024]{0:T(1024)S(1)} %get-tuple-element.33, f32[256]{0:T(256)S(1)} %convert_reduce_fusion.1), channel_id=1, replica_groups=mesh['row'=8,'col'=4] {'row','col'}, use_global_device_ids=true, to_apply=%region_4.0 | all-reduce | flops 1280 | bytes 10240 | tf_op jit(solution)/shard_map/psum | solution.py:27
  183.4 3.2 %fusion.7 = bf16[1024,256]{1,0:T(8,128)(2,1)} fusion(bf16[1024,1024]{1,0:T(8,128)(2,1)} %copy-done.11, bf16[1024,256]{1,0:T(8,128)(2,1)} %param.15, f32[256]{0:T(256)S(1)} %copy-done.10), kind=kOutput, calls=%fused_computation.20 | convolution fusion | flops 537395200 | bytes 3146752 | tf_op jit(solution)/shard_map/dot_general | solution.py:75
  186.6 3.1 %fusion.10 = bf16[1024,256]{1,0:T(8,128)(2,1)} fusion(f32[1024,256]{1,0:T(8,128)} %collective-permute-done.3, f32[1024,256]{1,0:T(8,128)} %collective-permute-done.2, f32[16,64,256]{2,1,0:T(8,128)S(1)} %copy-done.3, bf16[1024,1024]{1,0:T(8,128)(2,1)S(1)} %get-tuple-element.34, bf16[256,1024]{1,0:T(8,128)(2,1)S(1)} %copy-done.5), kind=kOutput, calls=%fused_computation.24 | convolution fusion | flops 537919488 | bytes 6291456 | tf_op jit(solution)/shard_map/dot_general | solution.py:90
  189.7 68.4 %all-reduce.4.cloned.1.call-done = (f32[256,1024]{0,1:T(8,128)}, f32[256,1024]{0,1:T(8,128)}, f32[1024,256]{1,0:T(8,128)}) async-done(((f32[256,1024]{0,1:T(8,128)}, f32[256,1024]{0,1:T(8,128)}, f32[1024,256]{1,0:T(8,128)}), (f32[256,1024]{0,1:T(8,128)}, f32[256,1024]{0,1:T(8,128)}, f32[1024,256]{1,0:T(8,128)})) %all-reduce.4.cloned.1.call-update) | async-done | bytes 3145744 | tf_op jit(solution)/shard_map/psum | solution.py:27
  258.1 1.7 broadcast_multiply_fusion.1
  262.4 2.3 broadcast_multiply_fusion
  (42 shorter events, 7.2 us)
Async XLA Ops:
  7.2 27.3 %copy-start = (bf16[256,1024]{1,0:T(8,128)(2,1)S(1)}, bf16[256,1024]{1,0:T(8,128)(2,1)}, u32[]{:S(2)}) copy-start(bf16[256,1024]{1,0:T(8,128)(2,1)} %param.13) | copy-start | bytes 1572868
  7.2 250.9 %all-reduce.4.cloned.1.call-start = ((), (), s32[]{:S(2)}) async-start(), calls=%async_computation | async-start | bytes 6291456 | tf_op jit(solution)/shard_map/psum | solution.py:27
  7.2 17.2 %collective-permute-start.1 = (bf16[1024,256]{1,0:T(8,128)(2,1)}, bf16[1024,256]{1,0:T(8,128)(2,1)S(1)}, u32[]{:S(2)}, u32[]{:S(2)}) collective-permute-start(bf16[1024,256]{1,0:T(8,128)(2,1)} %param.9), channel_id=1, source_target_pairs={{1,0},{2,1},{3,2},{4,3},{5,4},{6,5},{7,6},{8,7},{9,8},{10,9},{11,1... | collective-permute-start | bytes 1572872 | tf_op jit(solution)/shard_map/ppermute | solution.py:17
  8.7 18.1 %collective-permute-start = (bf16[1024,256]{1,0:T(8,128)(2,1)}, bf16[1024,256]{1,0:T(8,128)(2,1)}, u32[]{:S(2)}, u32[]{:S(2)}) collective-permute-start(bf16[1024,256]{1,0:T(8,128)(2,1)} %param.9), channel_id=1, source_target_pairs={{0,1},{1,2},{2,3},{3,4},{4,5},{5,6},{6,7},{7,8},{8,9},{9,10},{10,1... | collective-permute-start | bytes 1572872 | tf_op jit(solution)/shard_map/ppermute | solution.py:14
  16.1 10.7 %copy-start.4 = (bf16[1024,256]{1,0:T(8,128)(2,1)S(1)}, bf16[1024,256]{1,0:T(8,128)(2,1)}, u32[]{:S(2)}) copy-start(bf16[1024,256]{1,0:T(8,128)(2,1)} %param.9) | copy-start | bytes 1572868
  30.7 4.0 %copy-start.1 = (f32[1024,1024]{1,0:T(8,128)S(1)}, f32[1024,1024]{1,0:T(8,128)}, u32[]{:S(2)}) copy-start(f32[1024,1024]{1,0:T(8,128)} %fusion.16) | copy-start | bytes 12582916
  30.7 4.0 %copy-start.9 = (f32[1024]{0:T(1024)S(1)}, f32[1024]{0:T(1024)}, u32[]{:S(2)}) copy-start(f32[1024]{0:T(1024)} %param.14) | copy-start | bytes 12292
  34.7 2.0 copy-start.6
  34.7 2.0 copy-start.8
  36.7 12.3 %copy-start.11 = (bf16[1024,1024]{1,0:T(8,128)(2,1)}, bf16[1024,1024]{1,0:T(8,128)(2,1)S(1)}, u32[]{:S(2)}) copy-start(bf16[1024,1024]{1,0:T(8,128)(2,1)S(1)} %get-tuple-element.31) | copy-start | bytes 6291460
  40.8 3.7 %copy-start.2 = (s32[16,64,512]{2,1,0:T(8,128)S(1)}, s32[16,64,512]{2,1,0:T(8,128)}, u32[]{:S(2)}) copy-start(s32[16,64,512]{2,1,0:T(8,128)} %param.11) | copy-start | bytes 6291460
  79.2 14.9 %copy-start.7 = (bf16[1024,256]{1,0:T(8,128)(2,1)S(1)}, bf16[1024,256]{1,0:T(8,128)(2,1)}, u32[]{:S(2)}) copy-start(bf16[1024,256]{1,0:T(8,128)(2,1)} %param.17) | copy-start | bytes 1572868
  79.2 104.2 %copy-start.10 = (f32[256]{0:T(256)S(1)}, f32[256]{0:T(256)}, u32[]{:S(2)}) copy-start(f32[256]{0:T(256)} %param.16) | copy-start | bytes 3076
  82.9 103.7 %copy-start.5 = (bf16[256,1024]{1,0:T(8,128)(2,1)S(1)}, bf16[256,1024]{1,0:T(8,128)(2,1)}, u32[]{:S(2)}) copy-start(bf16[256,1024]{1,0:T(8,128)(2,1)} %param.12) | copy-start | bytes 1572868
  82.9 103.7 %collective-permute-start.3 = (f32[1024,256]{1,0:T(8,128)}, f32[1024,256]{1,0:T(8,128)}, u32[]{:S(2)}, u32[]{:S(2)}) collective-permute-start(f32[1024,256]{1,0:T(8,128)} %bitcast.8), channel_id=1, source_target_pairs={{1,0},{2,1},{3,2},{4,3},{5,4},{6,5},{7,6},{8,7},{9,8},{10,9},{11,1... | collective-permute-start | bytes 3145736 | tf_op jit(solution)/shard_map/ppermute | solution.py:17
  84.3 102.3 %collective-permute-start.2 = (f32[1024,256]{1,0:T(8,128)}, f32[1024,256]{1,0:T(8,128)}, u32[]{:S(2)}, u32[]{:S(2)}) collective-permute-start(f32[1024,256]{1,0:T(8,128)} %bitcast.7), channel_id=1, source_target_pairs={{0,1},{1,2},{2,3},{3,4},{4,5},{5,6},{6,7},{7,8},{8,9},{9,10},{10,1... | collective-permute-start | bytes 3145736 | tf_op jit(solution)/shard_map/ppermute | solution.py:14
  182.2 4.4 %copy-start.3 = (f32[16,64,256]{2,1,0:T(8,128)S(1)}, f32[16,64,256]{2,1,0:T(8,128)}, u32[]{:S(2)}) copy-start(f32[16,64,256]{2,1,0:T(8,128)} %get-tuple-element.28) | copy-start | bytes 3145732
Sparse Core Ops, SparseCore 0:
  79.3 178.7 all-reduce.3
where the time goes:
time: 272 us
  blocking collectives  88 us (32%)
  waiting for transfers between devices  75.2 us (28%)
  other arithmetic  33.5 us (12%)
  matrix products  29.9 us (11%)
  starting transfers between devices  19.1 us (7%)
  between operations  14.2 us (5%)
  local copies, waits for them, and re-layouts  11.8 us (4%)
    psum x1, blocking collectives, reduce_grads(): lax.psum((partials[0], partials[1], partials[2], partials[3], partials[4]...  88 us
    psum x1, waiting for transfers between devices, reduce_grads(): lax.psum((partials[0], partials[1], partials[2], partials[3], partials[4]...  68.4 us
    scatter-add x1, other arithmetic, adjoint_part(): spread_sum = spread_sum.at[local_idx.reshape(-1)].add(spread)  26.3 us
    ppermute x2, starting transfers between devices, extended(): lax.ppermute(lax.slice_in_dim(block, block.shape[dim] - width, None, axis...  16.2 us
  transfers between devices with their start and end apart: 5, of which 3 were waited for; matrix products, arithmetic and copies ran while one was open for 6% of the time, Pallas kernels for 0%

commit v1 on v0

v1 whole, which is shorter than its diff:
```python
import functools
import math

import jax
import jax.numpy as jnp
from jax import lax
from jax.experimental import pallas as pl
from jax.experimental.pallas import tpu as pltpu
from jax.sharding import PartitionSpec as P

BF16 = jnp.bfloat16
F32 = jnp.float32
GELU_C = math.sqrt(2.0 / math.pi)
GELU_A = 0.044715
VMEM_LIMIT = 40 * 1024 * 1024
LANES = 128
HALVES = 8
QUARTERS = 4


def vmem():
    return pl.BlockSpec(memory_space=pltpu.VMEM)


def smem():
    return pl.BlockSpec(memory_space=pltpu.SMEM)


def params():
    return pltpu.CompilerParams(vmem_limit_bytes=VMEM_LIMIT)


def dot(a, b):
    return jnp.dot(a, b, preferred_element_type=F32)


def prepare_kernel(tile_scale, tw, x, cot, ws, wn, wo, adj, lhs, cot_t, wo_t, w_back, bias_sum):
    for b in range(tw.shape[0]):
        adj[b] = (tw[b].astype(F32) * tile_scale).astype(BF16)
    width = x.shape[1]
    lhs[...] = x[...].T
    cot_t[...] = cot[...].T
    wo_t[...] = wo[...].T
    w_back[:, :width] = wn[...].T
    w_back[:, width:] = ws[...].T
    bias_sum[...] = jnp.sum(cot[...].astype(F32), axis=0, keepdims=True)


def forward_kernel(
    place, cols, lo, x, hi, adj, x_t, cot, cot_t, ws, wn, bias, wo_t, hid, dh, keep, send, bias_sum,
    window, agg, left
):
    rows, width = x.shape
    hidden = ws.shape[1]
    blocks, tile, _ = adj.shape
    slots = cols.shape[1]
    first, me, z = place[0], place[1], place[2]
    window[:rows] = lo[...]
    window[rows : 2 * rows] = x[...]
    window[2 * rows :] = hi[...]
    for b in range(blocks):
        parts = []
        for s in range(slots):
            at = pl.multiple_of((cols[b, s] - first) * tile, tile)
            parts.append(window[pl.ds(at, tile), :])
        agg[b * tile : (b + 1) * tile, :] = dot(adj[b], jnp.concatenate(parts, axis=0)).astype(BF16)
    left[:width] = x_t[...]
    left[width:] = agg[...].T
    chunk = 2 * LANES
    piece = width // QUARTERS
    core = lax.rem(me, 2)
    pair = me // 2

    def one(c, carry):
        at = pl.ds(pl.multiple_of(c * chunk, chunk), chunk)
        ws_c, wn_c, wo_c, bias_c = ws[:, at], wn[:, at], wo_t[:, at], bias[:, at]
        total = jnp.zeros((1, chunk), F32)
        step = 256
        for r in range(0, rows, step):
            sl = slice(r, r + step)
            v = dot(x[sl], ws_c) + dot(agg[sl], wn_c) + bias_c
            da = dot(cot[sl], wo_c)
            sq = v * v
            t = jnp.tanh(v * (GELU_C + (GELU_C * GELU_A) * sq))
            half = 0.5 + 0.5 * t
            hid[sl, at] = (v * half).astype(BF16)
            slope = half + (0.5 * v) * (1.0 - t * t) * (GELU_C + (3.0 * GELU_C * GELU_A) * sq)
            d = (da * slope).astype(BF16)
            dh[sl, at] = d
            total = total + jnp.sum(d.astype(F32), axis=0, keepdims=True)
        bias_sum[:, at] = total
        g = dot(left[...], dh[:, at])
        g_out = dot(cot_t[...], hid[:, at])
        rel = jnp.bitwise_xor(c, pair)
        for t, value in enumerate((g[:width], g[width:], g_out)):
            mine = jnp.where(core == 0, value[:, :LANES], value[:, LANES:])
            other = jnp.where(core == 0, value[:, LANES:], value[:, :LANES]).astype(BF16)
            for k in range(QUARTERS):
                q = jnp.bitwise_xor(k, z)
                keep[rel, q, t * piece : (t + 1) * piece] = mine[k * piece : (k + 1) * piece]
                send[rel, q, t * piece : (t + 1) * piece] = other[k * piece : (k + 1) * piece]
        return carry

    lax.fori_loop(0, hidden // chunk, one, 0)


def backward_kernel(
    place, cols, adj, hid, dh, wo, bias_out, w_back, embed, own, to_low, to_high, total, d_agg
):
    rows, width = embed.shape
    blocks, tile, _ = adj.shape
    slots = cols.shape[1]
    first = place[0]
    step = 256
    for r in range(0, rows, step):
        sl = slice(r, r + step)
        both = dot(dh[sl], w_back[...])
        d_agg[sl] = both[:, :width].astype(BF16)
        total[rows + r : rows + r + step] = both[:, width:]
    total[:rows] = jnp.zeros((rows, width), F32)
    total[2 * rows :] = jnp.zeros((rows, width), F32)
    for b in range(blocks):
        spread = lax.dot_general(
            adj[b], d_agg[b * tile : (b + 1) * tile], (((0,), (0,)), ((), ())), preferred_element_type=F32
        )
        for s in range(slots):
            at = pl.multiple_of((cols[b, s] - first) * tile, tile)
            total[pl.ds(at, tile), :] += spread[s * tile : (s + 1) * tile]
    to_low[...] = total[:rows].astype(BF16)
    to_high[...] = total[2 * rows :].astype(BF16)
    own[...] = total[rows : 2 * rows]
    for r in range(0, rows, step):
        sl = slice(r, r + step)
        embed[sl] = (dot(hid[sl], wo[...]) + bias_out[...]).astype(BF16)


def unpack_kernel(scale, place, mine, other, g_self, g_neigh, g_out, turned):
    width = g_self.shape[0]
    piece = width // QUARTERS
    me, z = place[1], place[2]
    core = lax.rem(me, 2)
    pair = me // 2
    for j in range(HALVES // 2):
        for half, ref in enumerate((mine, other)):
            p = 2 * jnp.bitwise_xor(j, pair) + jnp.bitwise_xor(core, half)
            at = pl.ds(pl.multiple_of(p * LANES, LANES), LANES)
            for k in range(QUARTERS):
                to = pl.ds(pl.multiple_of(jnp.bitwise_xor(k, z) * piece, piece), piece)
                g_self[to, at] = ref[j, k, :piece].astype(F32) * scale
                g_neigh[to, at] = ref[j, k, piece : 2 * piece].astype(F32) * scale
                turned[to, :] = ref[j, k, 2 * piece :].astype(F32) * scale
            g_out[at, :] = turned[...].T


def swap(value, axis, bit):
    return lax.ppermute(value, axis, [(i, i ^ bit) for i in range(lax.axis_size(axis))])


def split(value):
    high = lax.reduce_precision(value, 8, 7)
    return high, lax.reduce_precision(value - high, 8, 7)


def packed(high, low):
    return jnp.concatenate([high.reshape(-1, LANES), low.reshape(-1, LANES)]).astype(BF16)


def swap_with_bias(value, bias, axis, bit):
    high, low = split(bias)
    extra = packed(high, low)
    count = extra.shape[0]
    message = jnp.concatenate([value.reshape(-1, LANES), extra])
    got = swap(message, axis, bit)
    back = got[-count:].astype(F32).reshape((2,) + bias.shape)
    theirs = got[:-count].reshape(value.shape)
    return theirs, (high + low) + (back[0] + back[1])


def all_reduce(keep, send, bias):
    got, bias = swap_with_bias(send, bias, "row", 1)
    acc = keep + got.astype(F32)
    a, b = acc[:, :2], acc[:, 2:]
    got_a, bias = swap_with_bias(a[1::2].astype(BF16), bias, "row", 2)
    got_b = swap(b[2:].astype(BF16), "row", 4)
    a, b = a[0::2] + got_a.astype(F32), b[:2] + got_b.astype(F32)
    got_a, bias = swap_with_bias(a[1].astype(BF16), bias, "row", 4)
    got_b = swap(b[1].astype(BF16), "row", 2)
    a, b = a[0] + got_a.astype(F32), b[0] + got_b.astype(F32)
    got, bias = swap_with_bias(jnp.stack([a[1], b[1]]).astype(BF16), bias, "col", 1)
    s = jnp.stack([a[0], b[0]]) + got.astype(F32)
    got, bias = swap_with_bias(s[1].astype(BF16), bias, "col", 2)
    s = s[0] + got.astype(F32)
    bit = HALVES
    while bit < lax.axis_size("row"):
        s = s.astype(BF16)
        got, bias = swap_with_bias(s, bias, "row", bit)
        s = s.astype(F32) + got.astype(F32)
        bit *= 2
    s = s.astype(BF16)
    s = jnp.stack([s, swap(s, "col", 2)])
    t = swap(s, "col", 1)
    a, b = jnp.stack([s[0], t[0]]), jnp.stack([s[1], t[1]])
    a, b = jnp.stack([a, swap(a, "row", 4)]), jnp.stack([b, swap(b, "row", 2)])
    far_a, far_b = swap(a, "row", 2), swap(b, "row", 4)
    a = jnp.stack([a, far_a], axis=1).reshape((4,) + a.shape[1:])
    b = jnp.concatenate([b, far_b])
    mine = jnp.concatenate([a, b], axis=1)
    return mine, swap(mine, "row", 1), bias


def local(x, cols, tw, ws, wn, bias_hidden, wo, bias_out, cot):
    rows, width = x.shape
    hidden = ws.shape[1]
    blocks, tile, depth = tw.shape
    both = ("row", "col")
    count = lax.axis_size(both)
    tile_scale = 0.25 / math.sqrt(depth)
    grad_scale = 1.0 / math.sqrt(rows * count)
    forward = [(i, i + 1) for i in range(count - 1)]
    backward = [(j, i) for i, j in forward]
    place = jnp.stack(
        [
            lax.axis_index(both) * blocks - blocks,
            lax.rem(lax.axis_index("row"), HALVES),
            lax.axis_index("col"),
        ]
    ).astype(jnp.int32)
    sds = jax.ShapeDtypeStruct
    low = lax.ppermute(x, both, forward)
    high = lax.ppermute(x, both, backward)
    adj, x_t, cot_t, wo_t, w_back, cot_sum = pl.pallas_call(
        functools.partial(prepare_kernel, tile_scale),
        out_shape=(
            sds((blocks, tile, depth), BF16),
            sds((width, rows), BF16),
            sds((width, rows), BF16),
            sds((width, hidden), BF16),
            sds((hidden, 2 * width), BF16),
            sds((1, width), F32),
        ),
        in_specs=[vmem()] * 6,
        out_specs=[vmem()] * 6,
        compiler_params=params(),
        cost_estimate=pl.CostEstimate(flops=4 * blocks * tile * depth, bytes_accessed=9 << 20, transcendentals=0),
        name="prepare",
    )(tw, x, cot, ws, wn, wo)
    piece = 3 * width // QUARTERS
    shape = (HALVES // 2, QUARTERS, piece, LANES)
    hid, dh, keep, send, hidden_sum = pl.pallas_call(
        forward_kernel,
        out_shape=(
            sds((rows, hidden), BF16),
            sds((rows, hidden), BF16),
            sds(shape, F32),
            sds(shape, BF16),
            sds((1, hidden), F32),
        ),
        in_specs=[smem(), smem()] + [vmem()] * 11,
        out_specs=[vmem()] * 5,
        scratch_shapes=[
            pltpu.VMEM((3 * rows, width), BF16),
            pltpu.VMEM((rows, width), BF16),
            pltpu.VMEM((2 * width, rows), BF16),
        ],
        compiler_params=params(),
        cost_estimate=pl.CostEstimate(
            flops=2 * rows * width * (6 * hidden + depth), bytes_accessed=14 << 20, transcendentals=rows * hidden
        ),
        name="forward",
    )(place, cols, low, x, high, adj, x_t, cot, cot_t, ws, wn, bias_hidden.reshape(1, -1), wo_t)
    embed, own, to_low, to_high = pl.pallas_call(
        backward_kernel,
        out_shape=(
            sds((rows, width), BF16),
            sds((rows, width), F32),
            sds((rows, width), BF16),
            sds((rows, width), BF16),
        ),
        in_specs=[smem(), smem()] + [vmem()] * 6,
        out_specs=[vmem()] * 4,
        scratch_shapes=[pltpu.VMEM((3 * rows, width), F32), pltpu.VMEM((rows, width), BF16)],
        compiler_params=params(),
        cost_estimate=pl.CostEstimate(
            flops=2 * rows * width * (3 * hidden + depth), bytes_accessed=10 << 20, transcendentals=0
        ),
        name="backward",
    )(place, cols, adj, hid, dh, wo, bias_out.reshape(1, -1), w_back)
    from_high = lax.ppermute(to_low, both, backward)
    from_low = lax.ppermute(to_high, both, forward)
    grad_features = (own + from_low.astype(F32) + from_high.astype(F32)).astype(BF16)
    bias = jnp.concatenate([hidden_sum.reshape(-1, width), cot_sum])
    bias = jnp.pad(bias, ((0, 8 - bias.shape[0]), (0, 0)))
    mine, other, bias = all_reduce(keep, send, bias)
    g_self, g_neigh, g_out = pl.pallas_call(
        functools.partial(unpack_kernel, grad_scale),
        out_shape=(sds((width, hidden), F32), sds((width, hidden), F32), sds((hidden, width), F32)),
        in_specs=[smem(), vmem(), vmem()],
        out_specs=[vmem()] * 3,
        scratch_shapes=[pltpu.VMEM((width, LANES), F32)],
        compiler_params=params(),
        cost_estimate=pl.CostEstimate(flops=3 * width * hidden, bytes_accessed=9 * width * hidden, transcendentals=0),
        name="unpack",
    )(place, mine, other)
    bias = bias * grad_scale
    top = hidden // width
    return embed, grad_features, g_self, g_neigh, bias[:top].reshape(-1), g_out, bias[top]


def solution(mesh):
    share = P(("row", "col"), None)
    in_specs = (share, share, P(("row", "col"), None, None), P(), P(), P(), P(), P(), share)
    out_specs = (share, share, P(), P(), P(), P(), P())
    return jax.shard_map(local, mesh=mesh, in_specs=in_specs, out_specs=out_specs, check_vma=False)
```

time: 272 us -> 125 us (0.46)
  blocking collectives: 88 us -> 0 us
  other arithmetic: 33.5 us -> 3.46 us
  matrix products: 29.9 us -> 0 us
  waiting for transfers between devices: 75.2 us -> 51.6 us
  Pallas kernels: 0 us -> 16.5 us
  local copies, waits for them, and re-layouts: 11.8 us -> 27.4 us
  between operations: 14.2 us -> 1.21 us
  starting transfers between devices: 19.1 us -> 24.1 us
    psum x1 -> x0, blocking collectives: 88 us -> none  [reduce_grads(): lax.psum((partials[0], partials[1], partials[2], partials[3], partials[4]...]
    psum x1 -> x0, waiting for transfers between devices: 68.4 us -> none  [reduce_grads(): lax.psum((partials[0], partials[1], partials[2], partials[3], partials[4]...]
    ppermute x4 -> x18, waiting for transfers between devices: 6.77 us -> 51.6 us  [the longest x14 32.8 us: swap(): lax.ppermute(value, axis, [(i, i ^ bit) for i in range(lax.axis_size(axis...]
    dot_general x11 -> x0, matrix products: 29.9 us -> none  [the longest x1 4.52 us: adjoint_part(): jnp.einsum('bij,bif->bjf', adjacency, d_aggregate.reshape(block_rows, til...]
    scatter-add x1 -> x0, other arithmetic: 26.3 us -> none  [adjoint_part(): spread_sum = spread_sum.at[local_idx.reshape(-1)].add(spread)]
    unnamed x26 -> x59, local copies, waits for them, and re-layouts: 2.93 us -> 21.3 us
    pallas_call x0 -> x4, Pallas kernels: none -> 16.5 us  [the longest x1 7.75 us: local(): pl.pallas_call(forward_kernel, out_shape=(sds((rows, hidden), BF16), sds(...]
    mul x4 -> x1, other arithmetic: 5.16 us -> 0.02 us  [local(): bias = bias * grad_scale]
  transfers between devices with their start and end apart: 5 -> 18, of which waited for: 3 -> 13; matrix products, arithmetic and copies ran while one was open for 6% -> 7% of each run, Pallas kernels for 0% -> 5%
where the time goes in v1:
time: 125 us; the launch traced here: 124 us
  waiting for transfers between devices  51.6 us (41%)
  local copies, waits for them, and re-layouts  27.4 us (22%)
  starting transfers between devices  24.1 us (19%)
  Pallas kernels  16.5 us (13%)
  other arithmetic  3.46 us (3%)
    ppermute x14, waiting for transfers between devices, swap(): lax.ppermute(value, axis, [(i, i ^ bit) for i in range(lax.axis_size(axis...  32.8 us
    unnamed x59, local copies, waits for them, and re-layouts  21.3 us
    ppermute x1, waiting for transfers between devices, local(): high = lax.ppermute(x, both, backward)  12.8 us
    ppermute x14, starting transfers between devices, swap(): lax.ppermute(value, axis, [(i, i ^ bit) for i in range(lax.axis_size(axis...  12 us
    pallas_call x1, Pallas kernels, local(): pl.pallas_call(forward_kernel, out_shape=(sds((rows, hidden), BF16), sds(...  7.75 us
    pallas_call x1, Pallas kernels, local(): pl.pallas_call(backward_kernel, out_shape=(sds((rows, width), BF16), sds(...  5.03 us
    ppermute x1, starting transfers between devices, local(): low = lax.ppermute(x, both, forward)  4.96 us
    ppermute x1, starting transfers between devices, local(): from_low = lax.ppermute(to_high, both, forward)  4.58 us
  transfers between devices with their start and end apart: 18, of which 13 were waited for; matrix products, arithmetic and copies ran while one was open for 7% of the time, Pallas kernels for 5%

profile of v1, /device:TPU:0, one launch (start us, length us, event | category | flops | bytes accessed | tf_op | source)
XLA Modules:
  0.0 124.3 jit_solution(16836710380833538632)
XLA Ops:
  0.6 5.0 %collective-permute-start = (bf16[1024,256]{1,0:T(8,128)(2,1)}, bf16[1024,256]{1,0:T(8,128)(2,1)S(1)}, u32[]{:S(2)}, u32[]{:S(2)}) collective-permute-start(bf16[1024,256]{1,0:T(8,128)(2,1)} %x.5), channel_id=1, source_target_pairs={{0,1},{1,2},{2,3},{3,4},{4,5},{5,6},{6,7},{7,8},{8,9},{9,10},{10,1... | collective-permute-start | bytes 1572872 | tf_op jit(solution)/shard_map/ppermute | solution.py:229
  7.7 1.6 %copy-done = s32[16,64,512]{2,1,0:T(8,128)S(1)} copy-done((s32[16,64,512]{2,1,0:T(8,128)S(1)}, s32[16,64,512]{2,1,0:T(8,128)}, u32[]{:S(2)}) %copy-start) | copy-done | bytes 2097176
  16.6 1.6 %collective-permute-done.lo = bf16[1024,256]{1,0:T(8,128)(2,1)S(1)} collective-permute-done((bf16[1024,256]{1,0:T(8,128)(2,1)}, bf16[1024,256]{1,0:T(8,128)(2,1)S(1)}, u32[]{:S(2)}, u32[]{:S(2)}) %collective-permute-start) | collective-permute-done | bytes 524320 | tf_op jit(solution)/shard_map/ppermute | solution.py:229
  19.0 12.8 %collective-permute-done.1.hi = bf16[1024,256]{1,0:T(8,128)(2,1)S(1)} collective-permute-done((bf16[1024,256]{1,0:T(8,128)(2,1)}, bf16[1024,256]{1,0:T(8,128)(2,1)S(1)}, u32[]{:S(2)}, u32[]{:S(2)}) %collective-permute-start.1) | collective-permute-done | bytes 524320 | tf_op jit(solution)/shard_map/ppermute | solution.py:230
  34.7 7.8 %forward.1 = (bf16[1024,1024]{1,0:T(8,128)(2,1)S(1)}, bf16[1024,1024]{1,0:T(8,128)(2,1)S(1)}, f32[4,4,192,128]{3,2,1,0:T(8,128)S(1)}, bf16[4,4,192,128]{3,2,1,0:T(8,128)(2,1)S(1)}, f32[1,1024]{1,0:T(1,128)S(1)}) custom-call(s32[3]{0:T(128)S(1)} %pad_add_fusion.place, s32[16,8]{1,0:T(8,128)S(1)} %copy.19.cols, bf16[1024,256]{1,0:T(8,128)(2,1)S(1)} %copy-done.14, ...), custom_call_target="tpu_custom_call" | custom-call | flops 3489660928 | bytes 14680064 | tf_op jit(solution)/shard_map/forward/pallas_call | solution.py:249
  46.6 2.3 %collective-permute-done.4 = bf16[3104,128]{1,0:T(8,128)(2,1)S(1)} collective-permute-done((bf16[3104,128]{1,0:T(8,128)(2,1)S(1)}, bf16[3104,128]{1,0:T(8,128)(2,1)S(1)}, u32[]{:S(2)}, u32[]{:S(2)}) %collective-permute-start.4) | collective-permute-done | bytes 794656 | tf_op jit(solution)/shard_map/ppermute | solution.py:156
  52.6 2.1 %slice.258 = bf16[4,2,192,128]{3,2,1,0:T(8,128)(2,1)} slice(f32[4,4,192,128]{3,2,1,0:T(8,128)} %copy-done.23), slice={[0:4], [0:2], [0:192], [0:128]} | slice | bytes 786432 | tf_op jit(solution)/shard_map/slice | solution.py:182
  55.8 2.5 %collective-permute-done.7 = bf16[2,2,192,128]{3,2,1,0:T(8,128)(2,1)} collective-permute-done((bf16[2,2,192,128]{3,2,1,0:T(8,128)(2,1)}, bf16[2,2,192,128]{3,2,1,0:T(8,128)(2,1)}, u32[]{:S(2)}, u32[]{:S(2)}) %collective-permute-start.7) | collective-permute-done | bytes 196640 | tf_op jit(solution)/shard_map/ppermute | solution.py:156
  61.6 1.6 %collective-permute-done.5 = bf16[800,128]{1,0:T(8,128)(2,1)S(1)} collective-permute-done((bf16[800,128]{1,0:T(8,128)(2,1)S(1)}, bf16[800,128]{1,0:T(8,128)(2,1)S(1)}, u32[]{:S(2)}, u32[]{:S(2)}) %collective-permute-start.5) | collective-permute-done | bytes 204832 | tf_op jit(solution)/shard_map/ppermute | solution.py:156
  65.2 4.6 %collective-permute-done.6 = bf16[416,128]{1,0:T(8,128)(2,1)S(1)} collective-permute-done((bf16[416,128]{1,0:T(8,128)(2,1)S(1)}, bf16[416,128]{1,0:T(8,128)(2,1)S(1)}, u32[]{:S(2)}, u32[]{:S(2)}) %collective-permute-start.6) | collective-permute-done | bytes 106528 | tf_op jit(solution)/shard_map/ppermute | solution.py:156
  70.6 4.3 %collective-permute-done.9 = bf16[416,128]{1,0:T(8,128)(2,1)S(1)} collective-permute-done((bf16[416,128]{1,0:T(8,128)(2,1)S(1)}, bf16[416,128]{1,0:T(8,128)(2,1)S(1)}, u32[]{:S(2)}, u32[]{:S(2)}) %collective-permute-start.9) | collective-permute-done | bytes 106528 | tf_op jit(solution)/shard_map/ppermute | solution.py:156
  75.7 5.3 %collective-permute-done.10 = bf16[224,128]{1,0:T(8,128)(2,1)S(1)} collective-permute-done((bf16[224,128]{1,0:T(8,128)(2,1)S(1)}, bf16[224,128]{1,0:T(8,128)(2,1)S(1)}, u32[]{:S(2)}, u32[]{:S(2)}) %collective-permute-start.10) | collective-permute-done | bytes 57376 | tf_op jit(solution)/shard_map/ppermute | solution.py:156
  81.1 5.2 %collective-permute-done.11 = bf16[192,128]{1,0:T(8,128)(2,1)S(1)} collective-permute-done((bf16[192,128]{1,0:T(8,128)(2,1)S(1)}, bf16[192,128]{1,0:T(8,128)(2,1)S(1)}, u32[]{:S(2)}, u32[]{:S(2)}) %collective-permute-start.11) | collective-permute-done | bytes 49184 | tf_op jit(solution)/shard_map/ppermute | solution.py:156
  86.5 1.6 %copy-done.20 = bf16[1024,1024]{1,0:T(8,128)(2,1)S(1)} copy-done((bf16[1024,1024]{1,0:T(8,128)(2,1)S(1)}, bf16[1024,1024]{1,0:T(8,128)(2,1)}, u32[]{:S(2)}) %copy-start.20) | copy-done | bytes 2097176
  88.1 1.6 %copy-done.22 = bf16[1024,1024]{1,0:T(8,128)(2,1)S(1)} copy-done((bf16[1024,1024]{1,0:T(8,128)(2,1)S(1)}, bf16[1024,1024]{1,0:T(8,128)(2,1)}, u32[]{:S(2)}) %copy-start.22) | copy-done | bytes 2097176
  89.7 5.0 %backward.1 = (bf16[1024,256]{1,0:T(8,128)(2,1)}, f32[1024,256]{1,0:T(8,128)S(1)}, bf16[1024,256]{1,0:T(8,128)(2,1)S(1)}, bf16[1024,256]{1,0:T(8,128)(2,1)S(1)}) custom-call(s32[3]{0:T(128)S(1)} %pad_add_fusion.place, s32[16,8]{1,0:T(8,128)S(1)} %copy.19.cols, bf16[16,64,512]{2,1,0:T(8,128)(2,1)S(1)} %get-tuple-element.25.adj, ...), custom_call_target="tpu_custom_call" | custom-call | flops 1879048192 | bytes 10485760 | tf_op jit(solution)/shard_map/backward/pallas_call | solution.py:271
  96.0 4.6 %collective-permute-start.2 = (bf16[1024,256]{1,0:T(8,128)(2,1)S(1)}, bf16[1024,256]{1,0:T(8,128)(2,1)S(1)}, u32[]{:S(2)}, u32[]{:S(2)}) collective-permute-start(bf16[1024,256]{1,0:T(8,128)(2,1)S(1)} %get-tuple-element.34), channel_id=1, source_target_pairs={{0,1},{1,2},{2,3},{3,4},{4,5},{5,6},{6,7},{7,8},{8,9},{9,10},{10,1... | collective-permute-start | bytes 1572872 | tf_op jit(solution)/shard_map/ppermute | solution.py:289
  101.0 1.6 %collective-permute-start.13 = (bf16[2,192,128]{2,1,0:T(8,128)(2,1)S(1)}, bf16[2,192,128]{2,1,0:T(8,128)(2,1)S(1)}, u32[]{:S(2)}, u32[]{:S(2)}) collective-permute-start(bf16[2,192,128]{2,1,0:T(8,128)(2,1)S(1)} %get-tuple-element.50), channel_id=1, source_target_pairs={{0,16},{4,20},{8,24},{12,28},{16,0},{20,4},{24,8},{28,12},{1,17},{... | collective-permute-start | bytes 294920 | tf_op jit(solution)/shard_map/ppermute | solution.py:156
  102.6 3.9 %collective-permute-done.15 = bf16[2,192,128]{2,1,0:T(8,128)(2,1)S(1)} collective-permute-done((bf16[2,192,128]{2,1,0:T(8,128)(2,1)S(1)}, bf16[2,192,128]{2,1,0:T(8,128)(2,1)S(1)}, u32[]{:S(2)}, u32[]{:S(2)}) %collective-permute-start.15) | collective-permute-done | bytes 98336 | tf_op jit(solution)/shard_map/ppermute | solution.py:156
  106.7 1.9 %collective-permute-start.14 = (bf16[2,2,192,128]{3,2,1,0:T(8,128)(2,1)S(1)}, bf16[2,2,192,128]{3,2,1,0:T(8,128)(2,1)S(1)}, u32[]{:S(2)}, u32[]{:S(2)}) collective-permute-start(bf16[2,2,192,128]{3,2,1,0:T(8,128)(2,1)S(1)} %get-tuple-element.48), channel_id=1, source_target_pairs={{0,8},{4,12},{8,0},{12,4},{16,24},{20,28},{24,16},{28,20},{1,9},{5... | collective-permute-start | bytes 589832 | tf_op jit(solution)/shard_map/ppermute | solution.py:156
  108.6 4.3 %collective-permute-done.2 = bf16[1024,256]{1,0:T(8,128)(2,1)S(1)} collective-permute-done((bf16[1024,256]{1,0:T(8,128)(2,1)S(1)}, bf16[1024,256]{1,0:T(8,128)(2,1)S(1)}, u32[]{:S(2)}, u32[]{:S(2)}) %collective-permute-start.2) | collective-permute-done | bytes 524320 | tf_op jit(solution)/shard_map/ppermute | solution.py:289
  113.9 2.5 %collective-permute-done.14 = bf16[2,2,192,128]{3,2,1,0:T(8,128)(2,1)S(1)} collective-permute-done((bf16[2,2,192,128]{3,2,1,0:T(8,128)(2,1)S(1)}, bf16[2,2,192,128]{3,2,1,0:T(8,128)(2,1)S(1)}, u32[]{:S(2)}, u32[]{:S(2)}) %collective-permute-start.14) | collective-permute-done | bytes 196640 | tf_op jit(solution)/shard_map/ppermute | solution.py:156
  116.5 3.2 %collective-permute-start.17 = (bf16[4,4,192,128]{3,2,1,0:T(8,128)(2,1)S(1)}, bf16[4,4,192,128]{3,2,1,0:T(8,128)(2,1)S(1)}, u32[]{:S(2)}, u32[]{:S(2)}) collective-permute-start(bf16[4,4,192,128]{3,2,1,0:T(8,128)(2,1)S(1)} %maximum_maximum_fusion.mine), channel_id=1, source_target_pairs={{0,4},{4,0},{8,12},{12,8},{16,20},{20,16},{24,28},{28,24},{1,5},{5... | collective-permute-start | bytes 2359304 | tf_op jit(solution)/shard_map/ppermute | solution.py:156
  121.6 2.7 %unpack.1 = (f32[256,1024]{1,0:T(8,128)}, f32[256,1024]{1,0:T(8,128)}, f32[1024,256]{1,0:T(8,128)}) custom-call(s32[3]{0:T(128)S(1)} %pad_add_fusion.place, bf16[4,4,192,128]{3,2,1,0:T(8,128)(2,1)S(1)} %maximum_maximum_fusion.mine, bf16[4,4,192,128]{3,2,1,0:T(8,128)(2,1)S(1)} %collective-permute-done.17.other), custom_call_target="tpu_custom_call" | custom-call | flops 786432 | bytes 2359296 | tf_op jit(solution)/shard_map/unpack/pallas_call | solution.py:294
  (152 shorter events, 33.7 us)
Async XLA Ops:
  0.6 17.6 %collective-permute-start = (bf16[1024,256]{1,0:T(8,128)(2,1)}, bf16[1024,256]{1,0:T(8,128)(2,1)S(1)}, u32[]{:S(2)}, u32[]{:S(2)}) collective-permute-start(bf16[1024,256]{1,0:T(8,128)(2,1)} %x.5), channel_id=1, source_target_pairs={{0,1},{1,2},{2,3},{3,4},{4,5},{5,6},{6,7},{7,8},{8,9},{9,10},{10,1... | collective-permute-start | bytes 1572872 | tf_op jit(solution)/shard_map/ppermute | solution.py:229
  5.6 26.2 %collective-permute-start.1 = (bf16[1024,256]{1,0:T(8,128)(2,1)}, bf16[1024,256]{1,0:T(8,128)(2,1)S(1)}, u32[]{:S(2)}, u32[]{:S(2)}) collective-permute-start(bf16[1024,256]{1,0:T(8,128)(2,1)} %x.5), channel_id=1, source_target_pairs={{1,0},{2,1},{3,2},{4,3},{5,4},{6,5},{7,6},{8,7},{9,8},{10,9},{11,1... | collective-permute-start | bytes 1572872 | tf_op jit(solution)/shard_map/ppermute | solution.py:230
  14.5 18.1 %copy-start.6 = (bf16[256,1024]{1,0:T(8,128)(2,1)S(1)}, bf16[256,1024]{1,0:T(8,128)(2,1)}, u32[]{:S(2)}) copy-start(bf16[256,1024]{1,0:T(8,128)(2,1)} %ws.3) | copy-start | bytes 1572868
  14.5 18.1 %copy-start.8 = (bf16[256,1024]{1,0:T(8,128)(2,1)S(1)}, bf16[256,1024]{1,0:T(8,128)(2,1)}, u32[]{:S(2)}) copy-start(bf16[256,1024]{1,0:T(8,128)(2,1)} %wn.3) | copy-start | bytes 1572868
  14.5 18.1 %copy-start.17 = (f32[1024]{0:T(1024)S(1)}, f32[1024]{0:T(1024)}, u32[]{:S(2)}) copy-start(f32[1024]{0:T(1024)} %param.14) | copy-start | bytes 12292
  46.5 2.4 %collective-permute-start.4 = (bf16[3104,128]{1,0:T(8,128)(2,1)S(1)}, bf16[3104,128]{1,0:T(8,128)(2,1)S(1)}, u32[]{:S(2)}, u32[]{:S(2)}) collective-permute-start(bf16[3104,128]{1,0:T(8,128)(2,1)S(1)} %pad_maximum_fusion), channel_id=1, source_target_pairs={{0,4},{4,0},{8,12},{12,8},{16,20},{20,16},{24,28},{28,24},{1,5},{5... | collective-permute-start | bytes 2383880 | tf_op jit(solution)/shard_map/ppermute | solution.py:156
  51.0 7.3 %collective-permute-start.7 = (bf16[2,2,192,128]{3,2,1,0:T(8,128)(2,1)}, bf16[2,2,192,128]{3,2,1,0:T(8,128)(2,1)}, u32[]{:S(2)}, u32[]{:S(2)}) collective-permute-start(bf16[2,2,192,128]{3,2,1,0:T(8,128)(2,1)} %slice.254), channel_id=1, source_target_pairs={{0,16},{4,20},{8,24},{12,28},{16,0},{20,4},{24,8},{28,12},{1,17},{... | collective-permute-start | bytes 589832 | tf_op jit(solution)/shard_map/ppermute | solution.py:156
  55.7 7.5 %collective-permute-start.5 = (bf16[800,128]{1,0:T(8,128)(2,1)S(1)}, bf16[800,128]{1,0:T(8,128)(2,1)S(1)}, u32[]{:S(2)}, u32[]{:S(2)}) collective-permute-start(bf16[800,128]{1,0:T(8,128)(2,1)S(1)} %pad_maximum_fusion.2), channel_id=1, source_target_pairs={{0,8},{4,12},{8,0},{12,4},{16,24},{20,28},{24,16},{28,20},{1,9},{5... | collective-permute-start | bytes 614408 | tf_op jit(solution)/shard_map/ppermute | solution.py:156
  60.0 5.0 %collective-permute-start.8 = (bf16[2,192,128]{2,1,0:T(8,128)(2,1)S(1)}, bf16[2,192,128]{2,1,0:T(8,128)(2,1)S(1)}, u32[]{:S(2)}, u32[]{:S(2)}) collective-permute-start(bf16[2,192,128]{2,1,0:T(8,128)(2,1)S(1)} %fusion.2), channel_id=1, source_target_pairs={{0,8},{4,12},{8,0},{12,4},{16,24},{20,28},{24,16},{28,20},{1,9},{5... | collective-permute-start | bytes 294920 | tf_op jit(solution)/shard_map/ppermute | solution.py:156
  65.0 4.8 %collective-permute-start.6 = (bf16[416,128]{1,0:T(8,128)(2,1)S(1)}, bf16[416,128]{1,0:T(8,128)(2,1)S(1)}, u32[]{:S(2)}, u32[]{:S(2)}) collective-permute-start(bf16[416,128]{1,0:T(8,128)(2,1)S(1)} %pad_maximum_fusion.7), channel_id=1, source_target_pairs={{0,16},{4,20},{8,24},{12,28},{16,0},{20,4},{24,8},{28,12},{1,17},{... | collective-permute-start | bytes 319496 | tf_op jit(solution)/shard_map/ppermute | solution.py:156
  65.1 21.3 %copy-start.10 = (bf16[1024,256]{1,0:T(8,128)(2,1)S(1)}, bf16[1024,256]{1,0:T(8,128)(2,1)}, u32[]{:S(2)}) copy-start(bf16[1024,256]{1,0:T(8,128)(2,1)} %wo.3) | copy-start | bytes 1572868
  65.1 21.3 %copy-start.12 = (bf16[1024,512]{1,0:T(8,128)(2,1)S(1)}, bf16[1024,512]{1,0:T(8,128)(2,1)}, u32[]{:S(2)}) copy-start(bf16[1024,512]{1,0:T(8,128)(2,1)} %copy-done.11) | copy-start | bytes 3145732
  65.1 21.3 %copy-start.18 = (f32[256]{0:T(256)S(1)}, f32[256]{0:T(256)}, u32[]{:S(2)}) copy-start(f32[256]{0:T(256)} %param.16) | copy-start | bytes 3076
  69.9 5.0 %collective-permute-start.9 = (bf16[416,128]{1,0:T(8,128)(2,1)S(1)}, bf16[416,128]{1,0:T(8,128)(2,1)S(1)}, u32[]{:S(2)}, u32[]{:S(2)}) collective-permute-start(bf16[416,128]{1,0:T(8,128)(2,1)S(1)} %pad_maximum_fusion.8), channel_id=1, source_target_pairs={{0,1},{1,0},{2,3},{3,2},{4,5},{5,4},{6,7},{7,6},{8,9},{9,8},{10,11... | collective-permute-start | bytes 319496 | tf_op jit(solution)/shard_map/ppermute | solution.py:156
  75.0 6.0 %collective-permute-start.10 = (bf16[224,128]{1,0:T(8,128)(2,1)S(1)}, bf16[224,128]{1,0:T(8,128)(2,1)S(1)}, u32[]{:S(2)}, u32[]{:S(2)}) collective-permute-start(bf16[224,128]{1,0:T(8,128)(2,1)S(1)} %pad_maximum_fusion.11), channel_id=1, source_target_pairs={{0,2},{1,3},{2,0},{3,1},{4,6},{5,7},{6,4},{7,5},{8,10},{9,11},{10,... | collective-permute-start | bytes 172040 | tf_op jit(solution)/shard_map/ppermute | solution.py:156
  81.0 5.3 %collective-permute-start.11 = (bf16[192,128]{1,0:T(8,128)(2,1)S(1)}, bf16[192,128]{1,0:T(8,128)(2,1)S(1)}, u32[]{:S(2)}, u32[]{:S(2)}) collective-permute-start(bf16[192,128]{1,0:T(8,128)(2,1)S(1)} %fusion.4), channel_id=1, source_target_pairs={{0,2},{1,3},{2,0},{3,1},{4,6},{5,7},{6,4},{7,5},{8,10},{9,11},{10,... | collective-permute-start | bytes 147464 | tf_op jit(solution)/shard_map/ppermute | solution.py:156
  86.3 14.2 %collective-permute-start.12 = (bf16[2,192,128]{2,1,0:T(8,128)(2,1)S(1)}, bf16[2,192,128]{2,1,0:T(8,128)(2,1)S(1)}, u32[]{:S(2)}, u32[]{:S(2)}) collective-permute-start(bf16[2,192,128]{2,1,0:T(8,128)(2,1)S(1)} %pad_maximum_fusion.5), channel_id=1, source_target_pairs={{0,1},{1,0},{2,3},{3,2},{4,5},{5,4},{6,7},{7,6},{8,9},{9,8},{10,11... | collective-permute-start | bytes 294920 | tf_op jit(solution)/shard_map/ppermute | solution.py:156
  94.7 13.9 %collective-permute-start.3 = (bf16[1024,256]{1,0:T(8,128)(2,1)S(1)}, bf16[1024,256]{1,0:T(8,128)(2,1)S(1)}, u32[]{:S(2)}, u32[]{:S(2)}) collective-permute-start(bf16[1024,256]{1,0:T(8,128)(2,1)S(1)} %get-tuple-element.35), channel_id=1, source_target_pairs={{1,0},{2,1},{3,2},{4,3},{5,4},{6,5},{7,6},{8,7},{9,8},{10,9},{11,1... | collective-permute-start | bytes 1572872 | tf_op jit(solution)/shard_map/ppermute | solution.py:288
  96.0 16.9 %collective-permute-start.2 = (bf16[1024,256]{1,0:T(8,128)(2,1)S(1)}, bf16[1024,256]{1,0:T(8,128)(2,1)S(1)}, u32[]{:S(2)}, u32[]{:S(2)}) collective-permute-start(bf16[1024,256]{1,0:T(8,128)(2,1)S(1)} %get-tuple-element.34), channel_id=1, source_target_pairs={{0,1},{1,2},{2,3},{3,4},{4,5},{5,6},{6,7},{7,8},{8,9},{9,10},{10,1... | collective-permute-start | bytes 1572872 | tf_op jit(solution)/shard_map/ppermute | solution.py:289
  100.6 5.9 %collective-permute-start.15 = (bf16[2,192,128]{2,1,0:T(8,128)(2,1)S(1)}, bf16[2,192,128]{2,1,0:T(8,128)(2,1)S(1)}, u32[]{:S(2)}, u32[]{:S(2)}) collective-permute-start(bf16[2,192,128]{2,1,0:T(8,128)(2,1)S(1)} %get-tuple-element.54), channel_id=1, source_target_pairs={{0,8},{4,12},{8,0},{12,4},{16,24},{20,28},{24,16},{28,20},{1,9},{5... | collective-permute-start | bytes 294920 | tf_op jit(solution)/shard_map/ppermute | solution.py:156
  101.0 5.7 %collective-permute-start.13 = (bf16[2,192,128]{2,1,0:T(8,128)(2,1)S(1)}, bf16[2,192,128]{2,1,0:T(8,128)(2,1)S(1)}, u32[]{:S(2)}, u32[]{:S(2)}) collective-permute-start(bf16[2,192,128]{2,1,0:T(8,128)(2,1)S(1)} %get-tuple-element.50), channel_id=1, source_target_pairs={{0,16},{4,20},{8,24},{12,28},{16,0},{20,4},{24,8},{28,12},{1,17},{... | collective-permute-start | bytes 294920 | tf_op jit(solution)/shard_map/ppermute | solution.py:156
  106.6 9.8 %collective-permute-start.16 = (bf16[2,2,192,128]{3,2,1,0:T(8,128)(2,1)S(1)}, bf16[2,2,192,128]{3,2,1,0:T(8,128)(2,1)S(1)}, u32[]{:S(2)}, u32[]{:S(2)}) collective-permute-start(bf16[2,2,192,128]{3,2,1,0:T(8,128)(2,1)S(1)} %pad_maximum_fusion.4), channel_id=1, source_target_pairs={{0,16},{4,20},{8,24},{12,28},{16,0},{20,4},{24,8},{28,12},{1,17},{... | collective-permute-start | bytes 589832 | tf_op jit(solution)/shard_map/ppermute | solution.py:156
  106.7 9.6 %collective-permute-start.14 = (bf16[2,2,192,128]{3,2,1,0:T(8,128)(2,1)S(1)}, bf16[2,2,192,128]{3,2,1,0:T(8,128)(2,1)S(1)}, u32[]{:S(2)}, u32[]{:S(2)}) collective-permute-start(bf16[2,2,192,128]{3,2,1,0:T(8,128)(2,1)S(1)} %get-tuple-element.48), channel_id=1, source_target_pairs={{0,8},{4,12},{8,0},{12,4},{16,24},{20,28},{24,16},{28,20},{1,9},{5... | collective-permute-start | bytes 589832 | tf_op jit(solution)/shard_map/ppermute | solution.py:156
  116.5 5.1 %collective-permute-start.17 = (bf16[4,4,192,128]{3,2,1,0:T(8,128)(2,1)S(1)}, bf16[4,4,192,128]{3,2,1,0:T(8,128)(2,1)S(1)}, u32[]{:S(2)}, u32[]{:S(2)}) collective-permute-start(bf16[4,4,192,128]{3,2,1,0:T(8,128)(2,1)S(1)} %maximum_maximum_fusion.mine), channel_id=1, source_target_pairs={{0,4},{4,0},{8,12},{12,8},{16,20},{20,16},{24,28},{28,24},{1,5},{5... | collective-permute-start | bytes 2359304 | tf_op jit(solution)/shard_map/ppermute | solution.py:156
  (23 other events, 77.2 us)

commit v2 on v1

v2 whole, which is shorter than its diff:
```python
import functools
import math

import jax
import jax.numpy as jnp
from jax import lax
from jax.experimental import pallas as pl
from jax.experimental.pallas import tpu as pltpu
from jax.sharding import PartitionSpec as P

BF16 = jnp.bfloat16
F32 = jnp.float32
GELU_C = math.sqrt(2.0 / math.pi)
GELU_A = 0.044715
LANES = 128
HALVES = 8
QUARTERS = 4
BIAS_ROWS = 16


def vmem():
    return pl.BlockSpec(memory_space=pltpu.VMEM)


def smem():
    return pl.BlockSpec(memory_space=pltpu.SMEM)


def params(mib):
    return pltpu.CompilerParams(vmem_limit_bytes=mib * 1024 * 1024)


def dot(a, b):
    return jnp.dot(a, b, preferred_element_type=F32)


def prepare_kernel(
    tile_scale, tw, x, cot, ws, wn, wo, bias, adj, x_t, cot_t, wn_t, ws_t, pre, half_act, bias_sum
):
    rows, width = x.shape
    for b in range(tw.shape[0]):
        adj[b] = (tw[b].astype(F32) * tile_scale).astype(BF16)
    x_t[...] = x[...].T
    cot_t[...] = cot[...].T
    wn_t[...] = wn[...].T
    ws_t[...] = ws[...].T
    bias_sum[...] = jnp.sum(cot[...].astype(F32), axis=0, keepdims=True)
    wo_t = wo[...].T
    step = 256
    for r in range(0, rows, step):
        pre[r : r + step] = dot(x[r : r + step], ws[...]) + bias[...]
        half_act[r : r + step] = dot(cot[r : r + step], wo_t) * 0.5


def forward_kernel(
    place, cols, lo, x, hi, adj, x_t, cot_t, wn, pre, half_act, cot_sum, hid, dh, keep, send, bias,
    window, agg, left, sums
):
    rows, width = x.shape
    hidden = wn.shape[1]
    blocks, tile, _ = adj.shape
    slots = cols.shape[1]
    first, me, z = place[0], place[1], place[2]
    window[:rows] = lo[...]
    window[rows : 2 * rows] = x[...]
    window[2 * rows :] = hi[...]
    for b in range(blocks):
        parts = []
        for s in range(slots):
            at = pl.multiple_of((cols[b, s] - first) * tile, tile)
            parts.append(window[pl.ds(at, tile), :])
        agg[b * tile : (b + 1) * tile, :] = dot(adj[b], jnp.concatenate(parts, axis=0)).astype(BF16)
    left[:width] = x_t[...]
    left[width : 2 * width] = agg[...].T
    left[2 * width :] = jnp.ones((BIAS_ROWS, rows), BF16)
    chunk = 2 * LANES
    piece = width // QUARTERS
    core = lax.rem(me, 2)
    pair = me // 2
    sums[...] = jnp.zeros(sums.shape, F32)
    step = 256
    for c in range(hidden // chunk):
        at = slice(c * chunk, (c + 1) * chunk)
        for r in range(0, rows, step):
            sl = slice(r, r + step)
            v = dot(agg[sl], wn[:, at]) + pre[sl, at]
            sq = v * v
            t = jnp.tanh(v * (GELU_C + (GELU_C * GELU_A) * sq))
            h = 1.0 + t
            p = v * h
            hid[sl, at] = (0.5 * p).astype(BF16)
            slope = h + p * (GELU_C + (3.0 * GELU_C * GELU_A) * sq) * (1.0 - t)
            dh[sl, at] = (half_act[sl, at] * slope).astype(BF16)
        g = dot(left[...], dh[:, at])
        g_out = dot(cot_t[...], hid[:, at])
        for half in range(2):
            sums[2 * c + half : 2 * c + half + 1] = g[2 * width : 2 * width + 1, half * LANES : (half + 1) * LANES]
        base = jnp.bitwise_xor(c, pair) * QUARTERS
        for t, value in enumerate((g[:width], g[width : 2 * width], g_out)):
            mine = jnp.where(core == 0, value[:, :LANES], value[:, LANES:])
            other = jnp.where(core == 0, value[:, LANES:], value[:, :LANES]).astype(BF16)
            for k in range(QUARTERS):
                to = pl.multiple_of((base + jnp.bitwise_xor(k, z)) * (3 * piece) + t * piece, piece)
                keep[pl.ds(to, piece)] = mine[k * piece : (k + 1) * piece]
                send[pl.ds(to, piece)] = other[k * piece : (k + 1) * piece]
    top = hidden // LANES
    for i in range(width // LANES):
        sums[top + i : top + i + 1] = cot_sum[:, i * LANES : (i + 1) * LANES]
    high = sums[...].astype(BF16)
    low = (sums[...] - high.astype(F32)).astype(BF16)
    bias[...] = high.astype(F32) + low.astype(F32)
    end = send.shape[0] - 2 * BIAS_ROWS
    send[end : end + BIAS_ROWS] = high
    send[end + BIAS_ROWS :] = low


def spread_kernel(place, cols, adj, dh, wn_t, own, to_low, to_high, total, d_agg):
    rows, width = own.shape
    blocks, tile, _ = adj.shape
    slots = cols.shape[1]
    first = place[0]
    step = 256
    for r in range(0, rows, step):
        d_agg[r : r + step] = dot(dh[r : r + step], wn_t[...]).astype(BF16)
    total[...] = jnp.zeros(total.shape, F32)
    for b in range(blocks):
        spread = lax.dot_general(
            adj[b], d_agg[b * tile : (b + 1) * tile], (((0,), (0,)), ((), ())), preferred_element_type=F32
        )
        for s in range(slots):
            at = pl.multiple_of((cols[b, s] - first) * tile, tile)
            total[pl.ds(at, tile), :] += spread[s * tile : (s + 1) * tile]
    to_low[...] = total[:rows].astype(BF16)
    to_high[...] = total[2 * rows :].astype(BF16)
    own[...] = total[rows : 2 * rows]


def finish_kernel(hid, dh, wo, bias_out, ws_t, own, embed, near):
    rows = embed.shape[0]
    step = 256
    for r in range(0, rows, step):
        sl = slice(r, r + step)
        near[sl] = own[sl] + dot(dh[sl], ws_t[...])
        embed[sl] = (dot(hid[sl], wo[...]) + bias_out[...]).astype(BF16)


def unpack_kernel(scale, half, place, src, *refs):
    g_self, g_neigh, g_out, blocks, turned, flipped, sems = refs[-7:]
    width = g_self.shape[0]
    piece = width // QUARTERS
    me, z = place[1], place[2]
    copies = []
    for j in range(HALVES // 2):
        p = 2 * jnp.bitwise_xor(j, me // 2) + jnp.bitwise_xor(lax.rem(me, 2), half)
        at = pl.ds(pl.multiple_of(p * LANES, LANES), LANES)
        for k in range(QUARTERS):
            to = pl.ds(pl.multiple_of(jnp.bitwise_xor(k, z) * piece, piece), piece)
            blocks[0, j, to] = src[j, k, :piece].astype(F32) * scale
            blocks[1, j, to] = src[j, k, piece : 2 * piece].astype(F32) * scale
            turned[j, to] = src[j, k, 2 * piece :].astype(F32) * scale
        flipped[j] = turned[j].T
        copies.append(pltpu.make_async_copy(blocks.at[0, j], g_self.at[:, at], sems.at[j]))
        copies.append(pltpu.make_async_copy(blocks.at[1, j], g_neigh.at[:, at], sems.at[4 + j]))
        copies.append(pltpu.make_async_copy(flipped.at[j], g_out.at[at], sems.at[8 + j]))
        for copy in copies[-3:]:
            copy.start()
    for copy in copies:
        copy.wait()


def unpack(scale, half, place, src, width, hidden, before=()):
    sds = jax.ShapeDtypeStruct
    anywhere = pl.BlockSpec(memory_space=pl.ANY)
    return pl.pallas_call(
        functools.partial(unpack_kernel, scale, half),
        out_shape=(sds((width, hidden), F32), sds((width, hidden), F32), sds((hidden, width), F32)),
        in_specs=[smem(), vmem()] + [anywhere] * len(before),
        out_specs=[anywhere] * 3,
        input_output_aliases={2 + i: i for i in range(len(before))},
        scratch_shapes=[
            pltpu.VMEM((2, HALVES // 2, width, LANES), F32),
            pltpu.VMEM((HALVES // 2, width, LANES), F32),
            pltpu.VMEM((HALVES // 2, LANES, width), F32),
            pltpu.SemaphoreType.DMA((12,)),
        ],
        compiler_params=params(8),
        cost_estimate=pl.CostEstimate(flops=2 * width * hidden, bytes_accessed=9 * width * hidden, transcendentals=0),
        name="unpack",
    )(place, src, *before)


def swap(value, axis, bit):
    return lax.ppermute(value, axis, [(i, i ^ bit) for i in range(lax.axis_size(axis))])


def swap_with_bias(value, bias, axis, bit):
    high = lax.reduce_precision(bias, 8, 7)
    low = lax.reduce_precision(bias - high, 8, 7)
    message = jnp.concatenate([value.reshape(-1, LANES), high.astype(BF16), low.astype(BF16)])
    got, theirs = received(swap(message, axis, bit), value.shape)
    return got, (high + low) + theirs


def received(message, shape):
    end = message.shape[0] - 2 * BIAS_ROWS
    bias = message[end : end + BIAS_ROWS].astype(F32) + message[end + BIAS_ROWS :].astype(F32)
    return message[:end].reshape(shape), bias


def reduce_first(keep, send, bias):
    shape = (HALVES // 2, QUARTERS, -1, LANES)
    got, theirs = received(swap(send, "row", 1), keep.shape)
    return (keep + got.astype(F32)).reshape(shape), bias + theirs


def reduce_among(parts, bias, axis, bits):
    high = lax.reduce_precision(bias, 8, 7)
    low = lax.reduce_precision(bias - high, 8, 7)
    extra = [high.astype(BF16), low.astype(BF16)]
    shape = parts[0].shape
    one, two, three = [
        received(swap(jnp.concatenate([v.astype(BF16).reshape(-1, LANES)] + extra), axis, bit), shape)
        for v, bit in zip(parts[1:], bits)
    ]
    total = (parts[0] + one[0].astype(F32)) + (two[0].astype(F32) + three[0].astype(F32))
    return total, ((high + low) + one[1]) + (two[1] + three[1])


def reduce_far(s, bias):
    bit = HALVES
    while bit < lax.axis_size("row"):
        s = s.astype(BF16)
        got, bias = swap_with_bias(s, bias, "row", bit)
        s = s.astype(F32) + got.astype(F32)
        bit *= 2
    return s.astype(BF16), bias


def gather_among(s, axis, bits):
    return jnp.stack([s] + [swap(s, axis, bit) for bit in bits])


def gather_plane(s):
    a, b = s[:2], s[2:]
    a, b = jnp.stack([a, swap(a, "row", 4)]), jnp.stack([b, swap(b, "row", 2)])
    far_a, far_b = swap(a, "row", 2), swap(b, "row", 4)
    a = jnp.stack([a, far_a], axis=1).reshape((4,) + a.shape[1:])
    b = jnp.concatenate([b, far_b])
    return jnp.concatenate([a, b], axis=1)


def local(x, cols, tw, ws, wn, bias_hidden, wo, bias_out, cot):
    rows, width = x.shape
    hidden = ws.shape[1]
    blocks, tile, depth = tw.shape
    both = ("row", "col")
    count = lax.axis_size(both)
    tile_scale = 0.25 / math.sqrt(depth)
    grad_scale = 1.0 / math.sqrt(rows * count)
    forward = [(i, i + 1) for i in range(count - 1)]
    backward = [(j, i) for i, j in forward]
    place = jnp.stack(
        [
            lax.axis_index(both) * blocks - blocks,
            lax.rem(lax.axis_index("row"), HALVES),
            lax.axis_index("col"),
        ]
    ).astype(jnp.int32)
    sds = jax.ShapeDtypeStruct
    low = lax.ppermute(x, both, forward)
    high = lax.ppermute(x, both, backward)
    adj, x_t, cot_t, wn_t, ws_t, pre, half_act, cot_sum = pl.pallas_call(
        functools.partial(prepare_kernel, tile_scale),
        out_shape=(
            sds((blocks, tile, depth), BF16),
            sds((width, rows), BF16),
            sds((width, rows), BF16),
            sds((hidden, width), BF16),
            sds((hidden, width), BF16),
            sds((rows, hidden), F32),
            sds((rows, hidden), F32),
            sds((1, width), F32),
        ),
        in_specs=[vmem()] * 7,
        out_specs=[vmem()] * 8,
        compiler_params=params(22),
        cost_estimate=pl.CostEstimate(flops=4 * rows * width * hidden, bytes_accessed=9 << 20, transcendentals=0),
        name="prepare",
    )(tw, x, cot, ws, wn, wo, bias_hidden.reshape(1, -1))
    size = HALVES // 2 * 3 * width
    hid, dh, keep, send, bias = pl.pallas_call(
        forward_kernel,
        out_shape=(
            sds((rows, hidden), BF16),
            sds((rows, hidden), BF16),
            sds((size, LANES), F32),
            sds((size + 2 * BIAS_ROWS, LANES), BF16),
            sds((BIAS_ROWS, LANES), F32),
        ),
        in_specs=[smem(), smem()] + [vmem()] * 10,
        out_specs=[vmem()] * 5,
        scratch_shapes=[
            pltpu.VMEM((3 * rows, width), BF16),
            pltpu.VMEM((rows, width), BF16),
            pltpu.VMEM((2 * width + BIAS_ROWS, rows), BF16),
            pltpu.VMEM((BIAS_ROWS, LANES), F32),
        ],
        compiler_params=params(30),
        cost_estimate=pl.CostEstimate(
            flops=2 * rows * width * (4 * hidden + depth), bytes_accessed=14 << 20, transcendentals=rows * hidden
        ),
        name="forward",
    )(place, cols, low, x, high, adj, x_t, cot_t, wn, pre, half_act, cot_sum)
    acc, bias = reduce_first(keep, send, bias)
    acc, dh = lax.optimization_barrier((acc, dh))
    own, to_low, to_high = pl.pallas_call(
        spread_kernel,
        out_shape=(sds((rows, width), F32), sds((rows, width), BF16), sds((rows, width), BF16)),
        in_specs=[smem(), smem()] + [vmem()] * 3,
        out_specs=[vmem()] * 3,
        scratch_shapes=[pltpu.VMEM((3 * rows, width), F32), pltpu.VMEM((rows, width), BF16)],
        compiler_params=params(16),
        cost_estimate=pl.CostEstimate(
            flops=2 * rows * width * (hidden + depth), bytes_accessed=6 << 20, transcendentals=0
        ),
        name="spread",
    )(place, cols, adj, dh, wn_t)
    acc, bias = reduce_among([acc[i] for i in range(4)], bias, "row", (2, 4, 6))
    acc, hid, dh, own = lax.optimization_barrier((acc, hid, dh, own))
    embed, own = pl.pallas_call(
        finish_kernel,
        out_shape=(sds((rows, width), BF16), sds((rows, width), F32)),
        in_specs=[vmem()] * 6,
        out_specs=[vmem()] * 2,
        compiler_params=params(12),
        cost_estimate=pl.CostEstimate(flops=4 * rows * width * hidden, bytes_accessed=8 << 20, transcendentals=0),
        name="finish",
    )(hid, dh, wo, bias_out.reshape(1, -1), ws_t, own)
    part, bias = reduce_among([acc[i] for i in range(4)], bias, "col", (1, 2, 3))
    part, to_low, to_high = lax.optimization_barrier((part, to_low, to_high))
    part, bias = reduce_far(part, bias)
    from_high = lax.ppermute(to_low, both, backward)
    from_low = lax.ppermute(to_high, both, forward)
    part = gather_among(part, "col", (1, 2, 3))
    mine = gather_plane(part)
    mine, from_high, from_low = lax.optimization_barrier((mine, from_high, from_low))
    other = swap(mine, "row", 1)
    grad_features = (own + from_low.astype(F32) + from_high.astype(F32)).astype(BF16)
    grads = unpack(grad_scale, 0, place, mine, width, hidden)
    g_self, g_neigh, g_out = unpack(grad_scale, 1, place, other, width, hidden, grads)
    bias = bias * grad_scale
    top = hidden // LANES
    bias_h, bias_o = bias[:top].reshape(-1), bias[top : top + width // LANES].reshape(-1)
    return embed, grad_features, g_self, g_neigh, bias_h, g_out, bias_o


def solution(mesh):
    share = P(("row", "col"), None)
    in_specs = (share, share, P(("row", "col"), None, None), P(), P(), P(), P(), P(), share)
    out_specs = (share, share, P(), P(), P(), P(), P())
    return jax.shard_map(local, mesh=mesh, in_specs=in_specs, out_specs=out_specs, check_vma=False)
```

time: 125 us -> 99.7 us (0.80)
  the two profiles are of different devices: /device:TPU:0 before, /device:TPU:13 now
where the time goes in v2:
time: 99.7 us; the launch traced here: 99.1 us
  waiting for transfers between devices  44.9 us (45%)
  starting transfers between devices  25.9 us (26%)
  Pallas kernels  15.9 us (16%)
  local copies, waits for them, and re-layouts  9.51 us (10%)
  other arithmetic  1.79 us (2%)
  between operations  1.05 us (1%)
    ppermute x1, waiting for transfers between devices, local(): from_low = lax.ppermute(to_high, both, forward)  15.5 us
    ppermute x15, waiting for transfers between devices, swap(): lax.ppermute(value, axis, [(i, i ^ bit) for i in range(lax.axis_size(axis...  15.5 us
    ppermute x15, starting transfers between devices, swap(): lax.ppermute(value, axis, [(i, i ^ bit) for i in range(lax.axis_size(axis...  14.4 us
    ppermute x1, waiting for transfers between devices, local(): low = lax.ppermute(x, both, forward)  13.9 us
    unnamed x23, local copies, waits for them, and re-layouts  8.26 us
    pallas_call x1, Pallas kernels, local(): pl.pallas_call(forward_kernel, out_shape=(sds((rows, hidden), BF16), sds(...  5.66 us
    ppermute x1, starting transfers between devices, local(): from_high = lax.ppermute(to_low, both, backward)  4.18 us
    pallas_call x2, Pallas kernels, unpack(): pl.pallas_call(functools.partial(unpack_kernel, scale, half), out_shape=(...  3.68 us
  transfers between devices with their start and end apart: 19, of which 11 were waited for; matrix products, arithmetic and copies ran while one was open for 3% of the time, Pallas kernels for 8%

profile of v2, /device:TPU:13, one launch (start us, length us, event | category | flops | bytes accessed | tf_op | source)
XLA Modules:
  0.0 99.1 jit_solution(10496993268750781226)
XLA Ops:
  0.6 2.1 %collective-permute-start.1 = (bf16[1024,256]{1,0:T(8,128)(2,1)}, bf16[1024,256]{1,0:T(8,128)(2,1)S(1)}, u32[]{:S(2)}, u32[]{:S(2)}) collective-permute-start(bf16[1024,256]{1,0:T(8,128)(2,1)} %x.3), channel_id=1, source_target_pairs={{1,0},{2,1},{3,2},{4,3},{5,4},{6,5},{7,6},{8,7},{9,8},{10,9},{11,1... | collective-permute-start | bytes 1572872 | tf_op jit(solution)/shard_map/ppermute | solution.py:271
  2.7 3.2 %collective-permute-start = (bf16[1024,256]{1,0:T(8,128)(2,1)}, bf16[1024,256]{1,0:T(8,128)(2,1)S(1)}, u32[]{:S(2)}, u32[]{:S(2)}) collective-permute-start(bf16[1024,256]{1,0:T(8,128)(2,1)} %x.3), channel_id=1, source_target_pairs={{0,1},{1,2},{2,3},{3,4},{4,5},{5,6},{6,7},{7,8},{8,9},{9,10},{10,1... | collective-permute-start | bytes 1572872 | tf_op jit(solution)/shard_map/ppermute | solution.py:270
  6.7 1.6 %copy-done = s32[16,64,512]{2,1,0:T(8,128)S(1)} copy-done((s32[16,64,512]{2,1,0:T(8,128)S(1)}, s32[16,64,512]{2,1,0:T(8,128)}, u32[]{:S(2)}) %copy-start) | copy-done | bytes 2097176
  14.2 1.5 %prepare.1 = (bf16[16,64,512]{2,1,0:T(8,128)(2,1)S(1)}, bf16[256,1024]{1,0:T(8,128)(2,1)S(1)}, bf16[256,1024]{1,0:T(8,128)(2,1)S(1)}, bf16[1024,256]{1,0:T(8,128...) custom-call(s32[16,64,512]{2,1,0:T(8,128)S(1)} %copy-done, ...), custom_call_target="tpu_custom_call" | custom-call | flops 1073741824 | bytes 9437184 | tf_op jit(solution)/shard_map/prepare/pallas_call | solution.py:272
  15.8 13.9 %collective-permute-done.lo = bf16[1024,256]{1,0:T(8,128)(2,1)S(1)} collective-permute-done((bf16[1024,256]{1,0:T(8,128)(2,1)}, bf16[1024,256]{1,0:T(8,128)(2,1)S(1)}, u32[]{:S(2)}, u32[]{:S(2)}) %collective-permute-start) | collective-permute-done | bytes 524320 | tf_op jit(solution)/shard_map/ppermute | solution.py:270
  29.7 5.7 %forward.1 = (bf16[1024,1024]{1,0:T(8,128)(2,1)S(1)}, bf16[1024,1024]{1,0:T(8,128)(2,1)S(1)}, f32[3072,128]{1,0:T(8,128)S(1)}, bf16[3104,128]{1,0:T(8,128)(2,1)S(1)}, f32[16,128]{1,0:T(8,128)S(1)}) custom-call(s32[3]{0:T(128)S(1)} %pad_add_fusion.place, s32[16,8]{1,0:T(8,128)S(1)} %copy.21.cols, bf16[1024,256]{1,0:T(8,128)(2,1)S(1)} %collective-permute-done.lo, ...), custom_call_target="tpu_custom_call" | custom-call | flops 2415919104 | bytes 14680064 | tf_op jit(solution)/shard_map/forward/pallas_call | solution.py:291
  35.4 1.3 %collective-permute-start.2 = (bf16[3104,128]{1,0:T(8,128)(2,1)S(1)}, bf16[3104,128]{1,0:T(8,128)(2,1)S(1)}, u32[]{:S(2)}, u32[]{:S(2)}) collective-permute-start(bf16[3104,128]{1,0:T(8,128)(2,1)S(1)} %get-tuple-element.50), channel_id=1, source_target_pairs={{0,4},{4,0},{8,12},{12,8},{16,20},{20,16},{24,28},{28,24},{1,5},{5... | collective-permute-start | bytes 2383880 | tf_op jit(solution)/shard_map/ppermute | solution.py:193
  36.7 1.9 %collective-permute-done.2 = bf16[3104,128]{1,0:T(8,128)(2,1)S(1)} collective-permute-done((bf16[3104,128]{1,0:T(8,128)(2,1)S(1)}, bf16[3104,128]{1,0:T(8,128)(2,1)S(1)}, u32[]{:S(2)}, u32[]{:S(2)}) %collective-permute-start.2) | collective-permute-done | bytes 794656 | tf_op jit(solution)/shard_map/ppermute | solution.py:193
  39.0 1.2 %collective-permute-start.3 = (bf16[800,128]{1,0:T(8,128)(2,1)S(1)}, bf16[800,128]{1,0:T(8,128)(2,1)S(1)}, u32[]{:S(2)}, u32[]{:S(2)}) collective-permute-start(bf16[800,128]{1,0:T(8,128)(2,1)S(1)} %get-tuple-element.98), channel_id=1, source_target_pairs={{0,8},{4,12},{8,0},{12,4},{16,24},{20,28},{24,16},{28,20},{1,9},{5... | collective-permute-start | bytes 614408 | tf_op jit(solution)/shard_map/ppermute | solution.py:193
  41.7 3.0 %spread.1 = (f32[1024,256]{1,0:T(8,128)S(1)}, bf16[1024,256]{1,0:T(8,128)(2,1)S(1)}, bf16[1024,256]{1,0:T(8,128)(2,1)S(1)}) custom-call(s32[3]{0:T(128)S(1)} %pad_add_fusion.place, s32[16,8]{1,0:T(8,128)S(1)} %copy.21.cols, bf16[16,64,512]{2,1,0:T(8,128)(2,1)S(1)} %get-tuple-element.43.adj, bf16[1024,1024]{1,0:T(8,128)(2,1)S(1)} %get-tuple-element.59.dh, ...), custom_call_target="tpu_custom_call" | custom-call | flops 805306368 | bytes 6291456 | tf_op jit(solution)/shard_map/spread/pallas_call | solution.py:316
  45.4 5.2 %collective-permute-done.4 = bf16[800,128]{1,0:T(8,128)(2,1)S(1)} collective-permute-done((bf16[800,128]{1,0:T(8,128)(2,1)S(1)}, bf16[800,128]{1,0:T(8,128)(2,1)S(1)}, u32[]{:S(2)}, u32[]{:S(2)}) %collective-permute-start.4) | collective-permute-done | bytes 204832 | tf_op jit(solution)/shard_map/ppermute | solution.py:193
  50.9 2.0 %collective-permute-start.7 = (bf16[224,128]{1,0:T(8,128)(2,1)S(1)}, bf16[224,128]{1,0:T(8,128)(2,1)S(1)}, u32[]{:S(2)}, u32[]{:S(2)}) collective-permute-start(bf16[224,128]{1,0:T(8,128)(2,1)S(1)} %get-tuple-element.96), channel_id=1, source_target_pairs={{0,2},{1,3},{2,0},{3,1},{4,6},{5,7},{6,4},{7,5},{8,10},{9,11},{10,... | collective-permute-start | bytes 172040 | tf_op jit(solution)/shard_map/ppermute | solution.py:193
  55.1 1.5 %collective-permute-done.8 = bf16[224,128]{1,0:T(8,128)(2,1)S(1)} collective-permute-done((bf16[224,128]{1,0:T(8,128)(2,1)S(1)}, bf16[224,128]{1,0:T(8,128)(2,1)S(1)}, u32[]{:S(2)}, u32[]{:S(2)}) %collective-permute-start.8) | collective-permute-done | bytes 57376 | tf_op jit(solution)/shard_map/ppermute | solution.py:193
  56.6 2.5 %collective-permute-start.9 = (bf16[192,128]{1,0:T(8,128)(2,1)S(1)}, bf16[192,128]{1,0:T(8,128)(2,1)S(1)}, u32[]{:S(2)}, u32[]{:S(2)}) collective-permute-start(bf16[192,128]{1,0:T(8,128)(2,1)S(1)} %fusion.1), channel_id=1, source_target_pairs={{0,1},{1,0},{2,3},{3,2},{4,5},{5,4},{6,7},{7,6},{8,9},{9,8},{10,11... | collective-permute-start | bytes 147464 | tf_op jit(solution)/shard_map/ppermute | solution.py:193
  60.4 4.2 %collective-permute-start.16 = (bf16[1024,256]{1,0:T(8,128)(2,1)S(1)}, bf16[1024,256]{1,0:T(8,128)(2,1)S(1)}, u32[]{:S(2)}, u32[]{:S(2)}) collective-permute-start(bf16[1024,256]{1,0:T(8,128)(2,1)S(1)} %get-tuple-element.68), channel_id=1, source_target_pairs={{1,0},{2,1},{3,2},{4,3},{5,4},{6,5},{7,6},{8,7},{9,8},{10,9},{11,1... | collective-permute-start | bytes 1572872 | tf_op jit(solution)/shard_map/ppermute | solution.py:342
  64.6 2.1 %collective-permute-start.17 = (bf16[1024,256]{1,0:T(8,128)(2,1)S(1)}, bf16[1024,256]{1,0:T(8,128)(2,1)S(1)}, u32[]{:S(2)}, u32[]{:S(2)}) collective-permute-start(bf16[1024,256]{1,0:T(8,128)(2,1)S(1)} %get-tuple-element.69), channel_id=1, source_target_pairs={{0,1},{1,2},{2,3},{3,4},{4,5},{5,6},{6,7},{7,8},{8,9},{9,10},{10,1... | collective-permute-start | bytes 1572872 | tf_op jit(solution)/shard_map/ppermute | solution.py:343
  67.1 1.3 %collective-permute-start.14 = (bf16[2,192,128]{2,1,0:T(8,128)(2,1)S(1)}, bf16[2,192,128]{2,1,0:T(8,128)(2,1)S(1)}, u32[]{:S(2)}, u32[]{:S(2)}) collective-permute-start(bf16[2,192,128]{2,1,0:T(8,128)(2,1)S(1)} %get-tuple-element.94), channel_id=1, source_target_pairs={{0,8},{4,12},{8,0},{12,4},{16,24},{20,28},{24,16},{28,20},{1,9},{5... | collective-permute-start | bytes 294920 | tf_op jit(solution)/shard_map/ppermute | solution.py:193
  68.4 2.2 %collective-permute-done.10 = bf16[2,192,128]{2,1,0:T(8,128)(2,1)S(1)} collective-permute-done((bf16[2,192,128]{2,1,0:T(8,128)(2,1)S(1)}, bf16[2,192,128]{2,1,0:T(8,128)(2,1)S(1)}, u32[]{:S(2)}, u32[]{:S(2)}) %collective-permute-start.10) | collective-permute-done | bytes 98336 | tf_op jit(solution)/shard_map/ppermute | solution.py:193
  71.0 1.3 %collective-permute-start.15 = (bf16[2,2,192,128]{3,2,1,0:T(8,128)(2,1)S(1)}, bf16[2,2,192,128]{3,2,1,0:T(8,128)(2,1)S(1)}, u32[]{:S(2)}, u32[]{:S(2)}) collective-permute-start(bf16[2,2,192,128]{3,2,1,0:T(8,128)(2,1)S(1)} %pad_maximum_fusion.8), channel_id=1, source_target_pairs={{0,16},{4,20},{8,24},{12,28},{16,0},{20,4},{24,8},{28,12},{1,17},{... | collective-permute-start | bytes 589832 | tf_op jit(solution)/shard_map/ppermute | solution.py:193
  72.2 2.1 %finish.1 = (bf16[1024,256]{1,0:T(8,128)(2,1)}, f32[1024,256]{1,0:T(8,128)S(1)}) custom-call(bf16[1024,1024]{1,0:T(8,128)(2,1)S(1)} %get-tuple-element.58.hid, bf16[1024,1024]{1,0:T(8,128)(2,1)S(1)} %get-tuple-element.59.dh, bf16[1024,256]{1,0:T(8,128)(2,1)S(1)} %copy-done.6, f32[1,256]{1,0:T(1,128)S(1)} %bitcast.43, ...), custom_call_target="tpu_custom_call" | custom-call | flops 1073741824 | bytes 8388608 | tf_op jit(solution)/shard_map/finish/pallas_call | solution.py:330
  74.3 1.4 %collective-permute-done.11 = bf16[2,2,192,128]{3,2,1,0:T(8,128)(2,1)S(1)} collective-permute-done((bf16[2,2,192,128]{3,2,1,0:T(8,128)(2,1)S(1)}, bf16[2,2,192,128]{3,2,1,0:T(8,128)(2,1)S(1)}, u32[]{:S(2)}, u32[]{:S(2)}) %collective-permute-start.11) | collective-permute-done | bytes 196640 | tf_op jit(solution)/shard_map/ppermute | solution.py:193
  77.0 15.5 %collective-permute-done.17 = bf16[1024,256]{1,0:T(8,128)(2,1)S(1)} collective-permute-done((bf16[1024,256]{1,0:T(8,128)(2,1)S(1)}, bf16[1024,256]{1,0:T(8,128)(2,1)S(1)}, u32[]{:S(2)}, u32[]{:S(2)}) %collective-permute-start.17) | collective-permute-done | bytes 524320 | tf_op jit(solution)/shard_map/ppermute | solution.py:343
  94.3 1.8 %unpack.2 = (f32[256,1024]{1,0:T(8,128)}, f32[256,1024]{1,0:T(8,128)}, f32[1024,256]{1,0:T(8,128)}) custom-call(s32[3]{0:T(128)S(1)} %pad_add_fusion.place, bf16[4,4,192,128]{3,2,1,0:T(8,128)(2,1)S(1)} %maximum_maximum_fusion.src), custom_call_target="tpu_custom_call" | custom-call | flops 524288 | bytes 2359296 | tf_op jit(solution)/shard_map/unpack/pallas_call | solution.py:174
  97.1 1.8 %unpack.3 = (f32[256,1024]{1,0:T(8,128)}, f32[256,1024]{1,0:T(8,128)}, f32[1024,256]{1,0:T(8,128)}) custom-call(s32[3]{0:T(128)S(1)} %pad_add_fusion.place, bf16[4,4,192,128]{3,2,1,0:T(8,128)(2,1)S(1)} %collective-permute-done.18.src, f32[256,1024]{1,0:T(8,128)} %get-tuple-element.73.refs_0_, ...), custom_call_target="tpu_custom_call", output_to_operand_aliasing={{0}: (2, {}), {1}: (3, {}), {2}: (4, {})} | custom-call | flops 524288 | bytes 2359296 | tf_op jit(solution)/shard_map/unpack/pallas_call | solution.py:174
  (69 shorter events, 17.8 us)
Async XLA Ops:
  0.6 15.1 %collective-permute-start.1 = (bf16[1024,256]{1,0:T(8,128)(2,1)}, bf16[1024,256]{1,0:T(8,128)(2,1)S(1)}, u32[]{:S(2)}, u32[]{:S(2)}) collective-permute-start(bf16[1024,256]{1,0:T(8,128)(2,1)} %x.3), channel_id=1, source_target_pairs={{1,0},{2,1},{3,2},{4,3},{5,4},{6,5},{7,6},{8,7},{9,8},{10,9},{11,1... | collective-permute-start | bytes 1572872 | tf_op jit(solution)/shard_map/ppermute | solution.py:271
  2.7 27.0 %collective-permute-start = (bf16[1024,256]{1,0:T(8,128)(2,1)}, bf16[1024,256]{1,0:T(8,128)(2,1)S(1)}, u32[]{:S(2)}, u32[]{:S(2)}) collective-permute-start(bf16[1024,256]{1,0:T(8,128)(2,1)} %x.3), channel_id=1, source_target_pairs={{0,1},{1,2},{2,3},{3,4},{4,5},{5,6},{6,7},{7,8},{8,9},{9,10},{10,1... | collective-permute-start | bytes 1572872 | tf_op jit(solution)/shard_map/ppermute | solution.py:270
  6.7 1.6 %copy-start = (s32[16,64,512]{2,1,0:T(8,128)S(1)}, s32[16,64,512]{2,1,0:T(8,128)}, u32[]{:S(2)}) copy-start(s32[16,64,512]{2,1,0:T(8,128)} %tw.1) | copy-start | bytes 6291460
  14.2 15.5 %copy-start.2 = (bf16[1024,256]{1,0:T(8,128)(2,1)S(1)}, bf16[1024,256]{1,0:T(8,128)(2,1)}, u32[]{:S(2)}) copy-start(bf16[1024,256]{1,0:T(8,128)(2,1)} %x.3) | copy-start | bytes 1572868
  14.2 15.5 %copy-start.4 = (bf16[256,1024]{1,0:T(8,128)(2,1)S(1)}, bf16[256,1024]{1,0:T(8,128)(2,1)}, u32[]{:S(2)}) copy-start(bf16[256,1024]{1,0:T(8,128)(2,1)} %wn.3) | copy-start | bytes 1572868
  35.4 3.3 %collective-permute-start.2 = (bf16[3104,128]{1,0:T(8,128)(2,1)S(1)}, bf16[3104,128]{1,0:T(8,128)(2,1)S(1)}, u32[]{:S(2)}, u32[]{:S(2)}) collective-permute-start(bf16[3104,128]{1,0:T(8,128)(2,1)S(1)} %get-tuple-element.50), channel_id=1, source_target_pairs={{0,4},{4,0},{8,12},{12,8},{16,20},{20,16},{24,28},{28,24},{1,5},{5... | collective-permute-start | bytes 2383880 | tf_op jit(solution)/shard_map/ppermute | solution.py:193
  39.0 6.4 %collective-permute-start.3 = (bf16[800,128]{1,0:T(8,128)(2,1)S(1)}, bf16[800,128]{1,0:T(8,128)(2,1)S(1)}, u32[]{:S(2)}, u32[]{:S(2)}) collective-permute-start(bf16[800,128]{1,0:T(8,128)(2,1)S(1)} %get-tuple-element.98), channel_id=1, source_target_pairs={{0,8},{4,12},{8,0},{12,4},{16,24},{20,28},{24,16},{28,20},{1,9},{5... | collective-permute-start | bytes 614408 | tf_op jit(solution)/shard_map/ppermute | solution.py:193
  40.2 10.4 %collective-permute-start.4 = (bf16[800,128]{1,0:T(8,128)(2,1)S(1)}, bf16[800,128]{1,0:T(8,128)(2,1)S(1)}, u32[]{:S(2)}, u32[]{:S(2)}) collective-permute-start(bf16[800,128]{1,0:T(8,128)(2,1)S(1)} %get-tuple-element.99), channel_id=1, source_target_pairs={{0,16},{4,20},{8,24},{12,28},{16,0},{20,4},{24,8},{28,12},{1,17},{... | collective-permute-start | bytes 614408 | tf_op jit(solution)/shard_map/ppermute | solution.py:193
  40.5 10.1 %collective-permute-start.5 = (bf16[800,128]{1,0:T(8,128)(2,1)S(1)}, bf16[800,128]{1,0:T(8,128)(2,1)S(1)}, u32[]{:S(2)}, u32[]{:S(2)}) collective-permute-start(bf16[800,128]{1,0:T(8,128)(2,1)S(1)} %get-tuple-element.100), channel_id=1, source_target_pairs={{0,24},{4,28},{8,16},{12,20},{16,8},{20,12},{24,0},{28,4},{1,25},{... | collective-permute-start | bytes 614408 | tf_op jit(solution)/shard_map/ppermute | solution.py:193
  50.7 21.5 %copy-start.6 = (bf16[1024,256]{1,0:T(8,128)(2,1)S(1)}, bf16[1024,256]{1,0:T(8,128)(2,1)}, u32[]{:S(2)}) copy-start(bf16[1024,256]{1,0:T(8,128)(2,1)} %wo.3) | copy-start | bytes 1572868
  50.7 21.5 %copy-start.10 = (f32[256]{0:T(256)S(1)}, f32[256]{0:T(256)}, u32[]{:S(2)}) copy-start(f32[256]{0:T(256)} %param.16) | copy-start | bytes 3076
  50.8 3.1 %collective-permute-start.6 = (bf16[224,128]{1,0:T(8,128)(2,1)S(1)}, bf16[224,128]{1,0:T(8,128)(2,1)S(1)}, u32[]{:S(2)}, u32[]{:S(2)}) collective-permute-start(bf16[224,128]{1,0:T(8,128)(2,1)S(1)} %get-tuple-element.95), channel_id=1, source_target_pairs={{0,1},{1,0},{2,3},{3,2},{4,5},{5,4},{6,7},{7,6},{8,9},{9,8},{10,11... | collective-permute-start | bytes 172040 | tf_op jit(solution)/shard_map/ppermute | solution.py:193
  50.9 4.2 %collective-permute-start.7 = (bf16[224,128]{1,0:T(8,128)(2,1)S(1)}, bf16[224,128]{1,0:T(8,128)(2,1)S(1)}, u32[]{:S(2)}, u32[]{:S(2)}) collective-permute-start(bf16[224,128]{1,0:T(8,128)(2,1)S(1)} %get-tuple-element.96), channel_id=1, source_target_pairs={{0,2},{1,3},{2,0},{3,1},{4,6},{5,7},{6,4},{7,5},{8,10},{9,11},{10,... | collective-permute-start | bytes 172040 | tf_op jit(solution)/shard_map/ppermute | solution.py:193
  52.9 3.7 %collective-permute-start.8 = (bf16[224,128]{1,0:T(8,128)(2,1)S(1)}, bf16[224,128]{1,0:T(8,128)(2,1)S(1)}, u32[]{:S(2)}, u32[]{:S(2)}) collective-permute-start(bf16[224,128]{1,0:T(8,128)(2,1)S(1)} %get-tuple-element.97), channel_id=1, source_target_pairs={{0,3},{1,2},{2,1},{3,0},{4,7},{5,6},{6,5},{7,4},{8,11},{9,10},{10,... | collective-permute-start | bytes 172040 | tf_op jit(solution)/shard_map/ppermute | solution.py:193
  56.6 10.1 %collective-permute-start.9 = (bf16[192,128]{1,0:T(8,128)(2,1)S(1)}, bf16[192,128]{1,0:T(8,128)(2,1)S(1)}, u32[]{:S(2)}, u32[]{:S(2)}) collective-permute-start(bf16[192,128]{1,0:T(8,128)(2,1)S(1)} %fusion.1), channel_id=1, source_target_pairs={{0,1},{1,0},{2,3},{3,2},{4,5},{5,4},{6,7},{7,6},{8,9},{9,8},{10,11... | collective-permute-start | bytes 147464 | tf_op jit(solution)/shard_map/ppermute | solution.py:193
  59.1 8.0 %collective-permute-start.12 = (bf16[192,128]{1,0:T(8,128)(2,1)S(1)}, bf16[192,128]{1,0:T(8,128)(2,1)S(1)}, u32[]{:S(2)}, u32[]{:S(2)}) collective-permute-start(bf16[192,128]{1,0:T(8,128)(2,1)S(1)} %fusion.1), channel_id=1, source_target_pairs={{0,2},{1,3},{2,0},{3,1},{4,6},{5,7},{6,4},{7,5},{8,10},{9,11},{10,... | collective-permute-start | bytes 147464 | tf_op jit(solution)/shard_map/ppermute | solution.py:193
  59.3 7.8 %collective-permute-start.13 = (bf16[192,128]{1,0:T(8,128)(2,1)S(1)}, bf16[192,128]{1,0:T(8,128)(2,1)S(1)}, u32[]{:S(2)}, u32[]{:S(2)}) collective-permute-start(bf16[192,128]{1,0:T(8,128)(2,1)S(1)} %fusion.1), channel_id=1, source_target_pairs={{0,3},{1,2},{2,1},{3,0},{4,7},{5,6},{6,5},{7,4},{8,11},{9,10},{10,... | collective-permute-start | bytes 147464 | tf_op jit(solution)/shard_map/ppermute | solution.py:193
  60.4 16.6 %collective-permute-start.16 = (bf16[1024,256]{1,0:T(8,128)(2,1)S(1)}, bf16[1024,256]{1,0:T(8,128)(2,1)S(1)}, u32[]{:S(2)}, u32[]{:S(2)}) collective-permute-start(bf16[1024,256]{1,0:T(8,128)(2,1)S(1)} %get-tuple-element.68), channel_id=1, source_target_pairs={{1,0},{2,1},{3,2},{4,3},{5,4},{6,5},{7,6},{8,7},{9,8},{10,9},{11,1... | collective-permute-start | bytes 1572872 | tf_op jit(solution)/shard_map/ppermute | solution.py:342
  64.6 27.9 %collective-permute-start.17 = (bf16[1024,256]{1,0:T(8,128)(2,1)S(1)}, bf16[1024,256]{1,0:T(8,128)(2,1)S(1)}, u32[]{:S(2)}, u32[]{:S(2)}) collective-permute-start(bf16[1024,256]{1,0:T(8,128)(2,1)S(1)} %get-tuple-element.69), channel_id=1, source_target_pairs={{0,1},{1,2},{2,3},{3,4},{4,5},{5,6},{6,7},{7,8},{8,9},{9,10},{10,1... | collective-permute-start | bytes 1572872 | tf_op jit(solution)/shard_map/ppermute | solution.py:343
  66.7 3.8 %collective-permute-start.10 = (bf16[2,192,128]{2,1,0:T(8,128)(2,1)S(1)}, bf16[2,192,128]{2,1,0:T(8,128)(2,1)S(1)}, u32[]{:S(2)}, u32[]{:S(2)}) collective-permute-start(bf16[2,192,128]{2,1,0:T(8,128)(2,1)S(1)} %get-tuple-element.92), channel_id=1, source_target_pairs={{0,16},{4,20},{8,24},{12,28},{16,0},{20,4},{24,8},{28,12},{1,17},{... | collective-permute-start | bytes 294920 | tf_op jit(solution)/shard_map/ppermute | solution.py:193
  67.1 3.8 %collective-permute-start.14 = (bf16[2,192,128]{2,1,0:T(8,128)(2,1)S(1)}, bf16[2,192,128]{2,1,0:T(8,128)(2,1)S(1)}, u32[]{:S(2)}, u32[]{:S(2)}) collective-permute-start(bf16[2,192,128]{2,1,0:T(8,128)(2,1)S(1)} %get-tuple-element.94), channel_id=1, source_target_pairs={{0,8},{4,12},{8,0},{12,4},{16,24},{20,28},{24,16},{28,20},{1,9},{5... | collective-permute-start | bytes 294920 | tf_op jit(solution)/shard_map/ppermute | solution.py:193
  70.6 5.2 %collective-permute-start.11 = (bf16[2,2,192,128]{3,2,1,0:T(8,128)(2,1)S(1)}, bf16[2,2,192,128]{3,2,1,0:T(8,128)(2,1)S(1)}, u32[]{:S(2)}, u32[]{:S(2)}) collective-permute-start(bf16[2,2,192,128]{3,2,1,0:T(8,128)(2,1)S(1)} %get-tuple-element.87), channel_id=1, source_target_pairs={{0,8},{4,12},{8,0},{12,4},{16,24},{20,28},{24,16},{28,20},{1,9},{5... | collective-permute-start | bytes 589832 | tf_op jit(solution)/shard_map/ppermute | solution.py:193
  71.0 5.9 %collective-permute-start.15 = (bf16[2,2,192,128]{3,2,1,0:T(8,128)(2,1)S(1)}, bf16[2,2,192,128]{3,2,1,0:T(8,128)(2,1)S(1)}, u32[]{:S(2)}, u32[]{:S(2)}) collective-permute-start(bf16[2,2,192,128]{3,2,1,0:T(8,128)(2,1)S(1)} %pad_maximum_fusion.8), channel_id=1, source_target_pairs={{0,16},{4,20},{8,24},{12,28},{16,0},{20,4},{24,8},{28,12},{1,17},{... | collective-permute-start | bytes 589832 | tf_op jit(solution)/shard_map/ppermute | solution.py:193
  92.5 4.6 %collective-permute-start.18 = (bf16[4,4,192,128]{3,2,1,0:T(8,128)(2,1)S(1)}, bf16[4,4,192,128]{3,2,1,0:T(8,128)(2,1)S(1)}, u32[]{:S(2)}, u32[]{:S(2)}) collective-permute-start(bf16[4,4,192,128]{3,2,1,0:T(8,128)(2,1)S(1)} %maximum_maximum_fusion.src), channel_id=1, source_target_pairs={{0,4},{4,0},{8,12},{12,8},{16,20},{20,16},{24,28},{28,24},{1,5},{5... | collective-permute-start | bytes 2359304 | tf_op jit(solution)/shard_map/ppermute | solution.py:193
  (6 other events, 5.9 us)

commit v3 on v2

--- a/solution.py
+++ b/solution.py
@@ -144,8 +144,9 @@
         embed[sl] = (dot(hid[sl], wo[...]) + bias_out[...]).astype(BF16)
 
 
-def unpack_kernel(scale, half, place, src, *refs):
-    g_self, g_neigh, g_out, blocks, turned, flipped, sems = refs[-7:]
+def place_grads(scale, half, place, src, outs, scratch):
+    g_self, g_neigh, g_out = outs
+    blocks, turned, flipped, sems = scratch
     width = g_self.shape[0]
     piece = width // QUARTERS
     me, z = place[1], place[2]
@@ -164,29 +165,34 @@
         copies.append(pltpu.make_async_copy(flipped.at[j], g_out.at[at], sems.at[8 + j]))
         for copy in copies[-3:]:
             copy.start()
+    return copies
+
+
+def first_unpack_kernel(
+    scale, place, src, own, from_low, from_high, bias,
+    g_self, g_neigh, g_out, features, bias_hidden, bias_out, *scratch
+):
+    copies = place_grads(scale, 0, place, src, (g_self, g_neigh, g_out), scratch)
+    features[...] = (own[...] + from_low[...].astype(F32) + from_high[...].astype(F32)).astype(BF16)
+    top, count = bias_hidden.shape[0], bias_out.shape[0]
+    bias_hidden[...] = bias[:top] * scale
+    bias_out[...] = bias[top : top + count] * scale
     for copy in copies:
         copy.wait()
 
 
-def unpack(scale, half, place, src, width, hidden, before=()):
-    sds = jax.ShapeDtypeStruct
-    anywhere = pl.BlockSpec(memory_space=pl.ANY)
-    return pl.pallas_call(
-        functools.partial(unpack_kernel, scale, half),
-        out_shape=(sds((width, hidden), F32), sds((width, hidden), F32), sds((hidden, width), F32)),
-        in_specs=[smem(), vmem()] + [anywhere] * len(before),
-        out_specs=[anywhere] * 3,
-        input_output_aliases={2 + i: i for i in range(len(before))},
-        scratch_shapes=[
-            pltpu.VMEM((2, HALVES // 2, width, LANES), F32),
-            pltpu.VMEM((HALVES // 2, width, LANES), F32),
-            pltpu.VMEM((HALVES // 2, LANES, width), F32),
-            pltpu.SemaphoreType.DMA((12,)),
-        ],
-        compiler_params=params(8),
-        cost_estimate=pl.CostEstimate(flops=2 * width * hidden, bytes_accessed=9 * width * hidden, transcendentals=0),
-        name="unpack",
-    )(place, src, *before)
+def second_unpack_kernel(scale, place, src, _0, _1, _2, g_self, g_neigh, g_out, *scratch):
+    for copy in place_grads(scale, 1, place, src, (g_self, g_neigh, g_out), scratch):
+        copy.wait()
+
+
+def unpack_scratch(width):
+    return [
+        pltpu.VMEM((2, HALVES // 2, width, LANES), F32),
+        pltpu.VMEM((HALVES // 2, width, LANES), F32),
+        pltpu.VMEM((HALVES // 2, LANES, width), F32),
+        pltpu.SemaphoreType.DMA((12,)),
+    ]
 
 
 def swap(value, axis, bit):
@@ -240,9 +246,12 @@
     return jnp.stack([s] + [swap(s, axis, bit) for bit in bits])
 
 
-def gather_plane(s):
+def gather_near(s):
     a, b = s[:2], s[2:]
-    a, b = jnp.stack([a, swap(a, "row", 4)]), jnp.stack([b, swap(b, "row", 2)])
+    return jnp.stack([a, swap(a, "row", 4)]), jnp.stack([b, swap(b, "row", 2)])
+
+
+def gather_across(a, b):
     far_a, far_b = swap(a, "row", 2), swap(b, "row", 4)
     a = jnp.stack([a, far_a], axis=1).reshape((4,) + a.shape[1:])
     b = jnp.concatenate([b, far_b])
@@ -312,7 +321,7 @@
         name="forward",
     )(place, cols, low, x, high, adj, x_t, cot_t, wn, pre, half_act, cot_sum)
     acc, bias = reduce_first(keep, send, bias)
-    acc, dh = lax.optimization_barrier((acc, dh))
+    acc, dh, hid = lax.optimization_barrier((acc, dh, hid))
     own, to_low, to_high = pl.pallas_call(
         spread_kernel,
         out_shape=(sds((rows, width), F32), sds((rows, width), BF16), sds((rows, width), BF16)),
@@ -326,7 +335,6 @@
         name="spread",
     )(place, cols, adj, dh, wn_t)
     acc, bias = reduce_among([acc[i] for i in range(4)], bias, "row", (2, 4, 6))
-    acc, hid, dh, own = lax.optimization_barrier((acc, hid, dh, own))
     embed, own = pl.pallas_call(
         finish_kernel,
         out_shape=(sds((rows, width), BF16), sds((rows, width), F32)),
@@ -336,22 +344,46 @@
         cost_estimate=pl.CostEstimate(flops=4 * rows * width * hidden, bytes_accessed=8 << 20, transcendentals=0),
         name="finish",
     )(hid, dh, wo, bias_out.reshape(1, -1), ws_t, own)
+    cut = 8 * rows // 16
+    first = lax.ppermute(to_high[:cut], both, forward)
+    acc, first, embed, own = lax.optimization_barrier((acc, first, embed, own))
     part, bias = reduce_among([acc[i] for i in range(4)], bias, "col", (1, 2, 3))
     part, to_low, to_high = lax.optimization_barrier((part, to_low, to_high))
     part, bias = reduce_far(part, bias)
     from_high = lax.ppermute(to_low, both, backward)
-    from_low = lax.ppermute(to_high, both, forward)
+    last = lax.ppermute(to_high[cut:], both, forward)
     part = gather_among(part, "col", (1, 2, 3))
-    mine = gather_plane(part)
-    mine, from_high, from_low = lax.optimization_barrier((mine, from_high, from_low))
+    a, b = gather_near(part)
+    a, b, last = lax.optimization_barrier((a, b, last))
+    mine = gather_across(a, b)
+    mine, from_high = lax.optimization_barrier((mine, from_high))
+    from_low = jnp.concatenate([first, last])
     other = swap(mine, "row", 1)
-    grad_features = (own + from_low.astype(F32) + from_high.astype(F32)).astype(BF16)
-    grads = unpack(grad_scale, 0, place, mine, width, hidden)
-    g_self, g_neigh, g_out = unpack(grad_scale, 1, place, other, width, hidden, grads)
-    bias = bias * grad_scale
-    top = hidden // LANES
-    bias_h, bias_o = bias[:top].reshape(-1), bias[top : top + width // LANES].reshape(-1)
-    return embed, grad_features, g_self, g_neigh, bias_h, g_out, bias_o
+    anywhere = pl.BlockSpec(memory_space=pl.ANY)
+    grads = (sds((width, hidden), F32), sds((width, hidden), F32), sds((hidden, width), F32))
+    *grads_half, grad_features, bias_h, bias_o = pl.pallas_call(
+        functools.partial(first_unpack_kernel, grad_scale),
+        out_shape=grads
+        + (sds((rows, width), BF16), sds((hidden // LANES, LANES), F32), sds((width // LANES, LANES), F32)),
+        in_specs=[smem()] + [vmem()] * 5,
+        out_specs=[anywhere] * 3 + [vmem()] * 3,
+        scratch_shapes=unpack_scratch(width),
+        compiler_params=params(10),
+        cost_estimate=pl.CostEstimate(flops=4 * width * hidden, bytes_accessed=12 * width * hidden, transcendentals=0),
+        name="first_unpack",
+    )(place, mine, own, from_low, from_high, bias)
+    g_self, g_neigh, g_out = pl.pallas_call(
+        functools.partial(second_unpack_kernel, grad_scale),
+        out_shape=grads,
+        in_specs=[smem(), vmem()] + [anywhere] * 3,
+        out_specs=[anywhere] * 3,
+        input_output_aliases={2: 0, 3: 1, 4: 2},
+        scratch_shapes=unpack_scratch(width),
+        compiler_params=params(8),
+        cost_estimate=pl.CostEstimate(flops=2 * width * hidden, bytes_accessed=9 * width * hidden, transcendentals=0),
+        name="second_unpack",
+    )(place, other, *grads_half)
+    return embed, grad_features, g_self, g_neigh, bias_h.reshape(-1), g_out, bias_o.reshape(-1)
 
 
 def solution(mesh):

time: 99.7 us -> 96.4 us (0.967)
  the two profiles are of different devices: /device:TPU:13 before, /device:TPU:0 now
where the time goes in v3:
time: 96.4 us; the launch traced here: 95.8 us
  starting transfers between devices  47.4 us (49%)
  waiting for transfers between devices  21.6 us (22%)
  Pallas kernels  16.7 us (17%)
  local copies, waits for them, and re-layouts  8.39 us (9%)
    ppermute x15, starting transfers between devices, swap(): lax.ppermute(value, axis, [(i, i ^ bit) for i in range(lax.axis_size(axis...  31.4 us
    ppermute x15, waiting for transfers between devices, swap(): lax.ppermute(value, axis, [(i, i ^ bit) for i in range(lax.axis_size(axis...  18.9 us
    unnamed x23, local copies, waits for them, and re-layouts  8.26 us
    pallas_call x1, Pallas kernels, local(): pl.pallas_call(forward_kernel, out_shape=(sds((rows, hidden), BF16), sds(...  5.66 us
    ppermute x1, starting transfers between devices, local(): low = lax.ppermute(x, both, forward)  5.59 us
    ppermute x1, starting transfers between devices, local(): first = lax.ppermute(to_high[:cut], both, forward)  4.3 us
    ppermute x1, starting transfers between devices, local(): last = lax.ppermute(to_high[cut:], both, forward)  3.46 us
    pallas_call x1, Pallas kernels, local(): pl.pallas_call(spread_kernel, out_shape=(sds((rows, width), F32), sds((ro...  3.04 us
  transfers between devices with their start and end apart: 20, of which 8 were waited for; matrix products, arithmetic and copies ran while one was open for 1% of the time, Pallas kernels for 10%

profile of v3, /device:TPU:0, one launch (start us, length us, event | category | flops | bytes accessed | tf_op | source)
XLA Modules:
  0.0 95.8 jit_solution(10387347199593589182)
XLA Ops:
  1.9 5.6 %collective-permute-start = (bf16[1024,256]{1,0:T(8,128)(2,1)}, bf16[1024,256]{1,0:T(8,128)(2,1)S(1)}, u32[]{:S(2)}, u32[]{:S(2)}) collective-permute-start(bf16[1024,256]{1,0:T(8,128)(2,1)} %x.3), channel_id=1, source_target_pairs={{0,1},{1,2},{2,3},{3,4},{4,5},{5,6},{6,7},{7,8},{8,9},{9,10},{10,1... | collective-permute-start | bytes 1572872 | tf_op jit(solution)/shard_map/ppermute | solution.py:279
  8.3 1.6 %copy-done = s32[16,64,512]{2,1,0:T(8,128)S(1)} copy-done((s32[16,64,512]{2,1,0:T(8,128)S(1)}, s32[16,64,512]{2,1,0:T(8,128)}, u32[]{:S(2)}) %copy-start) | copy-done | bytes 2097176
  15.8 1.5 %prepare.1 = (bf16[16,64,512]{2,1,0:T(8,128)(2,1)S(1)}, bf16[256,1024]{1,0:T(8,128)(2,1)S(1)}, bf16[256,1024]{1,0:T(8,128)(2,1)S(1)}, bf16[1024,256]{1,0:T(8,128...) custom-call(s32[16,64,512]{2,1,0:T(8,128)S(1)} %copy-done, ...), custom_call_target="tpu_custom_call" | custom-call | flops 1073741824 | bytes 9437184 | tf_op jit(solution)/shard_map/prepare/pallas_call | solution.py:281
  17.7 2.3 %collective-permute-done.lo = bf16[1024,256]{1,0:T(8,128)(2,1)S(1)} collective-permute-done((bf16[1024,256]{1,0:T(8,128)(2,1)}, bf16[1024,256]{1,0:T(8,128)(2,1)S(1)}, u32[]{:S(2)}, u32[]{:S(2)}) %collective-permute-start) | collective-permute-done | bytes 524320 | tf_op jit(solution)/shard_map/ppermute | solution.py:279
  20.0 5.7 %forward.1 = (bf16[1024,1024]{1,0:T(8,128)(2,1)S(1)}, bf16[1024,1024]{1,0:T(8,128)(2,1)S(1)}, f32[3072,128]{1,0:T(8,128)S(1)}, bf16[3104,128]{1,0:T(8,128)(2,1)S(1)}, f32[16,128]{1,0:T(8,128)S(1)}) custom-call(s32[3]{0:T(128)S(1)} %pad_add_fusion.place, s32[16,8]{1,0:T(8,128)S(1)} %copy.21.cols, bf16[1024,256]{1,0:T(8,128)(2,1)S(1)} %collective-permute-done.lo, ...), custom_call_target="tpu_custom_call" | custom-call | flops 2415919104 | bytes 14680064 | tf_op jit(solution)/shard_map/forward/pallas_call | solution.py:300
  25.7 11.0 %collective-permute-start.2 = (bf16[3104,128]{1,0:T(8,128)(2,1)S(1)}, bf16[3104,128]{1,0:T(8,128)(2,1)S(1)}, u32[]{:S(2)}, u32[]{:S(2)}) collective-permute-start(bf16[3104,128]{1,0:T(8,128)(2,1)S(1)} %get-tuple-element.56), channel_id=1, source_target_pairs={{0,4},{4,0},{8,12},{12,8},{16,20},{20,16},{24,28},{28,24},{1,5},{5... | collective-permute-start | bytes 2383880 | tf_op jit(solution)/shard_map/ppermute | solution.py:199
  36.7 1.9 %collective-permute-done.2 = bf16[3104,128]{1,0:T(8,128)(2,1)S(1)} collective-permute-done((bf16[3104,128]{1,0:T(8,128)(2,1)S(1)}, bf16[3104,128]{1,0:T(8,128)(2,1)S(1)}, u32[]{:S(2)}, u32[]{:S(2)}) %collective-permute-start.2) | collective-permute-done | bytes 794656 | tf_op jit(solution)/shard_map/ppermute | solution.py:199
  39.0 1.9 %collective-permute-start.4 = (bf16[800,128]{1,0:T(8,128)(2,1)S(1)}, bf16[800,128]{1,0:T(8,128)(2,1)S(1)}, u32[]{:S(2)}, u32[]{:S(2)}) collective-permute-start(bf16[800,128]{1,0:T(8,128)(2,1)S(1)} %get-tuple-element.109), channel_id=1, source_target_pairs={{0,16},{4,20},{8,24},{12,28},{16,0},{20,4},{24,8},{28,12},{1,17},{... | collective-permute-start | bytes 614408 | tf_op jit(solution)/shard_map/ppermute | solution.py:199
  40.9 1.4 %collective-permute-start.5 = (bf16[800,128]{1,0:T(8,128)(2,1)S(1)}, bf16[800,128]{1,0:T(8,128)(2,1)S(1)}, u32[]{:S(2)}, u32[]{:S(2)}) collective-permute-start(bf16[800,128]{1,0:T(8,128)(2,1)S(1)} %get-tuple-element.110), channel_id=1, source_target_pairs={{0,24},{4,28},{8,16},{12,20},{16,8},{20,12},{24,0},{28,4},{1,25},{... | collective-permute-start | bytes 614408 | tf_op jit(solution)/shard_map/ppermute | solution.py:199
  42.3 3.0 %spread.1 = (f32[1024,256]{1,0:T(8,128)S(1)}, bf16[1024,256]{1,0:T(8,128)(2,1)S(1)}, bf16[1024,256]{1,0:T(8,128)(2,1)S(1)}) custom-call(s32[3]{0:T(128)S(1)} %pad_add_fusion.place, s32[16,8]{1,0:T(8,128)S(1)} %copy.21.cols, bf16[16,64,512]{2,1,0:T(8,128)(2,1)S(1)} %get-tuple-element.49.adj, bf16[1024,1024]{1,0:T(8,128)(2,1)S(1)} %get-tuple-element.61.dh, ...), custom_call_target="tpu_custom_call" | custom-call | flops 805306368 | bytes 6291456 | tf_op jit(solution)/shard_map/spread/pallas_call | solution.py:325
  45.4 4.3 %collective-permute-start.6 = (bf16[512,256]{1,0:T(8,128)(2,1)S(1)}, bf16[512,256]{1,0:T(8,128)(2,1)S(1)}, u32[]{:S(2)}, u32[]{:S(2)}) collective-permute-start(bf16[512,256]{1,0:T(8,128)(2,1)S(1)} %slice.113), channel_id=1, source_target_pairs={{0,1},{1,2},{2,3},{3,4},{4,5},{5,6},{6,7},{7,8},{8,9},{9,10},{10,1... | collective-permute-start | bytes 786440 | tf_op jit(solution)/shard_map/ppermute | solution.py:348
  49.9 2.1 %finish.1 = (bf16[1024,256]{1,0:T(8,128)(2,1)}, f32[1024,256]{1,0:T(8,128)S(1)}) custom-call(bf16[1024,1024]{1,0:T(8,128)(2,1)S(1)} %get-tuple-element.64.hid, bf16[1024,1024]{1,0:T(8,128)(2,1)S(1)} %get-tuple-element.61.dh, bf16[1024,256]{1,0:T(8,128)(2,1)S(1)} %copy-done.6, f32[1,256]{1,0:T(1,128)S(1)} %bitcast.40, ...), custom_call_target="tpu_custom_call" | custom-call | flops 1073741824 | bytes 8388608 | tf_op jit(solution)/shard_map/finish/pallas_call | solution.py:338
  52.0 6.8 %collective-permute-done.3 = bf16[800,128]{1,0:T(8,128)(2,1)S(1)} collective-permute-done((bf16[800,128]{1,0:T(8,128)(2,1)S(1)}, bf16[800,128]{1,0:T(8,128)(2,1)S(1)}, u32[]{:S(2)}, u32[]{:S(2)}) %collective-permute-start.3) | collective-permute-done | bytes 204832 | tf_op jit(solution)/shard_map/ppermute | solution.py:199
  59.8 3.7 %collective-permute-start.9 = (bf16[224,128]{1,0:T(8,128)(2,1)S(1)}, bf16[224,128]{1,0:T(8,128)(2,1)S(1)}, u32[]{:S(2)}, u32[]{:S(2)}) collective-permute-start(bf16[224,128]{1,0:T(8,128)(2,1)S(1)} %get-tuple-element.107), channel_id=1, source_target_pairs={{0,3},{1,2},{2,1},{3,0},{4,7},{5,6},{6,5},{7,4},{8,11},{9,10},{10,... | collective-permute-start | bytes 172040 | tf_op jit(solution)/shard_map/ppermute | solution.py:199
  64.7 1.6 %collective-permute-done.9 = bf16[224,128]{1,0:T(8,128)(2,1)S(1)} collective-permute-done((bf16[224,128]{1,0:T(8,128)(2,1)S(1)}, bf16[224,128]{1,0:T(8,128)(2,1)S(1)}, u32[]{:S(2)}, u32[]{:S(2)}) %collective-permute-start.9) | collective-permute-done | bytes 57376 | tf_op jit(solution)/shard_map/ppermute | solution.py:199
  66.7 3.4 %collective-permute-start.13 = (bf16[192,128]{1,0:T(8,128)(2,1)S(1)}, bf16[192,128]{1,0:T(8,128)(2,1)S(1)}, u32[]{:S(2)}, u32[]{:S(2)}) collective-permute-start(bf16[192,128]{1,0:T(8,128)(2,1)S(1)} %fusion.1), channel_id=1, source_target_pairs={{0,3},{1,2},{2,1},{3,0},{4,7},{5,6},{6,5},{7,4},{8,11},{9,10},{10,... | collective-permute-start | bytes 147464 | tf_op jit(solution)/shard_map/ppermute | solution.py:199
  70.6 3.5 %collective-permute-start.15 = (bf16[512,256]{1,0:T(8,128)(2,1)S(1)}, bf16[512,256]{1,0:T(8,128)(2,1)S(1)}, u32[]{:S(2)}, u32[]{:S(2)}) collective-permute-start(bf16[512,256]{1,0:T(8,128)(2,1)S(1)} %slice.127), channel_id=1, source_target_pairs={{0,1},{1,2},{2,3},{3,4},{4,5},{5,6},{6,7},{7,8},{8,9},{9,10},{10,1... | collective-permute-start | bytes 786440 | tf_op jit(solution)/shard_map/ppermute | solution.py:354
  75.4 3.6 %collective-permute-start.14 = (bf16[2,192,128]{2,1,0:T(8,128)(2,1)S(1)}, bf16[2,192,128]{2,1,0:T(8,128)(2,1)S(1)}, u32[]{:S(2)}, u32[]{:S(2)}) collective-permute-start(bf16[2,192,128]{2,1,0:T(8,128)(2,1)S(1)} %get-tuple-element.102), channel_id=1, source_target_pairs={{0,8},{4,12},{8,0},{12,4},{16,24},{20,28},{24,16},{28,20},{1,9},{5... | collective-permute-start | bytes 294920 | tf_op jit(solution)/shard_map/ppermute | solution.py:199
  79.0 1.7 %collective-permute-start.11 = (bf16[2,192,128]{2,1,0:T(8,128)(2,1)S(1)}, bf16[2,192,128]{2,1,0:T(8,128)(2,1)S(1)}, u32[]{:S(2)}, u32[]{:S(2)}) collective-permute-start(bf16[2,192,128]{2,1,0:T(8,128)(2,1)S(1)} %get-tuple-element.104), channel_id=1, source_target_pairs={{0,16},{4,20},{8,24},{12,28},{16,0},{20,4},{24,8},{28,12},{1,17},{... | collective-permute-start | bytes 294920 | tf_op jit(solution)/shard_map/ppermute | solution.py:199
  80.7 3.4 %collective-permute-done.14 = bf16[2,192,128]{2,1,0:T(8,128)(2,1)S(1)} collective-permute-done((bf16[2,192,128]{2,1,0:T(8,128)(2,1)S(1)}, bf16[2,192,128]{2,1,0:T(8,128)(2,1)S(1)}, u32[]{:S(2)}, u32[]{:S(2)}) %collective-permute-start.14) | collective-permute-done | bytes 98336 | tf_op jit(solution)/shard_map/ppermute | solution.py:199
  85.1 2.0 %collective-permute-start.17 = (bf16[2,2,192,128]{3,2,1,0:T(8,128)(2,1)S(1)}, bf16[2,2,192,128]{3,2,1,0:T(8,128)(2,1)S(1)}, u32[]{:S(2)}, u32[]{:S(2)}) collective-permute-start(bf16[2,2,192,128]{3,2,1,0:T(8,128)(2,1)S(1)} %pad_maximum_fusion.9), channel_id=1, source_target_pairs={{0,16},{4,20},{8,24},{12,28},{16,0},{20,4},{24,8},{28,12},{1,17},{... | collective-permute-start | bytes 589832 | tf_op jit(solution)/shard_map/ppermute | solution.py:199
  87.1 3.9 %collective-permute-done.16 = bf16[2,2,192,128]{3,2,1,0:T(8,128)(2,1)S(1)} collective-permute-done((bf16[2,2,192,128]{3,2,1,0:T(8,128)(2,1)S(1)}, bf16[2,2,192,128]{3,2,1,0:T(8,128)(2,1)S(1)}, u32[]{:S(2)}, u32[]{:S(2)}) %collective-permute-start.16) | collective-permute-done | bytes 196640 | tf_op jit(solution)/shard_map/ppermute | solution.py:199
  91.3 2.6 %first_unpack.1 = (f32[256,1024]{1,0:T(8,128)}, f32[256,1024]{1,0:T(8,128)}, f32[1024,256]{1,0:T(8,128)}, bf16[1024,256]{1,0:T(8,128)(2,1)}, f32[8,128]{1,0:T(8,128)}, /*index=5*/f32[2,128]{1,0:T(2,128)}) custom-call(s32[3]{0:T(128)S(1)} %pad_add_fusion.place, bf16[4,4,192,128]{3,2,1,0:T(8,128)(2,1)S(1)} %maximum_maximum_fusion.src, ...), custom_call_target="tpu_custom_call" | custom-call | flops 1048576 | bytes 3145728 | tf_op jit(solution)/shard_map/first_unpack/pallas_call | solution.py:364
  94.0 1.8 %second_unpack.1 = (f32[256,1024]{1,0:T(8,128)}, f32[256,1024]{1,0:T(8,128)}, f32[1024,256]{1,0:T(8,128)}) custom-call(s32[3]{0:T(128)S(1)} %pad_add_fusion.place, bf16[4,4,192,128]{3,2,1,0:T(8,128)(2,1)S(1)} %collective-permute-done.19.src, f32[256,1024]{1,0:T(8,128)} %get-tuple-element.83._0, ...), custom_call_target="tpu_custom_call", output_to_operand_aliasing={{0}: (2, {}), {1}: (3, {}), {2}: (4, {})} | custom-call | flops 524288 | bytes 2359296 | tf_op jit(solution)/shard_map/second_unpack/pallas_call | solution.py:375
  (71 shorter events, 14.5 us)
Async XLA Ops:
  0.6 17.1 %collective-permute-start.1 = (bf16[1024,256]{1,0:T(8,128)(2,1)}, bf16[1024,256]{1,0:T(8,128)(2,1)S(1)}, u32[]{:S(2)}, u32[]{:S(2)}) collective-permute-start(bf16[1024,256]{1,0:T(8,128)(2,1)} %x.3), channel_id=1, source_target_pairs={{1,0},{2,1},{3,2},{4,3},{5,4},{6,5},{7,6},{8,7},{9,8},{10,9},{11,1... | collective-permute-start | bytes 1572872 | tf_op jit(solution)/shard_map/ppermute | solution.py:280
  1.9 18.1 %collective-permute-start = (bf16[1024,256]{1,0:T(8,128)(2,1)}, bf16[1024,256]{1,0:T(8,128)(2,1)S(1)}, u32[]{:S(2)}, u32[]{:S(2)}) collective-permute-start(bf16[1024,256]{1,0:T(8,128)(2,1)} %x.3), channel_id=1, source_target_pairs={{0,1},{1,2},{2,3},{3,4},{4,5},{5,6},{6,7},{7,8},{8,9},{9,10},{10,1... | collective-permute-start | bytes 1572872 | tf_op jit(solution)/shard_map/ppermute | solution.py:279
  15.8 4.3 %copy-start.2 = (bf16[1024,256]{1,0:T(8,128)(2,1)S(1)}, bf16[1024,256]{1,0:T(8,128)(2,1)}, u32[]{:S(2)}) copy-start(bf16[1024,256]{1,0:T(8,128)(2,1)} %x.3) | copy-start | bytes 1572868
  15.8 4.3 %copy-start.4 = (bf16[256,1024]{1,0:T(8,128)(2,1)S(1)}, bf16[256,1024]{1,0:T(8,128)(2,1)}, u32[]{:S(2)}) copy-start(bf16[256,1024]{1,0:T(8,128)(2,1)} %wn.3) | copy-start | bytes 1572868
  25.7 12.9 %collective-permute-start.2 = (bf16[3104,128]{1,0:T(8,128)(2,1)S(1)}, bf16[3104,128]{1,0:T(8,128)(2,1)S(1)}, u32[]{:S(2)}, u32[]{:S(2)}) collective-permute-start(bf16[3104,128]{1,0:T(8,128)(2,1)S(1)} %get-tuple-element.56), channel_id=1, source_target_pairs={{0,4},{4,0},{8,12},{12,8},{16,20},{20,16},{24,28},{28,24},{1,5},{5... | collective-permute-start | bytes 2383880 | tf_op jit(solution)/shard_map/ppermute | solution.py:199
  39.0 13.0 %collective-permute-start.4 = (bf16[800,128]{1,0:T(8,128)(2,1)S(1)}, bf16[800,128]{1,0:T(8,128)(2,1)S(1)}, u32[]{:S(2)}, u32[]{:S(2)}) collective-permute-start(bf16[800,128]{1,0:T(8,128)(2,1)S(1)} %get-tuple-element.109), channel_id=1, source_target_pairs={{0,16},{4,20},{8,24},{12,28},{16,0},{20,4},{24,8},{28,12},{1,17},{... | collective-permute-start | bytes 614408 | tf_op jit(solution)/shard_map/ppermute | solution.py:199
  40.9 11.1 %collective-permute-start.5 = (bf16[800,128]{1,0:T(8,128)(2,1)S(1)}, bf16[800,128]{1,0:T(8,128)(2,1)S(1)}, u32[]{:S(2)}, u32[]{:S(2)}) collective-permute-start(bf16[800,128]{1,0:T(8,128)(2,1)S(1)} %get-tuple-element.110), channel_id=1, source_target_pairs={{0,24},{4,28},{8,16},{12,20},{16,8},{20,12},{24,0},{28,4},{1,25},{... | collective-permute-start | bytes 614408 | tf_op jit(solution)/shard_map/ppermute | solution.py:199
  42.3 7.6 %copy-start.6 = (bf16[1024,256]{1,0:T(8,128)(2,1)S(1)}, bf16[1024,256]{1,0:T(8,128)(2,1)}, u32[]{:S(2)}) copy-start(bf16[1024,256]{1,0:T(8,128)(2,1)} %wo.3) | copy-start | bytes 1572868
  42.3 7.6 %copy-start.10 = (f32[256]{0:T(256)S(1)}, f32[256]{0:T(256)}, u32[]{:S(2)}) copy-start(f32[256]{0:T(256)} %param.16) | copy-start | bytes 3076
  45.4 13.6 %collective-permute-start.6 = (bf16[512,256]{1,0:T(8,128)(2,1)S(1)}, bf16[512,256]{1,0:T(8,128)(2,1)S(1)}, u32[]{:S(2)}, u32[]{:S(2)}) collective-permute-start(bf16[512,256]{1,0:T(8,128)(2,1)S(1)} %slice.113), channel_id=1, source_target_pairs={{0,1},{1,2},{2,3},{3,4},{4,5},{5,6},{6,7},{7,8},{8,9},{9,10},{10,1... | collective-permute-start | bytes 786440 | tf_op jit(solution)/shard_map/ppermute | solution.py:348
  49.7 9.1 %collective-permute-start.3 = (bf16[800,128]{1,0:T(8,128)(2,1)S(1)}, bf16[800,128]{1,0:T(8,128)(2,1)S(1)}, u32[]{:S(2)}, u32[]{:S(2)}) collective-permute-start(bf16[800,128]{1,0:T(8,128)(2,1)S(1)} %get-tuple-element.108), channel_id=1, source_target_pairs={{0,8},{4,12},{8,0},{12,4},{16,24},{20,28},{24,16},{28,20},{1,9},{5... | collective-permute-start | bytes 614408 | tf_op jit(solution)/shard_map/ppermute | solution.py:199
  59.0 4.5 %collective-permute-start.7 = (bf16[224,128]{1,0:T(8,128)(2,1)S(1)}, bf16[224,128]{1,0:T(8,128)(2,1)S(1)}, u32[]{:S(2)}, u32[]{:S(2)}) collective-permute-start(bf16[224,128]{1,0:T(8,128)(2,1)S(1)} %get-tuple-element.105), channel_id=1, source_target_pairs={{0,1},{1,0},{2,3},{3,2},{4,5},{5,4},{6,7},{7,6},{8,9},{9,8},{10,11... | collective-permute-start | bytes 172040 | tf_op jit(solution)/shard_map/ppermute | solution.py:199
  59.1 5.6 %collective-permute-start.8 = (bf16[224,128]{1,0:T(8,128)(2,1)S(1)}, bf16[224,128]{1,0:T(8,128)(2,1)S(1)}, u32[]{:S(2)}, u32[]{:S(2)}) collective-permute-start(bf16[224,128]{1,0:T(8,128)(2,1)S(1)} %get-tuple-element.106), channel_id=1, source_target_pairs={{0,2},{1,3},{2,0},{3,1},{4,6},{5,7},{6,4},{7,5},{8,10},{9,11},{10,... | collective-permute-start | bytes 172040 | tf_op jit(solution)/shard_map/ppermute | solution.py:199
  59.8 6.6 %collective-permute-start.9 = (bf16[224,128]{1,0:T(8,128)(2,1)S(1)}, bf16[224,128]{1,0:T(8,128)(2,1)S(1)}, u32[]{:S(2)}, u32[]{:S(2)}) collective-permute-start(bf16[224,128]{1,0:T(8,128)(2,1)S(1)} %get-tuple-element.107), channel_id=1, source_target_pairs={{0,3},{1,2},{2,1},{3,0},{4,7},{5,6},{6,5},{7,4},{8,11},{9,10},{10,... | collective-permute-start | bytes 172040 | tf_op jit(solution)/shard_map/ppermute | solution.py:199
  66.4 9.0 %collective-permute-start.12 = (bf16[192,128]{1,0:T(8,128)(2,1)S(1)}, bf16[192,128]{1,0:T(8,128)(2,1)S(1)}, u32[]{:S(2)}, u32[]{:S(2)}) collective-permute-start(bf16[192,128]{1,0:T(8,128)(2,1)S(1)} %fusion.1), channel_id=1, source_target_pairs={{0,2},{1,3},{2,0},{3,1},{4,6},{5,7},{6,4},{7,5},{8,10},{9,11},{10,... | collective-permute-start | bytes 147464 | tf_op jit(solution)/shard_map/ppermute | solution.py:199
  66.7 8.7 %collective-permute-start.13 = (bf16[192,128]{1,0:T(8,128)(2,1)S(1)}, bf16[192,128]{1,0:T(8,128)(2,1)S(1)}, u32[]{:S(2)}, u32[]{:S(2)}) collective-permute-start(bf16[192,128]{1,0:T(8,128)(2,1)S(1)} %fusion.1), channel_id=1, source_target_pairs={{0,3},{1,2},{2,1},{3,0},{4,7},{5,6},{6,5},{7,4},{8,11},{9,10},{10,... | collective-permute-start | bytes 147464 | tf_op jit(solution)/shard_map/ppermute | solution.py:199
  70.1 8.9 %collective-permute-start.10 = (bf16[192,128]{1,0:T(8,128)(2,1)S(1)}, bf16[192,128]{1,0:T(8,128)(2,1)S(1)}, u32[]{:S(2)}, u32[]{:S(2)}) collective-permute-start(bf16[192,128]{1,0:T(8,128)(2,1)S(1)} %fusion.1), channel_id=1, source_target_pairs={{0,1},{1,0},{2,3},{3,2},{4,5},{5,4},{6,7},{7,6},{8,9},{9,8},{10,11... | collective-permute-start | bytes 147464 | tf_op jit(solution)/shard_map/ppermute | solution.py:199
  70.6 13.6 %collective-permute-start.15 = (bf16[512,256]{1,0:T(8,128)(2,1)S(1)}, bf16[512,256]{1,0:T(8,128)(2,1)S(1)}, u32[]{:S(2)}, u32[]{:S(2)}) collective-permute-start(bf16[512,256]{1,0:T(8,128)(2,1)S(1)} %slice.127), channel_id=1, source_target_pairs={{0,1},{1,2},{2,3},{3,4},{4,5},{5,6},{6,7},{7,8},{8,9},{9,10},{10,1... | collective-permute-start | bytes 786440 | tf_op jit(solution)/shard_map/ppermute | solution.py:354
  74.1 17.1 %collective-permute-start.18 = (bf16[1024,256]{1,0:T(8,128)(2,1)S(1)}, bf16[1024,256]{1,0:T(8,128)(2,1)S(1)}, u32[]{:S(2)}, u32[]{:S(2)}) collective-permute-start(bf16[1024,256]{1,0:T(8,128)(2,1)S(1)} %get-tuple-element.76), channel_id=1, source_target_pairs={{1,0},{2,1},{3,2},{4,3},{5,4},{6,5},{7,6},{8,7},{9,8},{10,9},{11,1... | collective-permute-start | bytes 1572872 | tf_op jit(solution)/shard_map/ppermute | solution.py:353
  75.4 8.7 %collective-permute-start.14 = (bf16[2,192,128]{2,1,0:T(8,128)(2,1)S(1)}, bf16[2,192,128]{2,1,0:T(8,128)(2,1)S(1)}, u32[]{:S(2)}, u32[]{:S(2)}) collective-permute-start(bf16[2,192,128]{2,1,0:T(8,128)(2,1)S(1)} %get-tuple-element.102), channel_id=1, source_target_pairs={{0,8},{4,12},{8,0},{12,4},{16,24},{20,28},{24,16},{28,20},{1,9},{5... | collective-permute-start | bytes 294920 | tf_op jit(solution)/shard_map/ppermute | solution.py:199
  79.0 5.1 %collective-permute-start.11 = (bf16[2,192,128]{2,1,0:T(8,128)(2,1)S(1)}, bf16[2,192,128]{2,1,0:T(8,128)(2,1)S(1)}, u32[]{:S(2)}, u32[]{:S(2)}) collective-permute-start(bf16[2,192,128]{2,1,0:T(8,128)(2,1)S(1)} %get-tuple-element.104), channel_id=1, source_target_pairs={{0,16},{4,20},{8,24},{12,28},{16,0},{20,4},{24,8},{28,12},{1,17},{... | collective-permute-start | bytes 294920 | tf_op jit(solution)/shard_map/ppermute | solution.py:199
  84.2 6.8 %collective-permute-start.16 = (bf16[2,2,192,128]{3,2,1,0:T(8,128)(2,1)S(1)}, bf16[2,2,192,128]{3,2,1,0:T(8,128)(2,1)S(1)}, u32[]{:S(2)}, u32[]{:S(2)}) collective-permute-start(bf16[2,2,192,128]{3,2,1,0:T(8,128)(2,1)S(1)} %pad_maximum_fusion.8), channel_id=1, source_target_pairs={{0,8},{4,12},{8,0},{12,4},{16,24},{20,28},{24,16},{28,20},{1,9},{5... | collective-permute-start | bytes 589832 | tf_op jit(solution)/shard_map/ppermute | solution.py:199
  85.1 6.0 %collective-permute-start.17 = (bf16[2,2,192,128]{3,2,1,0:T(8,128)(2,1)S(1)}, bf16[2,2,192,128]{3,2,1,0:T(8,128)(2,1)S(1)}, u32[]{:S(2)}, u32[]{:S(2)}) collective-permute-start(bf16[2,2,192,128]{3,2,1,0:T(8,128)(2,1)S(1)} %pad_maximum_fusion.9), channel_id=1, source_target_pairs={{0,16},{4,20},{8,24},{12,28},{16,0},{20,4},{24,8},{28,12},{1,17},{... | collective-permute-start | bytes 589832 | tf_op jit(solution)/shard_map/ppermute | solution.py:199
  91.2 2.8 %collective-permute-start.19 = (bf16[4,4,192,128]{3,2,1,0:T(8,128)(2,1)S(1)}, bf16[4,4,192,128]{3,2,1,0:T(8,128)(2,1)S(1)}, u32[]{:S(2)}, u32[]{:S(2)}) collective-permute-start(bf16[4,4,192,128]{3,2,1,0:T(8,128)(2,1)S(1)} %maximum_maximum_fusion.src), channel_id=1, source_target_pairs={{0,4},{4,0},{8,12},{12,8},{16,20},{20,16},{24,28},{28,24},{1,5},{5... | collective-permute-start | bytes 2359304 | tf_op jit(solution)/shard_map/ppermute | solution.py:199
  (7 other events, 7.5 us)

commit v4 on v3

--- a/solution.py
+++ b/solution.py
@@ -78,7 +78,7 @@
     core = lax.rem(me, 2)
     pair = me // 2
     sums[...] = jnp.zeros(sums.shape, F32)
-    step = 256
+    step = 512
     for c in range(hidden // chunk):
         at = slice(c * chunk, (c + 1) * chunk)
         for r in range(0, rows, step):
@@ -172,13 +172,17 @@
     scale, place, src, own, from_low, from_high, bias,
     g_self, g_neigh, g_out, features, bias_hidden, bias_out, *scratch
 ):
+    summed, done, *scratch = scratch
+    summed[...] = (own[...] + from_low[...].astype(F32) + from_high[...].astype(F32)).astype(BF16)
+    store = pltpu.make_async_copy(summed, features, done)
+    store.start()
     copies = place_grads(scale, 0, place, src, (g_self, g_neigh, g_out), scratch)
-    features[...] = (own[...] + from_low[...].astype(F32) + from_high[...].astype(F32)).astype(BF16)
     top, count = bias_hidden.shape[0], bias_out.shape[0]
     bias_hidden[...] = bias[:top] * scale
     bias_out[...] = bias[top : top + count] * scale
     for copy in copies:
         copy.wait()
+    store.wait()
 
 
 def second_unpack_kernel(scale, place, src, _0, _1, _2, g_self, g_neigh, g_out, *scratch):
@@ -335,6 +339,8 @@
         name="spread",
     )(place, cols, adj, dh, wn_t)
     acc, bias = reduce_among([acc[i] for i in range(4)], bias, "row", (2, 4, 6))
+    end = 6 * rows // 16
+    acc, hid, dh, own = lax.optimization_barrier((acc, hid, dh, own))
     embed, own = pl.pallas_call(
         finish_kernel,
         out_shape=(sds((rows, width), BF16), sds((rows, width), F32)),
@@ -344,20 +350,18 @@
         cost_estimate=pl.CostEstimate(flops=4 * rows * width * hidden, bytes_accessed=8 << 20, transcendentals=0),
         name="finish",
     )(hid, dh, wo, bias_out.reshape(1, -1), ws_t, own)
-    cut = 8 * rows // 16
-    first = lax.ppermute(to_high[:cut], both, forward)
-    acc, first, embed, own = lax.optimization_barrier((acc, first, embed, own))
     part, bias = reduce_among([acc[i] for i in range(4)], bias, "col", (1, 2, 3))
-    part, to_low, to_high = lax.optimization_barrier((part, to_low, to_high))
+    second = lax.ppermute(to_high[0:end], both, forward)
+    part, second, to_low, to_high, embed, own = lax.optimization_barrier((part, second, to_low, to_high, embed, own))
     part, bias = reduce_far(part, bias)
     from_high = lax.ppermute(to_low, both, backward)
-    last = lax.ppermute(to_high[cut:], both, forward)
+    last = lax.ppermute(to_high[end:], both, forward)
     part = gather_among(part, "col", (1, 2, 3))
     a, b = gather_near(part)
     a, b, last = lax.optimization_barrier((a, b, last))
     mine = gather_across(a, b)
     mine, from_high = lax.optimization_barrier((mine, from_high))
-    from_low = jnp.concatenate([first, last])
+    from_low = jnp.concatenate([second, last])
     other = swap(mine, "row", 1)
     anywhere = pl.BlockSpec(memory_space=pl.ANY)
     grads = (sds((width, hidden), F32), sds((width, hidden), F32), sds((hidden, width), F32))
@@ -366,8 +370,8 @@
         out_shape=grads
         + (sds((rows, width), BF16), sds((hidden // LANES, LANES), F32), sds((width // LANES, LANES), F32)),
         in_specs=[smem()] + [vmem()] * 5,
-        out_specs=[anywhere] * 3 + [vmem()] * 3,
-        scratch_shapes=unpack_scratch(width),
+        out_specs=[anywhere] * 4 + [vmem()] * 2,
+        scratch_shapes=[pltpu.VMEM((rows, width), BF16), pltpu.SemaphoreType.DMA] + unpack_scratch(width),
         compiler_params=params(10),
         cost_estimate=pl.CostEstimate(flops=4 * width * hidden, bytes_accessed=12 * width * hidden, transcendentals=0),
         name="first_unpack",

time: 96.4 us -> 93.8 us (0.973)
  waiting for transfers between devices: 21.6 us -> 17.6 us
  starting transfers between devices: 47.4 us -> 49 us
    ppermute x15, waiting for transfers between devices: 18.9 us -> 14.9 us  [swap(): lax.ppermute(value, axis, [(i, i ^ bit) for i in range(lax.axis_size(axis...]
    ppermute x15, starting transfers between devices: 31.4 us -> 34.7 us  [swap(): lax.ppermute(value, axis, [(i, i ^ bit) for i in range(lax.axis_size(axis...]
    ppermute x2, starting transfers between devices: 7.75 us -> 6.09 us  [the longest x1 4.17 us: local(): second = lax.ppermute(to_high[0:end], both, forward)]
  transfers between devices with their start and end apart: 20 -> 20, of which waited for: 8 -> 10; matrix products, arithmetic and copies ran while one was open for 1% -> 1% of each run, Pallas kernels for 10% -> 10%
where the time goes in v4:
time: 93.8 us; the launch traced here: 93.3 us
  starting transfers between devices  49 us (52%)
  waiting for transfers between devices  17.6 us (19%)
  Pallas kernels  16.4 us (17%)
  local copies, waits for them, and re-layouts  8.39 us (9%)
  between operations  0.95 us (1%)
    ppermute x15, starting transfers between devices, swap(): lax.ppermute(value, axis, [(i, i ^ bit) for i in range(lax.axis_size(axis...  34.7 us
    ppermute x15, waiting for transfers between devices, swap(): lax.ppermute(value, axis, [(i, i ^ bit) for i in range(lax.axis_size(axis...  14.9 us
    unnamed x23, local copies, waits for them, and re-layouts  8.26 us
    ppermute x1, starting transfers between devices, local(): low = lax.ppermute(x, both, forward)  5.59 us
    pallas_call x1, Pallas kernels, local(): pl.pallas_call(forward_kernel, out_shape=(sds((rows, hidden), BF16), sds(...  5.38 us
    ppermute x1, starting transfers between devices, local(): second = lax.ppermute(to_high[0:end], both, forward)  4.17 us
    pallas_call x1, Pallas kernels, local(): pl.pallas_call(spread_kernel, out_shape=(sds((rows, width), F32), sds((ro...  3.04 us
    pallas_call x1, Pallas kernels, local(): pl.pallas_call(functools.partial(first_unpack_kernel, grad_scale), out_sh...  2.63 us
  transfers between devices with their start and end apart: 20, of which 10 were waited for; matrix products, arithmetic and copies ran while one was open for 1% of the time, Pallas kernels for 10%

profile of v4, /device:TPU:0, one launch (start us, length us, event | category | flops | bytes accessed | tf_op | source)
XLA Modules:
  0.0 93.3 jit_solution(675526328506626188)
XLA Ops:
  1.9 5.6 %collective-permute-start = (bf16[1024,256]{1,0:T(8,128)(2,1)}, bf16[1024,256]{1,0:T(8,128)(2,1)S(1)}, u32[]{:S(2)}, u32[]{:S(2)}) collective-permute-start(bf16[1024,256]{1,0:T(8,128)(2,1)} %x.3), channel_id=1, source_target_pairs={{0,1},{1,2},{2,3},{3,4},{4,5},{5,6},{6,7},{7,8},{8,9},{9,10},{10,1... | collective-permute-start | bytes 1572872 | tf_op jit(solution)/shard_map/ppermute | solution.py:283
  8.3 1.6 %copy-done = s32[16,64,512]{2,1,0:T(8,128)S(1)} copy-done((s32[16,64,512]{2,1,0:T(8,128)S(1)}, s32[16,64,512]{2,1,0:T(8,128)}, u32[]{:S(2)}) %copy-start) | copy-done | bytes 2097176
  17.7 2.3 %collective-permute-done.lo = bf16[1024,256]{1,0:T(8,128)(2,1)S(1)} collective-permute-done((bf16[1024,256]{1,0:T(8,128)(2,1)}, bf16[1024,256]{1,0:T(8,128)(2,1)S(1)}, u32[]{:S(2)}, u32[]{:S(2)}) %collective-permute-start) | collective-permute-done | bytes 524320 | tf_op jit(solution)/shard_map/ppermute | solution.py:283
  20.0 5.4 %forward.1 = (bf16[1024,1024]{1,0:T(8,128)(2,1)S(1)}, bf16[1024,1024]{1,0:T(8,128)(2,1)S(1)}, f32[3072,128]{1,0:T(8,128)S(1)}, bf16[3104,128]{1,0:T(8,128)(2,1)S(1)}, f32[16,128]{1,0:T(8,128)S(1)}) custom-call(s32[3]{0:T(128)S(1)} %pad_add_fusion.place, s32[16,8]{1,0:T(8,128)S(1)} %copy.21.cols, bf16[1024,256]{1,0:T(8,128)(2,1)S(1)} %collective-permute-done.lo, ...), custom_call_target="tpu_custom_call" | custom-call | flops 2415919104 | bytes 14680064 | tf_op jit(solution)/shard_map/forward/pallas_call | solution.py:304
  25.4 11.0 %collective-permute-start.2 = (bf16[3104,128]{1,0:T(8,128)(2,1)S(1)}, bf16[3104,128]{1,0:T(8,128)(2,1)S(1)}, u32[]{:S(2)}, u32[]{:S(2)}) collective-permute-start(bf16[3104,128]{1,0:T(8,128)(2,1)S(1)} %get-tuple-element.59), channel_id=1, source_target_pairs={{0,4},{4,0},{8,12},{12,8},{16,20},{20,16},{24,28},{28,24},{1,5},{5... | collective-permute-start | bytes 2383880 | tf_op jit(solution)/shard_map/ppermute | solution.py:203
  36.4 1.9 %collective-permute-done.2 = bf16[3104,128]{1,0:T(8,128)(2,1)S(1)} collective-permute-done((bf16[3104,128]{1,0:T(8,128)(2,1)S(1)}, bf16[3104,128]{1,0:T(8,128)(2,1)S(1)}, u32[]{:S(2)}, u32[]{:S(2)}) %collective-permute-start.2) | collective-permute-done | bytes 794656 | tf_op jit(solution)/shard_map/ppermute | solution.py:203
  38.7 1.9 %collective-permute-start.3 = (bf16[800,128]{1,0:T(8,128)(2,1)S(1)}, bf16[800,128]{1,0:T(8,128)(2,1)S(1)}, u32[]{:S(2)}, u32[]{:S(2)}) collective-permute-start(bf16[800,128]{1,0:T(8,128)(2,1)S(1)} %get-tuple-element.114), channel_id=1, source_target_pairs={{0,8},{4,12},{8,0},{12,4},{16,24},{20,28},{24,16},{28,20},{1,9},{5... | collective-permute-start | bytes 614408 | tf_op jit(solution)/shard_map/ppermute | solution.py:203
  42.3 3.0 %spread.1 = (f32[1024,256]{1,0:T(8,128)S(1)}, bf16[1024,256]{1,0:T(8,128)(2,1)S(1)}, bf16[1024,256]{1,0:T(8,128)(2,1)S(1)}) custom-call(s32[3]{0:T(128)S(1)} %pad_add_fusion.place, s32[16,8]{1,0:T(8,128)S(1)} %copy.21.cols, bf16[16,64,512]{2,1,0:T(8,128)(2,1)S(1)} %get-tuple-element.52.adj, bf16[1024,1024]{1,0:T(8,128)(2,1)S(1)} %get-tuple-element.72.dh, ...), custom_call_target="tpu_custom_call" | custom-call | flops 805306368 | bytes 6291456 | tf_op jit(solution)/shard_map/spread/pallas_call | solution.py:329
  45.3 4.2 %collective-permute-start.9 = (bf16[384,256]{1,0:T(8,128)(2,1)S(1)}, bf16[384,256]{1,0:T(8,128)(2,1)S(1)}, u32[]{:S(2)}, u32[]{:S(2)}) collective-permute-start(bf16[384,256]{1,0:T(8,128)(2,1)S(1)} %slice.126), channel_id=1, source_target_pairs={{0,1},{1,2},{2,3},{3,4},{4,5},{5,6},{6,7},{7,8},{8,9},{9,10},{10,1... | collective-permute-start | bytes 589832 | tf_op jit(solution)/shard_map/ppermute | solution.py:354
  49.6 2.3 %collective-permute-done.4 = bf16[800,128]{1,0:T(8,128)(2,1)S(1)} collective-permute-done((bf16[800,128]{1,0:T(8,128)(2,1)S(1)}, bf16[800,128]{1,0:T(8,128)(2,1)S(1)}, u32[]{:S(2)}, u32[]{:S(2)}) %collective-permute-start.4) | collective-permute-done | bytes 204832 | tf_op jit(solution)/shard_map/ppermute | solution.py:203
  52.1 2.4 %collective-permute-start.6 = (bf16[224,128]{1,0:T(8,128)(2,1)S(1)}, bf16[224,128]{1,0:T(8,128)(2,1)S(1)}, u32[]{:S(2)}, u32[]{:S(2)}) collective-permute-start(bf16[224,128]{1,0:T(8,128)(2,1)S(1)} %get-tuple-element.111), channel_id=1, source_target_pairs={{0,1},{1,0},{2,3},{3,2},{4,5},{5,4},{6,7},{7,6},{8,9},{9,8},{10,11... | collective-permute-start | bytes 172040 | tf_op jit(solution)/shard_map/ppermute | solution.py:203
  54.5 2.1 %collective-permute-start.7 = (bf16[224,128]{1,0:T(8,128)(2,1)S(1)}, bf16[224,128]{1,0:T(8,128)(2,1)S(1)}, u32[]{:S(2)}, u32[]{:S(2)}) collective-permute-start(bf16[224,128]{1,0:T(8,128)(2,1)S(1)} %get-tuple-element.112), channel_id=1, source_target_pairs={{0,2},{1,3},{2,0},{3,1},{4,6},{5,7},{6,4},{7,5},{8,10},{9,11},{10,... | collective-permute-start | bytes 172040 | tf_op jit(solution)/shard_map/ppermute | solution.py:203
  57.0 2.1 %finish.1 = (bf16[1024,256]{1,0:T(8,128)(2,1)}, f32[1024,256]{1,0:T(8,128)S(1)}) custom-call(bf16[1024,1024]{1,0:T(8,128)(2,1)S(1)} %get-tuple-element.71.hid, bf16[1024,1024]{1,0:T(8,128)(2,1)S(1)} %get-tuple-element.72.dh, bf16[1024,256]{1,0:T(8,128)(2,1)S(1)} %copy-done.6, f32[1,256]{1,0:T(1,128)S(1)} %bitcast.40, ...), custom_call_target="tpu_custom_call" | custom-call | flops 1073741824 | bytes 8388608 | tf_op jit(solution)/shard_map/finish/pallas_call | solution.py:344
  60.5 2.2 %collective-permute-done.8 = bf16[224,128]{1,0:T(8,128)(2,1)S(1)} collective-permute-done((bf16[224,128]{1,0:T(8,128)(2,1)S(1)}, bf16[224,128]{1,0:T(8,128)(2,1)S(1)}, u32[]{:S(2)}, u32[]{:S(2)}) %collective-permute-start.8) | collective-permute-done | bytes 57376 | tf_op jit(solution)/shard_map/ppermute | solution.py:203
  64.2 2.2 %collective-permute-start.10 = (bf16[192,128]{1,0:T(8,128)(2,1)S(1)}, bf16[192,128]{1,0:T(8,128)(2,1)S(1)}, u32[]{:S(2)}, u32[]{:S(2)}) collective-permute-start(bf16[192,128]{1,0:T(8,128)(2,1)S(1)} %fusion.1), channel_id=1, source_target_pairs={{0,1},{1,0},{2,3},{3,2},{4,5},{5,4},{6,7},{7,6},{8,9},{9,8},{10,11... | collective-permute-start | bytes 147464 | tf_op jit(solution)/shard_map/ppermute | solution.py:203
  66.4 1.9 %collective-permute-start.15 = (bf16[640,256]{1,0:T(8,128)(2,1)S(1)}, bf16[640,256]{1,0:T(8,128)(2,1)S(1)}, u32[]{:S(2)}, u32[]{:S(2)}) collective-permute-start(bf16[640,256]{1,0:T(8,128)(2,1)S(1)} %slice.127), channel_id=1, source_target_pairs={{0,1},{1,2},{2,3},{3,4},{4,5},{5,6},{6,7},{7,8},{8,9},{9,10},{10,1... | collective-permute-start | bytes 983048 | tf_op jit(solution)/shard_map/ppermute | solution.py:358
  69.7 6.1 %collective-permute-start.14 = (bf16[2,192,128]{2,1,0:T(8,128)(2,1)S(1)}, bf16[2,192,128]{2,1,0:T(8,128)(2,1)S(1)}, u32[]{:S(2)}, u32[]{:S(2)}) collective-permute-start(bf16[2,192,128]{2,1,0:T(8,128)(2,1)S(1)} %get-tuple-element.108), channel_id=1, source_target_pairs={{0,8},{4,12},{8,0},{12,4},{16,24},{20,28},{24,16},{28,20},{1,9},{5... | collective-permute-start | bytes 294920 | tf_op jit(solution)/shard_map/ppermute | solution.py:203
  77.1 2.9 %collective-permute-done.14 = bf16[2,192,128]{2,1,0:T(8,128)(2,1)S(1)} collective-permute-done((bf16[2,192,128]{2,1,0:T(8,128)(2,1)S(1)}, bf16[2,192,128]{2,1,0:T(8,128)(2,1)S(1)}, u32[]{:S(2)}, u32[]{:S(2)}) %collective-permute-start.14) | collective-permute-done | bytes 98336 | tf_op jit(solution)/shard_map/ppermute | solution.py:203
  80.6 2.2 %collective-permute-start.16 = (bf16[2,2,192,128]{3,2,1,0:T(8,128)(2,1)S(1)}, bf16[2,2,192,128]{3,2,1,0:T(8,128)(2,1)S(1)}, u32[]{:S(2)}, u32[]{:S(2)}) collective-permute-start(bf16[2,2,192,128]{3,2,1,0:T(8,128)(2,1)S(1)} %pad_maximum_fusion.8), channel_id=1, source_target_pairs={{0,8},{4,12},{8,0},{12,4},{16,24},{20,28},{24,16},{28,20},{1,9},{5... | collective-permute-start | bytes 589832 | tf_op jit(solution)/shard_map/ppermute | solution.py:203
  82.8 2.1 %collective-permute-start.17 = (bf16[2,2,192,128]{3,2,1,0:T(8,128)(2,1)S(1)}, bf16[2,2,192,128]{3,2,1,0:T(8,128)(2,1)S(1)}, u32[]{:S(2)}, u32[]{:S(2)}) collective-permute-start(bf16[2,2,192,128]{3,2,1,0:T(8,128)(2,1)S(1)} %pad_maximum_fusion.9), channel_id=1, source_target_pairs={{0,16},{4,20},{8,24},{12,28},{16,0},{20,4},{24,8},{28,12},{1,17},{... | collective-permute-start | bytes 589832 | tf_op jit(solution)/shard_map/ppermute | solution.py:203
  84.9 1.5 %collective-permute-done.16 = bf16[2,2,192,128]{3,2,1,0:T(8,128)(2,1)S(1)} collective-permute-done((bf16[2,2,192,128]{3,2,1,0:T(8,128)(2,1)S(1)}, bf16[2,2,192,128]{3,2,1,0:T(8,128)(2,1)S(1)}, u32[]{:S(2)}, u32[]{:S(2)}) %collective-permute-start.16) | collective-permute-done | bytes 196640 | tf_op jit(solution)/shard_map/ppermute | solution.py:203
  86.5 2.0 %collective-permute-done.17 = bf16[2,2,192,128]{3,2,1,0:T(8,128)(2,1)S(1)} collective-permute-done((bf16[2,2,192,128]{3,2,1,0:T(8,128)(2,1)S(1)}, bf16[2,2,192,128]{3,2,1,0:T(8,128)(2,1)S(1)}, u32[]{:S(2)}, u32[]{:S(2)}) %collective-permute-start.17) | collective-permute-done | bytes 196640 | tf_op jit(solution)/shard_map/ppermute | solution.py:203
  88.8 2.6 %first_unpack.1 = (f32[256,1024]{1,0:T(8,128)}, f32[256,1024]{1,0:T(8,128)}, f32[1024,256]{1,0:T(8,128)}, bf16[1024,256]{1,0:T(8,128)(2,1)}, f32[8,128]{1,0:T(8,128)}, /*index=5*/f32[2,128]{1,0:T(2,128)}) custom-call(s32[3]{0:T(128)S(1)} %pad_add_fusion.place, bf16[4,4,192,128]{3,2,1,0:T(8,128)(2,1)S(1)} %maximum_maximum_fusion.src, ...), custom_call_target="tpu_custom_call" | custom-call | flops 1048576 | bytes 3145728 | tf_op jit(solution)/shard_map/first_unpack/pallas_call | solution.py:368
  91.4 1.8 %second_unpack.1 = (f32[256,1024]{1,0:T(8,128)}, f32[256,1024]{1,0:T(8,128)}, f32[1024,256]{1,0:T(8,128)}) custom-call(s32[3]{0:T(128)S(1)} %pad_add_fusion.place, bf16[4,4,192,128]{3,2,1,0:T(8,128)(2,1)S(1)} %collective-permute-done.19.src, f32[256,1024]{1,0:T(8,128)} %get-tuple-element.89._0, ...), custom_call_target="tpu_custom_call", output_to_operand_aliasing={{0}: (2, {}), {1}: (3, {}), {2}: (4, {})} | custom-call | flops 524288 | bytes 2359296 | tf_op jit(solution)/shard_map/second_unpack/pallas_call | solution.py:379
  (71 shorter events, 18.9 us)
Async XLA Ops:
  0.6 17.1 %collective-permute-start.1 = (bf16[1024,256]{1,0:T(8,128)(2,1)}, bf16[1024,256]{1,0:T(8,128)(2,1)S(1)}, u32[]{:S(2)}, u32[]{:S(2)}) collective-permute-start(bf16[1024,256]{1,0:T(8,128)(2,1)} %x.3), channel_id=1, source_target_pairs={{1,0},{2,1},{3,2},{4,3},{5,4},{6,5},{7,6},{8,7},{9,8},{10,9},{11,1... | collective-permute-start | bytes 1572872 | tf_op jit(solution)/shard_map/ppermute | solution.py:284
  1.9 18.1 %collective-permute-start = (bf16[1024,256]{1,0:T(8,128)(2,1)}, bf16[1024,256]{1,0:T(8,128)(2,1)S(1)}, u32[]{:S(2)}, u32[]{:S(2)}) collective-permute-start(bf16[1024,256]{1,0:T(8,128)(2,1)} %x.3), channel_id=1, source_target_pairs={{0,1},{1,2},{2,3},{3,4},{4,5},{5,6},{6,7},{7,8},{8,9},{9,10},{10,1... | collective-permute-start | bytes 1572872 | tf_op jit(solution)/shard_map/ppermute | solution.py:283
  15.8 4.3 %copy-start.2 = (bf16[1024,256]{1,0:T(8,128)(2,1)S(1)}, bf16[1024,256]{1,0:T(8,128)(2,1)}, u32[]{:S(2)}) copy-start(bf16[1024,256]{1,0:T(8,128)(2,1)} %x.3) | copy-start | bytes 1572868
  15.8 4.3 %copy-start.4 = (bf16[256,1024]{1,0:T(8,128)(2,1)S(1)}, bf16[256,1024]{1,0:T(8,128)(2,1)}, u32[]{:S(2)}) copy-start(bf16[256,1024]{1,0:T(8,128)(2,1)} %wn.3) | copy-start | bytes 1572868
  25.4 12.9 %collective-permute-start.2 = (bf16[3104,128]{1,0:T(8,128)(2,1)S(1)}, bf16[3104,128]{1,0:T(8,128)(2,1)S(1)}, u32[]{:S(2)}, u32[]{:S(2)}) collective-permute-start(bf16[3104,128]{1,0:T(8,128)(2,1)S(1)} %get-tuple-element.59), channel_id=1, source_target_pairs={{0,4},{4,0},{8,12},{12,8},{16,20},{20,16},{24,28},{28,24},{1,5},{5... | collective-permute-start | bytes 2383880 | tf_op jit(solution)/shard_map/ppermute | solution.py:203
  38.7 10.8 %collective-permute-start.3 = (bf16[800,128]{1,0:T(8,128)(2,1)S(1)}, bf16[800,128]{1,0:T(8,128)(2,1)S(1)}, u32[]{:S(2)}, u32[]{:S(2)}) collective-permute-start(bf16[800,128]{1,0:T(8,128)(2,1)S(1)} %get-tuple-element.114), channel_id=1, source_target_pairs={{0,8},{4,12},{8,0},{12,4},{16,24},{20,28},{24,16},{28,20},{1,9},{5... | collective-permute-start | bytes 614408 | tf_op jit(solution)/shard_map/ppermute | solution.py:203
  40.6 11.2 %collective-permute-start.4 = (bf16[800,128]{1,0:T(8,128)(2,1)S(1)}, bf16[800,128]{1,0:T(8,128)(2,1)S(1)}, u32[]{:S(2)}, u32[]{:S(2)}) collective-permute-start(bf16[800,128]{1,0:T(8,128)(2,1)S(1)} %get-tuple-element.115), channel_id=1, source_target_pairs={{0,16},{4,20},{8,24},{12,28},{16,0},{20,4},{24,8},{28,12},{1,17},{... | collective-permute-start | bytes 614408 | tf_op jit(solution)/shard_map/ppermute | solution.py:203
  42.1 9.7 %collective-permute-start.5 = (bf16[800,128]{1,0:T(8,128)(2,1)S(1)}, bf16[800,128]{1,0:T(8,128)(2,1)S(1)}, u32[]{:S(2)}, u32[]{:S(2)}) collective-permute-start(bf16[800,128]{1,0:T(8,128)(2,1)S(1)} %get-tuple-element.116), channel_id=1, source_target_pairs={{0,24},{4,28},{8,16},{12,20},{16,8},{20,12},{24,0},{28,4},{1,25},{... | collective-permute-start | bytes 614408 | tf_op jit(solution)/shard_map/ppermute | solution.py:203
  45.3 17.5 %collective-permute-start.9 = (bf16[384,256]{1,0:T(8,128)(2,1)S(1)}, bf16[384,256]{1,0:T(8,128)(2,1)S(1)}, u32[]{:S(2)}, u32[]{:S(2)}) collective-permute-start(bf16[384,256]{1,0:T(8,128)(2,1)S(1)} %slice.126), channel_id=1, source_target_pairs={{0,1},{1,2},{2,3},{3,4},{4,5},{5,6},{6,7},{7,8},{8,9},{9,10},{10,1... | collective-permute-start | bytes 589832 | tf_op jit(solution)/shard_map/ppermute | solution.py:354
  49.5 7.4 %copy-start.6 = (bf16[1024,256]{1,0:T(8,128)(2,1)S(1)}, bf16[1024,256]{1,0:T(8,128)(2,1)}, u32[]{:S(2)}) copy-start(bf16[1024,256]{1,0:T(8,128)(2,1)} %wo.3) | copy-start | bytes 1572868
  49.6 7.4 %copy-start.10 = (f32[256]{0:T(256)S(1)}, f32[256]{0:T(256)}, u32[]{:S(2)}) copy-start(f32[256]{0:T(256)} %param.16) | copy-start | bytes 3076
  52.1 6.9 %collective-permute-start.6 = (bf16[224,128]{1,0:T(8,128)(2,1)S(1)}, bf16[224,128]{1,0:T(8,128)(2,1)S(1)}, u32[]{:S(2)}, u32[]{:S(2)}) collective-permute-start(bf16[224,128]{1,0:T(8,128)(2,1)S(1)} %get-tuple-element.111), channel_id=1, source_target_pairs={{0,1},{1,0},{2,3},{3,2},{4,5},{5,4},{6,7},{7,6},{8,9},{9,8},{10,11... | collective-permute-start | bytes 172040 | tf_op jit(solution)/shard_map/ppermute | solution.py:203
  54.5 6.0 %collective-permute-start.7 = (bf16[224,128]{1,0:T(8,128)(2,1)S(1)}, bf16[224,128]{1,0:T(8,128)(2,1)S(1)}, u32[]{:S(2)}, u32[]{:S(2)}) collective-permute-start(bf16[224,128]{1,0:T(8,128)(2,1)S(1)} %get-tuple-element.112), channel_id=1, source_target_pairs={{0,2},{1,3},{2,0},{3,1},{4,6},{5,7},{6,4},{7,5},{8,10},{9,11},{10,... | collective-permute-start | bytes 172040 | tf_op jit(solution)/shard_map/ppermute | solution.py:203
  56.6 6.2 %collective-permute-start.8 = (bf16[224,128]{1,0:T(8,128)(2,1)S(1)}, bf16[224,128]{1,0:T(8,128)(2,1)S(1)}, u32[]{:S(2)}, u32[]{:S(2)}) collective-permute-start(bf16[224,128]{1,0:T(8,128)(2,1)S(1)} %get-tuple-element.113), channel_id=1, source_target_pairs={{0,3},{1,2},{2,1},{3,0},{4,7},{5,6},{6,5},{7,4},{8,11},{9,10},{10,... | collective-permute-start | bytes 172040 | tf_op jit(solution)/shard_map/ppermute | solution.py:203
  62.8 6.8 %collective-permute-start.12 = (bf16[192,128]{1,0:T(8,128)(2,1)S(1)}, bf16[192,128]{1,0:T(8,128)(2,1)S(1)}, u32[]{:S(2)}, u32[]{:S(2)}) collective-permute-start(bf16[192,128]{1,0:T(8,128)(2,1)S(1)} %fusion.1), channel_id=1, source_target_pairs={{0,2},{1,3},{2,0},{3,1},{4,6},{5,7},{6,4},{7,5},{8,10},{9,11},{10,... | collective-permute-start | bytes 147464 | tf_op jit(solution)/shard_map/ppermute | solution.py:203
  63.2 6.4 %collective-permute-start.13 = (bf16[192,128]{1,0:T(8,128)(2,1)S(1)}, bf16[192,128]{1,0:T(8,128)(2,1)S(1)}, u32[]{:S(2)}, u32[]{:S(2)}) collective-permute-start(bf16[192,128]{1,0:T(8,128)(2,1)S(1)} %fusion.1), channel_id=1, source_target_pairs={{0,3},{1,2},{2,1},{3,0},{4,7},{5,6},{6,5},{7,4},{8,11},{9,10},{10,... | collective-permute-start | bytes 147464 | tf_op jit(solution)/shard_map/ppermute | solution.py:203
  64.2 11.6 %collective-permute-start.10 = (bf16[192,128]{1,0:T(8,128)(2,1)S(1)}, bf16[192,128]{1,0:T(8,128)(2,1)S(1)}, u32[]{:S(2)}, u32[]{:S(2)}) collective-permute-start(bf16[192,128]{1,0:T(8,128)(2,1)S(1)} %fusion.1), channel_id=1, source_target_pairs={{0,1},{1,0},{2,3},{3,2},{4,5},{5,4},{6,7},{7,6},{8,9},{9,8},{10,11... | collective-permute-start | bytes 147464 | tf_op jit(solution)/shard_map/ppermute | solution.py:203
  66.4 14.2 %collective-permute-start.15 = (bf16[640,256]{1,0:T(8,128)(2,1)S(1)}, bf16[640,256]{1,0:T(8,128)(2,1)S(1)}, u32[]{:S(2)}, u32[]{:S(2)}) collective-permute-start(bf16[640,256]{1,0:T(8,128)(2,1)S(1)} %slice.127), channel_id=1, source_target_pairs={{0,1},{1,2},{2,3},{3,4},{4,5},{5,6},{6,7},{7,8},{8,9},{9,10},{10,1... | collective-permute-start | bytes 983048 | tf_op jit(solution)/shard_map/ppermute | solution.py:358
  68.3 20.3 %collective-permute-start.18 = (bf16[1024,256]{1,0:T(8,128)(2,1)S(1)}, bf16[1024,256]{1,0:T(8,128)(2,1)S(1)}, u32[]{:S(2)}, u32[]{:S(2)}) collective-permute-start(bf16[1024,256]{1,0:T(8,128)(2,1)S(1)} %get-tuple-element.82), channel_id=1, source_target_pairs={{1,0},{2,1},{3,2},{4,3},{5,4},{6,5},{7,6},{8,7},{9,8},{10,9},{11,1... | collective-permute-start | bytes 1572872 | tf_op jit(solution)/shard_map/ppermute | solution.py:357
  69.7 10.3 %collective-permute-start.14 = (bf16[2,192,128]{2,1,0:T(8,128)(2,1)S(1)}, bf16[2,192,128]{2,1,0:T(8,128)(2,1)S(1)}, u32[]{:S(2)}, u32[]{:S(2)}) collective-permute-start(bf16[2,192,128]{2,1,0:T(8,128)(2,1)S(1)} %get-tuple-element.108), channel_id=1, source_target_pairs={{0,8},{4,12},{8,0},{12,4},{16,24},{20,28},{24,16},{28,20},{1,9},{5... | collective-permute-start | bytes 294920 | tf_op jit(solution)/shard_map/ppermute | solution.py:203
  75.8 4.7 %collective-permute-start.11 = (bf16[2,192,128]{2,1,0:T(8,128)(2,1)S(1)}, bf16[2,192,128]{2,1,0:T(8,128)(2,1)S(1)}, u32[]{:S(2)}, u32[]{:S(2)}) collective-permute-start(bf16[2,192,128]{2,1,0:T(8,128)(2,1)S(1)} %get-tuple-element.110), channel_id=1, source_target_pairs={{0,16},{4,20},{8,24},{12,28},{16,0},{20,4},{24,8},{28,12},{1,17},{... | collective-permute-start | bytes 294920 | tf_op jit(solution)/shard_map/ppermute | solution.py:203
  80.6 5.8 %collective-permute-start.16 = (bf16[2,2,192,128]{3,2,1,0:T(8,128)(2,1)S(1)}, bf16[2,2,192,128]{3,2,1,0:T(8,128)(2,1)S(1)}, u32[]{:S(2)}, u32[]{:S(2)}) collective-permute-start(bf16[2,2,192,128]{3,2,1,0:T(8,128)(2,1)S(1)} %pad_maximum_fusion.8), channel_id=1, source_target_pairs={{0,8},{4,12},{8,0},{12,4},{16,24},{20,28},{24,16},{28,20},{1,9},{5... | collective-permute-start | bytes 589832 | tf_op jit(solution)/shard_map/ppermute | solution.py:203
  82.8 5.8 %collective-permute-start.17 = (bf16[2,2,192,128]{3,2,1,0:T(8,128)(2,1)S(1)}, bf16[2,2,192,128]{3,2,1,0:T(8,128)(2,1)S(1)}, u32[]{:S(2)}, u32[]{:S(2)}) collective-permute-start(bf16[2,2,192,128]{3,2,1,0:T(8,128)(2,1)S(1)} %pad_maximum_fusion.9), channel_id=1, source_target_pairs={{0,16},{4,20},{8,24},{12,28},{16,0},{20,4},{24,8},{28,12},{1,17},{... | collective-permute-start | bytes 589832 | tf_op jit(solution)/shard_map/ppermute | solution.py:203
  88.6 2.8 %collective-permute-start.19 = (bf16[4,4,192,128]{3,2,1,0:T(8,128)(2,1)S(1)}, bf16[4,4,192,128]{3,2,1,0:T(8,128)(2,1)S(1)}, u32[]{:S(2)}, u32[]{:S(2)}) collective-permute-start(bf16[4,4,192,128]{3,2,1,0:T(8,128)(2,1)S(1)} %maximum_maximum_fusion.src), channel_id=1, source_target_pairs={{0,4},{4,0},{8,12},{12,8},{16,20},{20,16},{24,28},{28,24},{1,5},{5... | collective-permute-start | bytes 2359304 | tf_op jit(solution)/shard_map/ppermute | solution.py:203
  (7 other events, 7.5 us)

commit v5 on v4

--- a/solution.py
+++ b/solution.py
@@ -339,7 +339,7 @@
         name="spread",
     )(place, cols, adj, dh, wn_t)
     acc, bias = reduce_among([acc[i] for i in range(4)], bias, "row", (2, 4, 6))
-    end = 6 * rows // 16
+    end = rows // 2
     acc, hid, dh, own = lax.optimization_barrier((acc, hid, dh, own))
     embed, own = pl.pallas_call(
         finish_kernel,

time: 93.8 us -> 95.9 us (1.022)
  the two profiles are of different devices: /device:TPU:0 before, /device:TPU:21 now
where the time goes in v5:
time: 95.9 us; the launch traced here: 95.4 us
  waiting for transfers between devices  36.4 us (38%)
  starting transfers between devices  32.3 us (34%)
  Pallas kernels  16.4 us (17%)
  local copies, waits for them, and re-layouts  8.39 us (9%)
    ppermute x15, starting transfers between devices, swap(): lax.ppermute(value, axis, [(i, i ^ bit) for i in range(lax.axis_size(axis...  17.7 us
    ppermute x15, waiting for transfers between devices, swap(): lax.ppermute(value, axis, [(i, i ^ bit) for i in range(lax.axis_size(axis...  15.5 us
    ppermute x1, waiting for transfers between devices, local(): low = lax.ppermute(x, both, forward)  13.7 us
    unnamed x23, local copies, waits for them, and re-layouts  8.26 us
    ppermute x1, waiting for transfers between devices, local(): from_high = lax.ppermute(to_low, both, backward)  7.24 us
    pallas_call x1, Pallas kernels, local(): pl.pallas_call(forward_kernel, out_shape=(sds((rows, hidden), BF16), sds(...  5.38 us
    ppermute x1, starting transfers between devices, local(): from_high = lax.ppermute(to_low, both, backward)  3.92 us
    ppermute x1, starting transfers between devices, local(): low = lax.ppermute(x, both, forward)  3.21 us
  transfers between devices with their start and end apart: 20, of which 10 were waited for; matrix products, arithmetic and copies ran while one was open for 1% of the time, Pallas kernels for 10%

profile of v5, /device:TPU:21, one launch (start us, length us, event | category | flops | bytes accessed | tf_op | source)
XLA Modules:
  0.0 95.4 jit_solution(12397873157490692097)
XLA Ops:
  0.6 2.1 %collective-permute-start.1 = (bf16[1024,256]{1,0:T(8,128)(2,1)}, bf16[1024,256]{1,0:T(8,128)(2,1)S(1)}, u32[]{:S(2)}, u32[]{:S(2)}) collective-permute-start(bf16[1024,256]{1,0:T(8,128)(2,1)} %x.3), channel_id=1, source_target_pairs={{1,0},{2,1},{3,2},{4,3},{5,4},{6,5},{7,6},{8,7},{9,8},{10,9},{11,1... | collective-permute-start | bytes 1572872 | tf_op jit(solution)/shard_map/ppermute | solution.py:284
  2.7 3.2 %collective-permute-start = (bf16[1024,256]{1,0:T(8,128)(2,1)}, bf16[1024,256]{1,0:T(8,128)(2,1)S(1)}, u32[]{:S(2)}, u32[]{:S(2)}) collective-permute-start(bf16[1024,256]{1,0:T(8,128)(2,1)} %x.3), channel_id=1, source_target_pairs={{0,1},{1,2},{2,3},{3,4},{4,5},{5,6},{6,7},{7,8},{8,9},{9,10},{10,1... | collective-permute-start | bytes 1572872 | tf_op jit(solution)/shard_map/ppermute | solution.py:283
  6.7 1.6 %copy-done = s32[16,64,512]{2,1,0:T(8,128)S(1)} copy-done((s32[16,64,512]{2,1,0:T(8,128)S(1)}, s32[16,64,512]{2,1,0:T(8,128)}, u32[]{:S(2)}) %copy-start) | copy-done | bytes 2097176
  14.2 1.5 %prepare.1 = (bf16[16,64,512]{2,1,0:T(8,128)(2,1)S(1)}, bf16[256,1024]{1,0:T(8,128)(2,1)S(1)}, bf16[256,1024]{1,0:T(8,128)(2,1)S(1)}, bf16[1024,256]{1,0:T(8,128...) custom-call(s32[16,64,512]{2,1,0:T(8,128)S(1)} %copy-done, ...), custom_call_target="tpu_custom_call" | custom-call | flops 1073741824 | bytes 9437184 | tf_op jit(solution)/shard_map/prepare/pallas_call | solution.py:285
  15.8 13.7 %collective-permute-done.lo = bf16[1024,256]{1,0:T(8,128)(2,1)S(1)} collective-permute-done((bf16[1024,256]{1,0:T(8,128)(2,1)}, bf16[1024,256]{1,0:T(8,128)(2,1)S(1)}, u32[]{:S(2)}, u32[]{:S(2)}) %collective-permute-start) | collective-permute-done | bytes 524320 | tf_op jit(solution)/shard_map/ppermute | solution.py:283
  29.5 5.4 %forward.1 = (bf16[1024,1024]{1,0:T(8,128)(2,1)S(1)}, bf16[1024,1024]{1,0:T(8,128)(2,1)S(1)}, f32[3072,128]{1,0:T(8,128)S(1)}, bf16[3104,128]{1,0:T(8,128)(2,1)S(1)}, f32[16,128]{1,0:T(8,128)S(1)}) custom-call(s32[3]{0:T(128)S(1)} %pad_add_fusion.place, s32[16,8]{1,0:T(8,128)S(1)} %copy.21.cols, bf16[1024,256]{1,0:T(8,128)(2,1)S(1)} %collective-permute-done.lo, ...), custom_call_target="tpu_custom_call" | custom-call | flops 2415919104 | bytes 14680064 | tf_op jit(solution)/shard_map/forward/pallas_call | solution.py:304
  35.9 1.9 %collective-permute-done.2 = bf16[3104,128]{1,0:T(8,128)(2,1)S(1)} collective-permute-done((bf16[3104,128]{1,0:T(8,128)(2,1)S(1)}, bf16[3104,128]{1,0:T(8,128)(2,1)S(1)}, u32[]{:S(2)}, u32[]{:S(2)}) %collective-permute-start.2) | collective-permute-done | bytes 794656 | tf_op jit(solution)/shard_map/ppermute | solution.py:203
  40.9 3.0 %spread.1 = (f32[1024,256]{1,0:T(8,128)S(1)}, bf16[1024,256]{1,0:T(8,128)(2,1)S(1)}, bf16[1024,256]{1,0:T(8,128)(2,1)S(1)}) custom-call(s32[3]{0:T(128)S(1)} %pad_add_fusion.place, s32[16,8]{1,0:T(8,128)S(1)} %copy.21.cols, bf16[16,64,512]{2,1,0:T(8,128)(2,1)S(1)} %get-tuple-element.52.adj, bf16[1024,1024]{1,0:T(8,128)(2,1)S(1)} %get-tuple-element.72.dh, ...), custom_call_target="tpu_custom_call" | custom-call | flops 805306368 | bytes 6291456 | tf_op jit(solution)/shard_map/spread/pallas_call | solution.py:329
  44.0 3.2 %collective-permute-start.9 = (bf16[512,256]{1,0:T(8,128)(2,1)S(1)}, bf16[512,256]{1,0:T(8,128)(2,1)S(1)}, u32[]{:S(2)}, u32[]{:S(2)}) collective-permute-start(bf16[512,256]{1,0:T(8,128)(2,1)S(1)} %slice.126), channel_id=1, source_target_pairs={{0,1},{1,2},{2,3},{3,4},{4,5},{5,6},{6,7},{7,8},{8,9},{9,10},{10,1... | collective-permute-start | bytes 786440 | tf_op jit(solution)/shard_map/ppermute | solution.py:354
  47.2 2.6 %collective-permute-done.4 = bf16[800,128]{1,0:T(8,128)(2,1)S(1)} collective-permute-done((bf16[800,128]{1,0:T(8,128)(2,1)S(1)}, bf16[800,128]{1,0:T(8,128)(2,1)S(1)}, u32[]{:S(2)}, u32[]{:S(2)}) %collective-permute-start.4) | collective-permute-done | bytes 204832 | tf_op jit(solution)/shard_map/ppermute | solution.py:203
  52.8 2.1 %finish.1 = (bf16[1024,256]{1,0:T(8,128)(2,1)}, f32[1024,256]{1,0:T(8,128)S(1)}) custom-call(bf16[1024,1024]{1,0:T(8,128)(2,1)S(1)} %get-tuple-element.71.hid, bf16[1024,1024]{1,0:T(8,128)(2,1)S(1)} %get-tuple-element.72.dh, bf16[1024,256]{1,0:T(8,128)(2,1)S(1)} %copy-done.6, f32[1,256]{1,0:T(1,128)S(1)} %bitcast.40, ...), custom_call_target="tpu_custom_call" | custom-call | flops 1073741824 | bytes 8388608 | tf_op jit(solution)/shard_map/finish/pallas_call | solution.py:344
  54.8 1.8 %collective-permute-done.6 = bf16[224,128]{1,0:T(8,128)(2,1)S(1)} collective-permute-done((bf16[224,128]{1,0:T(8,128)(2,1)S(1)}, bf16[224,128]{1,0:T(8,128)(2,1)S(1)}, u32[]{:S(2)}, u32[]{:S(2)}) %collective-permute-start.6) | collective-permute-done | bytes 57376 | tf_op jit(solution)/shard_map/ppermute | solution.py:203
  56.7 2.2 %collective-permute-done.8 = bf16[224,128]{1,0:T(8,128)(2,1)S(1)} collective-permute-done((bf16[224,128]{1,0:T(8,128)(2,1)S(1)}, bf16[224,128]{1,0:T(8,128)(2,1)S(1)}, u32[]{:S(2)}, u32[]{:S(2)}) %collective-permute-start.8) | collective-permute-done | bytes 57376 | tf_op jit(solution)/shard_map/ppermute | solution.py:203
  59.0 1.6 %collective-permute-start.12 = (bf16[192,128]{1,0:T(8,128)(2,1)S(1)}, bf16[192,128]{1,0:T(8,128)(2,1)S(1)}, u32[]{:S(2)}, u32[]{:S(2)}) collective-permute-start(bf16[192,128]{1,0:T(8,128)(2,1)S(1)} %fusion.1), channel_id=1, source_target_pairs={{0,2},{1,3},{2,0},{3,1},{4,6},{5,7},{6,4},{7,5},{8,10},{9,11},{10,... | collective-permute-start | bytes 147464 | tf_op jit(solution)/shard_map/ppermute | solution.py:203
  62.6 2.2 %collective-permute-start.15 = (bf16[512,256]{1,0:T(8,128)(2,1)S(1)}, bf16[512,256]{1,0:T(8,128)(2,1)S(1)}, u32[]{:S(2)}, u32[]{:S(2)}) collective-permute-start(bf16[512,256]{1,0:T(8,128)(2,1)S(1)} %slice.127), channel_id=1, source_target_pairs={{0,1},{1,2},{2,3},{3,4},{4,5},{5,6},{6,7},{7,8},{8,9},{9,10},{10,1... | collective-permute-start | bytes 786440 | tf_op jit(solution)/shard_map/ppermute | solution.py:358
  64.9 3.9 %collective-permute-start.18 = (bf16[1024,256]{1,0:T(8,128)(2,1)S(1)}, bf16[1024,256]{1,0:T(8,128)(2,1)S(1)}, u32[]{:S(2)}, u32[]{:S(2)}) collective-permute-start(bf16[1024,256]{1,0:T(8,128)(2,1)S(1)} %get-tuple-element.82), channel_id=1, source_target_pairs={{1,0},{2,1},{3,2},{4,3},{5,4},{6,5},{7,6},{8,7},{9,8},{10,9},{11,1... | collective-permute-start | bytes 1572872 | tf_op jit(solution)/shard_map/ppermute | solution.py:357
  69.0 1.6 %collective-permute-start.11 = (bf16[2,192,128]{2,1,0:T(8,128)(2,1)S(1)}, bf16[2,192,128]{2,1,0:T(8,128)(2,1)S(1)}, u32[]{:S(2)}, u32[]{:S(2)}) collective-permute-start(bf16[2,192,128]{2,1,0:T(8,128)(2,1)S(1)} %get-tuple-element.110), channel_id=1, source_target_pairs={{0,16},{4,20},{8,24},{12,28},{16,0},{20,4},{24,8},{28,12},{1,17},{... | collective-permute-start | bytes 294920 | tf_op jit(solution)/shard_map/ppermute | solution.py:203
  70.5 2.1 %collective-permute-done.14 = bf16[2,192,128]{2,1,0:T(8,128)(2,1)S(1)} collective-permute-done((bf16[2,192,128]{2,1,0:T(8,128)(2,1)S(1)}, bf16[2,192,128]{2,1,0:T(8,128)(2,1)S(1)}, u32[]{:S(2)}, u32[]{:S(2)}) %collective-permute-start.14) | collective-permute-done | bytes 98336 | tf_op jit(solution)/shard_map/ppermute | solution.py:203
  72.9 1.5 %collective-permute-start.16 = (bf16[2,2,192,128]{3,2,1,0:T(8,128)(2,1)S(1)}, bf16[2,2,192,128]{3,2,1,0:T(8,128)(2,1)S(1)}, u32[]{:S(2)}, u32[]{:S(2)}) collective-permute-start(bf16[2,2,192,128]{3,2,1,0:T(8,128)(2,1)S(1)} %pad_maximum_fusion.8), channel_id=1, source_target_pairs={{0,8},{4,12},{8,0},{12,4},{16,24},{20,28},{24,16},{28,20},{1,9},{5... | collective-permute-start | bytes 589832 | tf_op jit(solution)/shard_map/ppermute | solution.py:203
  74.5 3.3 %collective-permute-done.16 = bf16[2,2,192,128]{3,2,1,0:T(8,128)(2,1)S(1)} collective-permute-done((bf16[2,2,192,128]{3,2,1,0:T(8,128)(2,1)S(1)}, bf16[2,2,192,128]{3,2,1,0:T(8,128)(2,1)S(1)}, u32[]{:S(2)}, u32[]{:S(2)}) %collective-permute-start.16) | collective-permute-done | bytes 196640 | tf_op jit(solution)/shard_map/ppermute | solution.py:203
  79.2 7.2 %collective-permute-done.18.from_high = bf16[1024,256]{1,0:T(8,128)(2,1)S(1)} collective-permute-done((bf16[1024,256]{1,0:T(8,128)(2,1)S(1)}, bf16[1024,256]{1,0:T(8,128)(2,1)S(1)}, u32[]{:S(2)}, u32[]{:S(2)}) %collective-permute-start.18) | collective-permute-done | bytes 524320 | tf_op jit(solution)/shard_map/ppermute | solution.py:357
  86.5 4.4 %collective-permute-start.19 = (bf16[4,4,192,128]{3,2,1,0:T(8,128)(2,1)S(1)}, bf16[4,4,192,128]{3,2,1,0:T(8,128)(2,1)S(1)}, u32[]{:S(2)}, u32[]{:S(2)}) collective-permute-start(bf16[4,4,192,128]{3,2,1,0:T(8,128)(2,1)S(1)} %maximum_maximum_fusion.src), channel_id=1, source_target_pairs={{0,4},{4,0},{8,12},{12,8},{16,20},{20,16},{24,28},{28,24},{1,5},{5... | collective-permute-start | bytes 2359304 | tf_op jit(solution)/shard_map/ppermute | solution.py:203
  90.9 2.6 %first_unpack.1 = (f32[256,1024]{1,0:T(8,128)}, f32[256,1024]{1,0:T(8,128)}, f32[1024,256]{1,0:T(8,128)}, bf16[1024,256]{1,0:T(8,128)(2,1)}, f32[8,128]{1,0:T(8,128)}, /*index=5*/f32[2,128]{1,0:T(2,128)}) custom-call(s32[3]{0:T(128)S(1)} %pad_add_fusion.place, bf16[4,4,192,128]{3,2,1,0:T(8,128)(2,1)S(1)} %maximum_maximum_fusion.src, ...), custom_call_target="tpu_custom_call" | custom-call | flops 1048576 | bytes 3145728 | tf_op jit(solution)/shard_map/first_unpack/pallas_call | solution.py:368
  93.5 1.8 %second_unpack.1 = (f32[256,1024]{1,0:T(8,128)}, f32[256,1024]{1,0:T(8,128)}, f32[1024,256]{1,0:T(8,128)}) custom-call(s32[3]{0:T(128)S(1)} %pad_add_fusion.place, bf16[4,4,192,128]{3,2,1,0:T(8,128)(2,1)S(1)} %collective-permute-done.19.src, f32[256,1024]{1,0:T(8,128)} %get-tuple-element.89._0, ...), custom_call_target="tpu_custom_call", output_to_operand_aliasing={{0}: (2, {}), {1}: (3, {}), {2}: (4, {})} | custom-call | flops 524288 | bytes 2359296 | tf_op jit(solution)/shard_map/second_unpack/pallas_call | solution.py:379
  (71 shorter events, 17.8 us)
Async XLA Ops:
  0.6 15.1 %collective-permute-start.1 = (bf16[1024,256]{1,0:T(8,128)(2,1)}, bf16[1024,256]{1,0:T(8,128)(2,1)S(1)}, u32[]{:S(2)}, u32[]{:S(2)}) collective-permute-start(bf16[1024,256]{1,0:T(8,128)(2,1)} %x.3), channel_id=1, source_target_pairs={{1,0},{2,1},{3,2},{4,3},{5,4},{6,5},{7,6},{8,7},{9,8},{10,9},{11,1... | collective-permute-start | bytes 1572872 | tf_op jit(solution)/shard_map/ppermute | solution.py:284
  2.7 26.7 %collective-permute-start = (bf16[1024,256]{1,0:T(8,128)(2,1)}, bf16[1024,256]{1,0:T(8,128)(2,1)S(1)}, u32[]{:S(2)}, u32[]{:S(2)}) collective-permute-start(bf16[1024,256]{1,0:T(8,128)(2,1)} %x.3), channel_id=1, source_target_pairs={{0,1},{1,2},{2,3},{3,4},{4,5},{5,6},{6,7},{7,8},{8,9},{9,10},{10,1... | collective-permute-start | bytes 1572872 | tf_op jit(solution)/shard_map/ppermute | solution.py:283
  14.2 15.3 %copy-start.2 = (bf16[1024,256]{1,0:T(8,128)(2,1)S(1)}, bf16[1024,256]{1,0:T(8,128)(2,1)}, u32[]{:S(2)}) copy-start(bf16[1024,256]{1,0:T(8,128)(2,1)} %x.3) | copy-start | bytes 1572868
  14.2 15.3 %copy-start.4 = (bf16[256,1024]{1,0:T(8,128)(2,1)S(1)}, bf16[256,1024]{1,0:T(8,128)(2,1)}, u32[]{:S(2)}) copy-start(bf16[256,1024]{1,0:T(8,128)(2,1)} %wn.3) | copy-start | bytes 1572868
  34.9 2.9 %collective-permute-start.2 = (bf16[3104,128]{1,0:T(8,128)(2,1)S(1)}, bf16[3104,128]{1,0:T(8,128)(2,1)S(1)}, u32[]{:S(2)}, u32[]{:S(2)}) collective-permute-start(bf16[3104,128]{1,0:T(8,128)(2,1)S(1)} %get-tuple-element.59), channel_id=1, source_target_pairs={{0,4},{4,0},{8,12},{12,8},{16,20},{20,16},{24,28},{28,24},{1,5},{5... | collective-permute-start | bytes 2383880 | tf_op jit(solution)/shard_map/ppermute | solution.py:203
  38.2 9.0 %collective-permute-start.3 = (bf16[800,128]{1,0:T(8,128)(2,1)S(1)}, bf16[800,128]{1,0:T(8,128)(2,1)S(1)}, u32[]{:S(2)}, u32[]{:S(2)}) collective-permute-start(bf16[800,128]{1,0:T(8,128)(2,1)S(1)} %get-tuple-element.114), channel_id=1, source_target_pairs={{0,8},{4,12},{8,0},{12,4},{16,24},{20,28},{24,16},{28,20},{1,9},{5... | collective-permute-start | bytes 614408 | tf_op jit(solution)/shard_map/ppermute | solution.py:203
  39.5 10.4 %collective-permute-start.4 = (bf16[800,128]{1,0:T(8,128)(2,1)S(1)}, bf16[800,128]{1,0:T(8,128)(2,1)S(1)}, u32[]{:S(2)}, u32[]{:S(2)}) collective-permute-start(bf16[800,128]{1,0:T(8,128)(2,1)S(1)} %get-tuple-element.115), channel_id=1, source_target_pairs={{0,16},{4,20},{8,24},{12,28},{16,0},{20,4},{24,8},{28,12},{1,17},{... | collective-permute-start | bytes 614408 | tf_op jit(solution)/shard_map/ppermute | solution.py:203
  39.7 10.1 %collective-permute-start.5 = (bf16[800,128]{1,0:T(8,128)(2,1)S(1)}, bf16[800,128]{1,0:T(8,128)(2,1)S(1)}, u32[]{:S(2)}, u32[]{:S(2)}) collective-permute-start(bf16[800,128]{1,0:T(8,128)(2,1)S(1)} %get-tuple-element.116), channel_id=1, source_target_pairs={{0,24},{4,28},{8,16},{12,20},{16,8},{20,12},{24,0},{28,4},{1,25},{... | collective-permute-start | bytes 614408 | tf_op jit(solution)/shard_map/ppermute | solution.py:203
  44.0 15.0 %collective-permute-start.9 = (bf16[512,256]{1,0:T(8,128)(2,1)S(1)}, bf16[512,256]{1,0:T(8,128)(2,1)S(1)}, u32[]{:S(2)}, u32[]{:S(2)}) collective-permute-start(bf16[512,256]{1,0:T(8,128)(2,1)S(1)} %slice.126), channel_id=1, source_target_pairs={{0,1},{1,2},{2,3},{3,4},{4,5},{5,6},{6,7},{7,8},{8,9},{9,10},{10,1... | collective-permute-start | bytes 786440 | tf_op jit(solution)/shard_map/ppermute | solution.py:354
  47.2 5.6 %copy-start.6 = (bf16[1024,256]{1,0:T(8,128)(2,1)S(1)}, bf16[1024,256]{1,0:T(8,128)(2,1)}, u32[]{:S(2)}) copy-start(bf16[1024,256]{1,0:T(8,128)(2,1)} %wo.3) | copy-start | bytes 1572868
  47.2 5.6 %copy-start.10 = (f32[256]{0:T(256)S(1)}, f32[256]{0:T(256)}, u32[]{:S(2)}) copy-start(f32[256]{0:T(256)} %param.16) | copy-start | bytes 3076
  50.1 6.6 %collective-permute-start.6 = (bf16[224,128]{1,0:T(8,128)(2,1)S(1)}, bf16[224,128]{1,0:T(8,128)(2,1)S(1)}, u32[]{:S(2)}, u32[]{:S(2)}) collective-permute-start(bf16[224,128]{1,0:T(8,128)(2,1)S(1)} %get-tuple-element.111), channel_id=1, source_target_pairs={{0,1},{1,0},{2,3},{3,2},{4,5},{5,4},{6,7},{7,6},{8,9},{9,8},{10,11... | collective-permute-start | bytes 172040 | tf_op jit(solution)/shard_map/ppermute | solution.py:203
  51.4 5.3 %collective-permute-start.7 = (bf16[224,128]{1,0:T(8,128)(2,1)S(1)}, bf16[224,128]{1,0:T(8,128)(2,1)S(1)}, u32[]{:S(2)}, u32[]{:S(2)}) collective-permute-start(bf16[224,128]{1,0:T(8,128)(2,1)S(1)} %get-tuple-element.112), channel_id=1, source_target_pairs={{0,2},{1,3},{2,0},{3,1},{4,6},{5,7},{6,4},{7,5},{8,10},{9,11},{10,... | collective-permute-start | bytes 172040 | tf_op jit(solution)/shard_map/ppermute | solution.py:203
  52.0 7.0 %collective-permute-start.8 = (bf16[224,128]{1,0:T(8,128)(2,1)S(1)}, bf16[224,128]{1,0:T(8,128)(2,1)S(1)}, u32[]{:S(2)}, u32[]{:S(2)}) collective-permute-start(bf16[224,128]{1,0:T(8,128)(2,1)S(1)} %get-tuple-element.113), channel_id=1, source_target_pairs={{0,3},{1,2},{2,1},{3,0},{4,7},{5,6},{6,5},{7,4},{8,11},{9,10},{10,... | collective-permute-start | bytes 172040 | tf_op jit(solution)/shard_map/ppermute | solution.py:203
  59.0 9.8 %collective-permute-start.12 = (bf16[192,128]{1,0:T(8,128)(2,1)S(1)}, bf16[192,128]{1,0:T(8,128)(2,1)S(1)}, u32[]{:S(2)}, u32[]{:S(2)}) collective-permute-start(bf16[192,128]{1,0:T(8,128)(2,1)S(1)} %fusion.1), channel_id=1, source_target_pairs={{0,2},{1,3},{2,0},{3,1},{4,6},{5,7},{6,4},{7,5},{8,10},{9,11},{10,... | collective-permute-start | bytes 147464 | tf_op jit(solution)/shard_map/ppermute | solution.py:203
  60.6 8.2 %collective-permute-start.13 = (bf16[192,128]{1,0:T(8,128)(2,1)S(1)}, bf16[192,128]{1,0:T(8,128)(2,1)S(1)}, u32[]{:S(2)}, u32[]{:S(2)}) collective-permute-start(bf16[192,128]{1,0:T(8,128)(2,1)S(1)} %fusion.1), channel_id=1, source_target_pairs={{0,3},{1,2},{2,1},{3,0},{4,7},{5,6},{6,5},{7,4},{8,11},{9,10},{10,... | collective-permute-start | bytes 147464 | tf_op jit(solution)/shard_map/ppermute | solution.py:203
  61.5 7.5 %collective-permute-start.10 = (bf16[192,128]{1,0:T(8,128)(2,1)S(1)}, bf16[192,128]{1,0:T(8,128)(2,1)S(1)}, u32[]{:S(2)}, u32[]{:S(2)}) collective-permute-start(bf16[192,128]{1,0:T(8,128)(2,1)S(1)} %fusion.1), channel_id=1, source_target_pairs={{0,1},{1,0},{2,3},{3,2},{4,5},{5,4},{6,7},{7,6},{8,9},{9,8},{10,11... | collective-permute-start | bytes 147464 | tf_op jit(solution)/shard_map/ppermute | solution.py:203
  62.6 10.3 %collective-permute-start.15 = (bf16[512,256]{1,0:T(8,128)(2,1)S(1)}, bf16[512,256]{1,0:T(8,128)(2,1)S(1)}, u32[]{:S(2)}, u32[]{:S(2)}) collective-permute-start(bf16[512,256]{1,0:T(8,128)(2,1)S(1)} %slice.127), channel_id=1, source_target_pairs={{0,1},{1,2},{2,3},{3,4},{4,5},{5,6},{6,7},{7,8},{8,9},{9,10},{10,1... | collective-permute-start | bytes 786440 | tf_op jit(solution)/shard_map/ppermute | solution.py:358
  64.9 21.6 %collective-permute-start.18 = (bf16[1024,256]{1,0:T(8,128)(2,1)S(1)}, bf16[1024,256]{1,0:T(8,128)(2,1)S(1)}, u32[]{:S(2)}, u32[]{:S(2)}) collective-permute-start(bf16[1024,256]{1,0:T(8,128)(2,1)S(1)} %get-tuple-element.82), channel_id=1, source_target_pairs={{1,0},{2,1},{3,2},{4,3},{5,4},{6,5},{7,6},{8,7},{9,8},{10,9},{11,1... | collective-permute-start | bytes 1572872 | tf_op jit(solution)/shard_map/ppermute | solution.py:357
  68.8 3.8 %collective-permute-start.14 = (bf16[2,192,128]{2,1,0:T(8,128)(2,1)S(1)}, bf16[2,192,128]{2,1,0:T(8,128)(2,1)S(1)}, u32[]{:S(2)}, u32[]{:S(2)}) collective-permute-start(bf16[2,192,128]{2,1,0:T(8,128)(2,1)S(1)} %get-tuple-element.108), channel_id=1, source_target_pairs={{0,8},{4,12},{8,0},{12,4},{16,24},{20,28},{24,16},{28,20},{1,9},{5... | collective-permute-start | bytes 294920 | tf_op jit(solution)/shard_map/ppermute | solution.py:203
  69.0 3.9 %collective-permute-start.11 = (bf16[2,192,128]{2,1,0:T(8,128)(2,1)S(1)}, bf16[2,192,128]{2,1,0:T(8,128)(2,1)S(1)}, u32[]{:S(2)}, u32[]{:S(2)}) collective-permute-start(bf16[2,192,128]{2,1,0:T(8,128)(2,1)S(1)} %get-tuple-element.110), channel_id=1, source_target_pairs={{0,16},{4,20},{8,24},{12,28},{16,0},{20,4},{24,8},{28,12},{1,17},{... | collective-permute-start | bytes 294920 | tf_op jit(solution)/shard_map/ppermute | solution.py:203
  72.9 4.9 %collective-permute-start.16 = (bf16[2,2,192,128]{3,2,1,0:T(8,128)(2,1)S(1)}, bf16[2,2,192,128]{3,2,1,0:T(8,128)(2,1)S(1)}, u32[]{:S(2)}, u32[]{:S(2)}) collective-permute-start(bf16[2,2,192,128]{3,2,1,0:T(8,128)(2,1)S(1)} %pad_maximum_fusion.8), channel_id=1, source_target_pairs={{0,8},{4,12},{8,0},{12,4},{16,24},{20,28},{24,16},{28,20},{1,9},{5... | collective-permute-start | bytes 589832 | tf_op jit(solution)/shard_map/ppermute | solution.py:203
  74.3 4.8 %collective-permute-start.17 = (bf16[2,2,192,128]{3,2,1,0:T(8,128)(2,1)S(1)}, bf16[2,2,192,128]{3,2,1,0:T(8,128)(2,1)S(1)}, u32[]{:S(2)}, u32[]{:S(2)}) collective-permute-start(bf16[2,2,192,128]{3,2,1,0:T(8,128)(2,1)S(1)} %pad_maximum_fusion.9), channel_id=1, source_target_pairs={{0,16},{4,20},{8,24},{12,28},{16,0},{20,4},{24,8},{28,12},{1,17},{... | collective-permute-start | bytes 589832 | tf_op jit(solution)/shard_map/ppermute | solution.py:203
  86.5 7.1 %collective-permute-start.19 = (bf16[4,4,192,128]{3,2,1,0:T(8,128)(2,1)S(1)}, bf16[4,4,192,128]{3,2,1,0:T(8,128)(2,1)S(1)}, u32[]{:S(2)}, u32[]{:S(2)}) collective-permute-start(bf16[4,4,192,128]{3,2,1,0:T(8,128)(2,1)S(1)} %maximum_maximum_fusion.src), channel_id=1, source_target_pairs={{0,4},{4,0},{8,12},{12,8},{16,20},{20,16},{24,28},{28,24},{1,5},{5... | collective-permute-start | bytes 2359304 | tf_op jit(solution)/shard_map/ppermute | solution.py:203
  (7 other events, 7.5 us)
